TPU v7x, 128 devices: a whole 4x4x4 slice. The times are simulated.
128 devices in a mesh: member: 8 (over x, y_hi), grid: 16 (over y_lo, z, core).
Axes of the slice: x: 4, y: 4 (y_hi: 2, y_lo: 2; y = y_hi * 2 + y_lo), z: 4, core: 2. Of those that a mesh axis runs over, the one named last changes fastest.
Arguments:
- latent_grids: bfloat16 [8, 8192, 1024], P('member', 'grid'), may hold values from -6 to 6
- cycle_points: int32 [64], replicated, may hold values from 1 to 128, 5120 in all
- norm_gain: float32 [1024], replicated, may hold values from 0.1 to 1.9
- w_query: bfloat16 [1024, 1024], replicated, may hold values from -0.1875 to 0.1875
- w_key: bfloat16 [1024, 1024], replicated, may hold values from -0.1875 to 0.1875
- w_value: bfloat16 [1024, 1024], replicated, may hold values from -0.1875 to 0.1875
- w_out: bfloat16 [1024, 1024], replicated, may hold values from -0.1875 to 0.1875
- dec_gain: float32 [1024], replicated, may hold values from 0.1 to 1.9
- w_dec: bfloat16 [100, 1024], replicated, may hold values from -0.1875 to 0.1875
- target: float32 [100, 8192], P(None, 'grid'), may hold values from -6 to 6
Outputs:
- predicted_maps: bfloat16 [8, 100, 8192], P('member', None, 'grid')
- latent_sensitivity: float32 [8, 8192, 1024], P('member', 'grid')
- out_grad: float32 [1024, 1024], P('grid', 'member')
Inputs may be any that keep to these rules, and one draw needn't show every extreme that they name: `cycle_points`: every cycle has at least one live point and at most 128; some cycle is full.
All inputs are finite; a program needn't handle non-finite values.
Results may differ from a plain program's by a relative error of at most 0.038.
Values may be sent and summed in bfloat16 or wider, within the bound.
No kernel may reach another device: no remote copies, remote signals or barrier semaphores. Data moves between devices by JAX's collectives and lax.ppermute only.
A program may use at most 256 MiB of HBM per device.

v0:
```python
import jax
import jax.numpy as jnp
from jax import lax
from jax.sharding import PartitionSpec as P

HEAD_DIM = 64
CYCLE_MAX = 128
WINDOW = 256


def extended(shard, sides, width):
    for axis, dim in sides:
        peers, length = (lax.axis_size(axis), shard.shape[dim])
        up = [(i, (i + 1) % peers) for i in range(peers - 1)]
        down = [(j, i) for i, j in up]
        last = lax.slice_in_dim(shard, length - width, length, axis=dim)
        leading = lax.slice_in_dim(shard, 0, width, axis=dim)
        before = lax.ppermute(last, axis, up)
        after = lax.ppermute(leading, axis, down)
        shard = jnp.concatenate([before, shard, after], axis=dim)
    return shard


def shifted(value, axis, steps):
    count = lax.axis_size(axis)
    leading, last = (max(0, -steps), min(count, count - steps))
    return lax.ppermute(value, axis, [(source, source + steps) for source in range(leading, last)])


def rms_norm(values, gain):
    return values * lax.rsqrt(jnp.mean(values * values, -1, keepdims=True) + 1e-05) * gain


def head_norm(values):
    shaped = values.reshape(values.shape[0], -1, HEAD_DIM)
    shaped = shaped * lax.rsqrt(jnp.mean(shaped * shaped, -1, keepdims=True) + 1e-06)
    return shaped.reshape(values.shape)


def live_points(positions, cycle_points, total_slots):
    cycle_ids = jnp.floor_divide(positions, CYCLE_MAX)
    slot_ids = positions - cycle_ids * CYCLE_MAX
    table = jnp.arange(cycle_points.shape[0], dtype=jnp.int32)
    cycle_len = jnp.sum(
        jnp.where(cycle_ids[:, None] == table[None, :], cycle_points[None, :], 0), 1
    )
    return (slot_ids < cycle_len) & (positions >= 0) & (positions < total_slots)


def attend(query_bf, pair_bf, key_mask):
    row_count, feature_width = query_bf.shape
    extended_count = pair_bf.shape[0]
    groups = feature_width // (4 * HEAD_DIM)
    queries = query_bf.reshape(row_count, groups, 4, HEAD_DIM).transpose(1, 0, 2, 3)
    key_part = (
        pair_bf[:, :feature_width]
        .reshape(extended_count, groups, 4, HEAD_DIM)
        .transpose(1, 0, 2, 3)
    )
    value_part = (
        pair_bf[:, feature_width:]
        .reshape(extended_count, groups, 4, HEAD_DIM)
        .transpose(1, 0, 2, 3)
    )

    def head_block(operands):
        q_blk, k_blk, v_blk = operands
        scores = jnp.einsum(
            "rhd,ehd->hre", q_blk, k_blk, preferred_element_type=jnp.float32
        ) * HEAD_DIM ** (-0.5)
        weights = jnp.exp(scores) * key_mask[None]
        weights = weights / jnp.sum(weights, -1, keepdims=True)
        weights_bf = weights.astype(jnp.bfloat16)
        return jnp.einsum("hre,ehd->rhd", weights_bf, v_blk, preferred_element_type=jnp.float32)

    blocks = lax.map(head_block, (queries, key_part, value_part))
    return blocks.transpose(1, 0, 2, 3).reshape(row_count, feature_width)


def decode(level, dec_gain, w_dec):
    decoded = rms_norm(level, dec_gain).astype(jnp.bfloat16)
    return jnp.dot(w_dec, decoded.T, preferred_element_type=jnp.float32)


def kernel_slope(diff):
    return diff * lax.rsqrt(diff * diff + 0.01)


def crps_grad(own_fields, whole_ensemble_decoding, truth_part, live_part):
    ensemble = whole_ensemble_decoding.shape[0]
    pair_sum = jnp.sum(kernel_slope(own_fields[:, None] - whole_ensemble_decoding[None]), 1)
    return (kernel_slope(own_fields - truth_part[None]) - pair_sum / (ensemble - 1)) * live_part[
        None, None, :
    ]


def contract_rows(left, right):
    return lax.dot_general(
        left, right, (((0,), (0,)), ((), ())), preferred_element_type=jnp.float32
    )


def contract_cols(left, right):
    return lax.dot_general(
        left, right, (((1,), (1,)), ((), ())), preferred_element_type=jnp.float32
    )


def body(
    latent_grids, cycle_points, norm_gain, w_query, w_key, w_value, w_out, dec_gain, w_dec, target
):
    row_count = latent_grids.shape[1]
    feature_width = latent_grids.shape[2]
    window_rows = WINDOW
    band_index = lax.axis_index("grid")
    band_count = lax.axis_size("grid")
    total_slots = band_count * row_count
    current = latent_grids[0].astype(jnp.float32)
    normed = rms_norm(current, norm_gain).astype(jnp.bfloat16)
    query_raw = jnp.dot(normed, w_query, preferred_element_type=jnp.float32)
    key_raw = jnp.dot(normed, w_key, preferred_element_type=jnp.float32)
    value_raw = jnp.dot(normed, w_value, preferred_element_type=jnp.float32)
    query_bf = head_norm(query_raw).astype(jnp.bfloat16)
    pair_bf = jnp.concatenate(
        [head_norm(key_raw).astype(jnp.bfloat16), value_raw.astype(jnp.bfloat16)], 1
    )
    ext_pair = extended(pair_bf, (("grid", 0),), window_rows)
    query_pos = band_index * row_count + jnp.arange(row_count, dtype=jnp.int32)
    key_pos = (
        band_index * row_count
        - window_rows
        + jnp.arange(row_count + 2 * window_rows, dtype=jnp.int32)
    )
    in_window = jnp.abs(query_pos[:, None] - key_pos[None, :]) <= window_rows
    key_mask = (in_window & live_points(key_pos, cycle_points, total_slots)[None, :]).astype(
        jnp.float32
    )
    query_live = live_points(query_pos, cycle_points, total_slots).astype(jnp.float32)
    attended = attend(query_bf, ext_pair, key_mask).astype(jnp.bfloat16)
    level = current + jnp.dot(attended, w_out, preferred_element_type=jnp.float32)
    field, decode_back = jax.vjp(lambda level_in: decode(level_in, dec_gain, w_dec), level)
    field_bf = field.astype(jnp.bfloat16)
    whole_ensemble_decoding = lax.all_gather(field_bf[None], "member", axis=0, tiled=True).astype(
        jnp.float32
    )
    field_grad = crps_grad(
        field_bf[None].astype(jnp.float32), whole_ensemble_decoding, target, query_live
    )[0]
    level_grad = decode_back(field_grad)[0]
    level_grad_b = level_grad.astype(jnp.bfloat16)
    out_term = contract_rows(attended, level_grad_b)
    attended_grad = contract_cols(level_grad_b, w_out).astype(jnp.bfloat16)
    _, attend_back = jax.vjp(
        lambda query_in, pair_in: attend(query_in, pair_in, key_mask), query_bf, ext_pair
    )
    query_piece, pair_piece = attend_back(attended_grad.astype(jnp.float32))
    from_next = shifted(pair_piece[:window_rows], "grid", -1)
    from_prev = shifted(pair_piece[row_count + window_rows :], "grid", 1)
    pair_grad = pair_piece[window_rows : window_rows + row_count].astype(jnp.float32)
    pair_grad = pair_grad.at[:window_rows].add(from_prev.astype(jnp.float32))
    pair_grad = pair_grad.at[row_count - window_rows :].add(from_next.astype(jnp.float32))
    query_in = jax.vjp(head_norm, query_raw)[1](query_piece.astype(jnp.float32))[0].astype(
        jnp.bfloat16
    )
    key_source = jax.vjp(head_norm, key_raw)[1](pair_grad[:, :feature_width])[0].astype(
        jnp.bfloat16
    )
    value_in = pair_grad[:, feature_width:].astype(jnp.bfloat16)
    normed_grad = (
        contract_cols(query_in, w_query)
        + contract_cols(key_source, w_key)
        + contract_cols(value_in, w_value)
    )
    _, norm_back = jax.vjp(lambda state_in: rms_norm(state_in, norm_gain), current)
    latent_sensitivity = level_grad + norm_back(normed_grad)[0]
    partial_rows = lax.psum_scatter(
        out_term.astype(jnp.bfloat16), "grid", scatter_dimension=0, tiled=True
    )
    weight_part = lax.psum_scatter(partial_rows, "member", scatter_dimension=1, tiled=True).astype(
        jnp.float32
    )
    return (field_bf[None], latent_sensitivity[None], weight_part)


def solution(mesh):
    placed = (P("member", "grid", None), P(), P(), P(), P(), P(), P(), P(), P(), P(None, "grid"))
    return jax.shard_map(
        body,
        mesh=mesh,
        in_specs=placed,
        out_specs=(P("member", None, "grid"), P("member", "grid", None), P("grid", "member")),
        check_vma=False,
    )
```

profile of v0, /device:TPU:24, one launch (start us, length us, event | category | flops | bytes accessed | tf_op | source)
XLA Modules:
  0.0 436.2 jit_solution(15268301374989435230)
XLA Ops:
  27.9 5.9 %collective-permute-start.1 = (bf16[256,2048]{1,0:T(8,128)(2,1)}, bf16[256,2048]{1,0:T(8,128)(2,1)}, u32[]{:S(2)}, u32[]{:S(2)}) collective-permute-start(bf16[256,2048]{1,0:T(8,128)(2,1)} %get-tuple-element.566), channel_id=1, source_target_pairs={{1,0},{2,1},{3,2},{4,3},{5,4},{6,5},{7,6},{8,7},{9,8},{10,9},{11,1... | collective-permute-start | bytes 3145736 | tf_op jit(solution)/shard_map/ppermute | solution.py:19
  59.4 30.8 %while.51 = (s32[]{:T(128)}, bf16[4,512,4,64]{1,3,2,0:T(8,128)(2,1)}, bf16[4,1024,4,64]{1,3,2,0:T(8,128)(2,1)}, bf16[4,512,4,64]{1,3,2,0:T(8,128)(2,1)}, bf16[4,...) while((s32[]{:T(128)}, ...), condition=%wide.region_6.7_spmd.clone, body=%wide.region_4.6_spmd.clone.sunk | while | flops 554170368 | bytes 24929372 | solution.py:76
  93.4 36.1 %all-gather.1 = bf16[8,100,512]{2,1,0:T(8,128)(2,1)S(1)} all-gather(bf16[1,100,512]{2,1,0:T(8,128)(2,1)S(1)} %bitcast.266), channel_id=2, replica_groups=mesh['member'=8,'grid'=16] {'member'}, dimensions={0}, use_global_device_ids=true | all-gather | bytes 921600 | tf_op jit(solution)/shard_map/all_gather | solution.py:143
  138.6 57.2 %while.52 = (s32[]{:T(128)}, f32[4,4,512,1024]{3,2,1,0:T(8,128)}, f32[4,4,512,1]{2,1,3,0:T(4,128)S(1)}, f32[4,4,512,1024]{3,2,1,0:T(8,128)}, f32[4,4,512,1]{2,1,...) while((s32[]{:T(128)}, f32[4,4,512,1024]{3,2,1,0:T(8,128)}, ...), condition=%wide.region_13.14_spmd.clone, body=%wide.region_11.13_spmd.clone.sunk | while | flops 289933312 | bytes 55362680 | solution.py:76
  139.2 8.7 %bitcast_dynamic-update-slice_fusion.6 = (f32[4,4,512,1024]{3,2,1,0:T(8,128)}, f32[4,4,512,1024]{3,2,1,0:T(8,128)}, f32[4,512,1024]{2,1,0:T(8,128)S(1)}) fusion(f32[4,4,512,1024]{3,2,1,0:T(8,128)} %get-tuple-element.860, s32[]{:T(128)} %get-tuple-element.857, f32[512,1024]{1,0:T(8,128)S(1)} %convert_bitcast_fusion.5, ...), kind=kOutput, calls=%fused_computation.22.clone.1 | convolution fusion | flops 272629760 | bytes 28050944 | tf_op jit(solution)/shard_map/jvp()/while/body/eval_jaxpr/rhd,ehd->hre/dot_general | solution.py:68
  153.5 8.7 %bitcast_dynamic-update-slice_fusion.6 = (f32[4,4,512,1024]{3,2,1,0:T(8,128)}, f32[4,4,512,1024]{3,2,1,0:T(8,128)}, f32[4,512,1024]{2,1,0:T(8,128)S(1)}) fusion(f32[4,4,512,1024]{3,2,1,0:T(8,128)} %get-tuple-element.860, s32[]{:T(128)} %get-tuple-element.857, f32[512,1024]{1,0:T(8,128)S(1)} %convert_bitcast_fusion.5, ...), kind=kOutput, calls=%fused_computation.22.clone.1 | convolution fusion | flops 272629760 | bytes 28050944 | tf_op jit(solution)/shard_map/jvp()/while/body/eval_jaxpr/rhd,ehd->hre/dot_general | solution.py:68
  167.8 8.7 %bitcast_dynamic-update-slice_fusion.6 = (f32[4,4,512,1024]{3,2,1,0:T(8,128)}, f32[4,4,512,1024]{3,2,1,0:T(8,128)}, f32[4,512,1024]{2,1,0:T(8,128)S(1)}) fusion(f32[4,4,512,1024]{3,2,1,0:T(8,128)} %get-tuple-element.860, s32[]{:T(128)} %get-tuple-element.857, f32[512,1024]{1,0:T(8,128)S(1)} %convert_bitcast_fusion.5, ...), kind=kOutput, calls=%fused_computation.22.clone.1 | convolution fusion | flops 272629760 | bytes 28050944 | tf_op jit(solution)/shard_map/jvp()/while/body/eval_jaxpr/rhd,ehd->hre/dot_general | solution.py:68
  182.2 8.7 %bitcast_dynamic-update-slice_fusion.6 = (f32[4,4,512,1024]{3,2,1,0:T(8,128)}, f32[4,4,512,1024]{3,2,1,0:T(8,128)}, f32[4,512,1024]{2,1,0:T(8,128)S(1)}) fusion(f32[4,4,512,1024]{3,2,1,0:T(8,128)} %get-tuple-element.860, s32[]{:T(128)} %get-tuple-element.857, f32[512,1024]{1,0:T(8,128)S(1)} %convert_bitcast_fusion.5, ...), kind=kOutput, calls=%fused_computation.22.clone.1 | convolution fusion | flops 272629760 | bytes 28050944 | tf_op jit(solution)/shard_map/jvp()/while/body/eval_jaxpr/rhd,ehd->hre/dot_general | solution.py:68
  200.2 83.0 %while.53 = (s32[]{:T(128)}, bf16[4,512,4,64]{1,3,2,0:T(8,128)(2,1)}, bf16[4,1024,4,64]{1,3,2,0:T(8,128)(2,1)}, bf16[4,1024,4,64]{1,3,2,0:T(8,128)(2,1)}, bf16[4...) while((s32[]{:T(128)}, ...), condition=%wide.region_16.17_spmd.clone, body=%wide.region_14.16_spmd.clone.sunk | while | flops 1110310912 | bytes 51492020 | solution.py:76
  200.2 5.2 %fusion.185 = (f32[4,512]{1,0:T(4,128)S(1)}, bf16[4,512,1024]{2,1,0:T(8,128)(2,1)S(1)}) fusion(f32[4,4,512,1024]{3,2,1,0:T(8,128)} %get-tuple-element.925, s32[]{:T(128)S(6)} %sub.209, f32[4,512]{1,0:T(4,128)S(1)} %get-tuple-element.814, bf16[4,1024,4,64]{1,3,2,0:T(8,128)(2,1)} %get-tuple-element.922, bf16[4,512,4,64]{1,3,2,0:T(8,128)(2,1)} %get-tuple-element.921), kind=kOutput, calls=%fused_computation.48.clone.1 | convolution fusion | flops 276822016 | bytes 13387264 | tf_op jit(solution)/shard_map/transpose(jvp())/while/body/eval_jaxpr/hre,ehd->rhd/dot_general | solution.py:74
  206.0 5.6 %fusion.187 = bf16[4,1024,4,64]{1,3,2,0:T(8,128)(2,1)} fusion(bf16[4,1024,4,64]{1,3,2,0:T(8,128)(2,1)} %get-tuple-element.901, s32[]{:T(128)S(6)} %sub.209, bf16[4,512,4,64]{1,3,2,0:T(8,128)(2,1)S(1)} %get-tuple-element.928, bf16[4,512,1024]{2,1,0:T(8,128)(2,1)S(1)} %get-tuple-element.815, f32[4,4,512,1024]{3,2,1,0:T(8,128)} %get-tuple-element.926, ...), kind=kOutput, calls=%fused_computation.61.clone.1 | convolution fusion | flops 281280512 | bytes 15484416 | tf_op jit(solution)/shard_map/transpose(jvp())/while/body/eval_jaxpr/rhd,ehd->hre/dot_general | solution.py:68
  211.6 5.5 %fusion.186 = bf16[4,512,4,64]{1,3,2,0:T(8,128)(2,1)} fusion(bf16[4,512,4,64]{1,3,2,0:T(8,128)(2,1)} %get-tuple-element.900, s32[]{:T(128)S(6)} %sub.209, bf16[4,1024,4,64]{1,3,2,0:T(8,128)(2,1)} %get-tuple-element.927, bf16[4,512,1024]{2,1,0:T(8,128)(2,1)S(1)} %get-tuple-element.815, f32[4,4,512,1024]{3,2,1,0:T(8,128)} %get-tuple-element.926, ...), kind=kOutput, calls=%fused_computation.64.clone.1 | convolution fusion | flops 281149440 | bytes 15484416 | tf_op jit(solution)/shard_map/transpose(jvp())/while/body/eval_jaxpr/rhd,ehd->hre/dot_general | solution.py:68
  221.0 5.2 %fusion.185 = (f32[4,512]{1,0:T(4,128)S(1)}, bf16[4,512,1024]{2,1,0:T(8,128)(2,1)S(1)}) fusion(f32[4,4,512,1024]{3,2,1,0:T(8,128)} %get-tuple-element.925, s32[]{:T(128)S(6)} %sub.209, f32[4,512]{1,0:T(4,128)S(1)} %get-tuple-element.814, bf16[4,1024,4,64]{1,3,2,0:T(8,128)(2,1)} %get-tuple-element.922, bf16[4,512,4,64]{1,3,2,0:T(8,128)(2,1)} %get-tuple-element.921), kind=kOutput, calls=%fused_computation.48.clone.1 | convolution fusion | flops 276822016 | bytes 13387264 | tf_op jit(solution)/shard_map/transpose(jvp())/while/body/eval_jaxpr/hre,ehd->rhd/dot_general | solution.py:74
  226.8 5.5 %fusion.187 = bf16[4,1024,4,64]{1,3,2,0:T(8,128)(2,1)} fusion(bf16[4,1024,4,64]{1,3,2,0:T(8,128)(2,1)} %get-tuple-element.901, s32[]{:T(128)S(6)} %sub.209, bf16[4,512,4,64]{1,3,2,0:T(8,128)(2,1)S(1)} %get-tuple-element.928, bf16[4,512,1024]{2,1,0:T(8,128)(2,1)S(1)} %get-tuple-element.815, f32[4,4,512,1024]{3,2,1,0:T(8,128)} %get-tuple-element.926, ...), kind=kOutput, calls=%fused_computation.61.clone.1 | convolution fusion | flops 281280512 | bytes 15484416 | tf_op jit(solution)/shard_map/transpose(jvp())/while/body/eval_jaxpr/rhd,ehd->hre/dot_general | solution.py:68
  232.4 5.5 %fusion.186 = bf16[4,512,4,64]{1,3,2,0:T(8,128)(2,1)} fusion(bf16[4,512,4,64]{1,3,2,0:T(8,128)(2,1)} %get-tuple-element.900, s32[]{:T(128)S(6)} %sub.209, bf16[4,1024,4,64]{1,3,2,0:T(8,128)(2,1)} %get-tuple-element.927, bf16[4,512,1024]{2,1,0:T(8,128)(2,1)S(1)} %get-tuple-element.815, f32[4,4,512,1024]{3,2,1,0:T(8,128)} %get-tuple-element.926, ...), kind=kOutput, calls=%fused_computation.64.clone.1 | convolution fusion | flops 281149440 | bytes 15484416 | tf_op jit(solution)/shard_map/transpose(jvp())/while/body/eval_jaxpr/rhd,ehd->hre/dot_general | solution.py:68
  241.8 5.2 %fusion.185 = (f32[4,512]{1,0:T(4,128)S(1)}, bf16[4,512,1024]{2,1,0:T(8,128)(2,1)S(1)}) fusion(f32[4,4,512,1024]{3,2,1,0:T(8,128)} %get-tuple-element.925, s32[]{:T(128)S(6)} %sub.209, f32[4,512]{1,0:T(4,128)S(1)} %get-tuple-element.814, bf16[4,1024,4,64]{1,3,2,0:T(8,128)(2,1)} %get-tuple-element.922, bf16[4,512,4,64]{1,3,2,0:T(8,128)(2,1)} %get-tuple-element.921), kind=kOutput, calls=%fused_computation.48.clone.1 | convolution fusion | flops 276822016 | bytes 13387264 | tf_op jit(solution)/shard_map/transpose(jvp())/while/body/eval_jaxpr/hre,ehd->rhd/dot_general | solution.py:74
  247.6 5.5 %fusion.187 = bf16[4,1024,4,64]{1,3,2,0:T(8,128)(2,1)} fusion(bf16[4,1024,4,64]{1,3,2,0:T(8,128)(2,1)} %get-tuple-element.901, s32[]{:T(128)S(6)} %sub.209, bf16[4,512,4,64]{1,3,2,0:T(8,128)(2,1)S(1)} %get-tuple-element.928, bf16[4,512,1024]{2,1,0:T(8,128)(2,1)S(1)} %get-tuple-element.815, f32[4,4,512,1024]{3,2,1,0:T(8,128)} %get-tuple-element.926, ...), kind=kOutput, calls=%fused_computation.61.clone.1 | convolution fusion | flops 281280512 | bytes 15484416 | tf_op jit(solution)/shard_map/transpose(jvp())/while/body/eval_jaxpr/rhd,ehd->hre/dot_general | solution.py:68
  253.1 5.5 %fusion.186 = bf16[4,512,4,64]{1,3,2,0:T(8,128)(2,1)} fusion(bf16[4,512,4,64]{1,3,2,0:T(8,128)(2,1)} %get-tuple-element.900, s32[]{:T(128)S(6)} %sub.209, bf16[4,1024,4,64]{1,3,2,0:T(8,128)(2,1)} %get-tuple-element.927, bf16[4,512,1024]{2,1,0:T(8,128)(2,1)S(1)} %get-tuple-element.815, f32[4,4,512,1024]{3,2,1,0:T(8,128)} %get-tuple-element.926, ...), kind=kOutput, calls=%fused_computation.64.clone.1 | convolution fusion | flops 281149440 | bytes 15484416 | tf_op jit(solution)/shard_map/transpose(jvp())/while/body/eval_jaxpr/rhd,ehd->hre/dot_general | solution.py:68
  262.5 5.2 %fusion.185 = (f32[4,512]{1,0:T(4,128)S(1)}, bf16[4,512,1024]{2,1,0:T(8,128)(2,1)S(1)}) fusion(f32[4,4,512,1024]{3,2,1,0:T(8,128)} %get-tuple-element.925, s32[]{:T(128)S(6)} %sub.209, f32[4,512]{1,0:T(4,128)S(1)} %get-tuple-element.814, bf16[4,1024,4,64]{1,3,2,0:T(8,128)(2,1)} %get-tuple-element.922, bf16[4,512,4,64]{1,3,2,0:T(8,128)(2,1)} %get-tuple-element.921), kind=kOutput, calls=%fused_computation.48.clone.1 | convolution fusion | flops 276822016 | bytes 13387264 | tf_op jit(solution)/shard_map/transpose(jvp())/while/body/eval_jaxpr/hre,ehd->rhd/dot_general | solution.py:74
  268.3 5.5 %fusion.187 = bf16[4,1024,4,64]{1,3,2,0:T(8,128)(2,1)} fusion(bf16[4,1024,4,64]{1,3,2,0:T(8,128)(2,1)} %get-tuple-element.901, s32[]{:T(128)S(6)} %sub.209, bf16[4,512,4,64]{1,3,2,0:T(8,128)(2,1)S(1)} %get-tuple-element.928, bf16[4,512,1024]{2,1,0:T(8,128)(2,1)S(1)} %get-tuple-element.815, f32[4,4,512,1024]{3,2,1,0:T(8,128)} %get-tuple-element.926, ...), kind=kOutput, calls=%fused_computation.61.clone.1 | convolution fusion | flops 281280512 | bytes 15484416 | tf_op jit(solution)/shard_map/transpose(jvp())/while/body/eval_jaxpr/rhd,ehd->hre/dot_general | solution.py:68
  273.8 5.5 %fusion.186 = bf16[4,512,4,64]{1,3,2,0:T(8,128)(2,1)} fusion(bf16[4,512,4,64]{1,3,2,0:T(8,128)(2,1)} %get-tuple-element.900, s32[]{:T(128)S(6)} %sub.209, bf16[4,1024,4,64]{1,3,2,0:T(8,128)(2,1)} %get-tuple-element.927, bf16[4,512,1024]{2,1,0:T(8,128)(2,1)S(1)} %get-tuple-element.815, f32[4,4,512,1024]{3,2,1,0:T(8,128)} %get-tuple-element.926, ...), kind=kOutput, calls=%fused_computation.64.clone.1 | convolution fusion | flops 281149440 | bytes 15484416 | tf_op jit(solution)/shard_map/transpose(jvp())/while/body/eval_jaxpr/rhd,ehd->hre/dot_general | solution.py:68
  288.5 5.8 %collective-permute-start.3 = (bf16[256,2048]{0,1:T(8,128)(2,1)}, bf16[256,2048]{0,1:T(8,128)(2,1)}, u32[]{:S(2)}, u32[]{:S(2)}) collective-permute-start(bf16[256,2048]{0,1:T(8,128)(2,1)} %get-tuple-element.561), channel_id=1, source_target_pairs={{1,0},{2,1},{3,2},{4,3},{5,4},{6,5},{7,6},{8,7},{9,8},{10,9},{11,1... | collective-permute-start | bytes 3145736 | tf_op jit(solution)/shard_map/ppermute | solution.py:27
  318.8 37.6 %reduce-scatter.5.cloned.1.call-done = bf16[64,1024]{1,0:T(8,128)(2,1)} async-done(((bf16[1024,1024]{1,0:T(8,128)(2,1)}), bf16[64,1024]{1,0:T(8,128)(2,1)}) %reduce-scatter.5.cloned.1.call-update) | async-done | bytes 131088 | tf_op jit(solution)/shard_map/reduce_scatter | solution.py:176
  363.0 64.8 %reduce-scatter.7.cloned.1.call-done = bf16[128,64]{1,0:T(8,128)(2,1)} async-done(((bf16[1024,64]{1,0:T(8,128)(2,1)}), bf16[128,64]{1,0:T(8,128)(2,1)}) %reduce-scatter.7.cloned.1.call-update) | async-done | bytes 16400
  (204 shorter events, 171.6 us)
Async XLA Ops:
  7.2 83.0 %copy-start = (bf16[1024,1024]{1,0:T(8,128)(2,1)S(1)}, bf16[1024,1024]{1,0:T(8,128)(2,1)}, u32[]{:S(2)}) copy-start(bf16[1024,1024]{1,0:T(8,128)(2,1)} %param.26) | copy-start | bytes 6291460
  7.2 349.2 %reduce-scatter.5.cloned.1.call-start = ((), (), s32[]{:S(2)}) async-start(), calls=%async_computation.2 | async-start | bytes 2228224 | tf_op jit(solution)/shard_map/reduce_scatter | solution.py:176
  9.4 28.7 %copy-start.40 = (f32[512]{0:T(512)}, f32[512]{0:T(512)S(1)}, u32[]{:S(2)}) copy-start(f32[512]{0:T(512)S(1)} %fusion.138) | copy-start | bytes 6148
  26.0 18.5 %collective-permute-start = (bf16[256,2048]{1,0:T(8,128)(2,1)}, bf16[256,2048]{1,0:T(8,128)(2,1)}, u32[]{:S(2)}, u32[]{:S(2)}) collective-permute-start(bf16[256,2048]{1,0:T(8,128)(2,1)} %get-tuple-element.565), channel_id=1, source_target_pairs={{0,1},{1,2},{2,3},{3,4},{4,5},{5,6},{6,7},{7,8},{8,9},{9,10},{10,1... | collective-permute-start | bytes 3145736 | tf_op jit(solution)/shard_map/ppermute | solution.py:18
  27.9 18.4 %collective-permute-start.1 = (bf16[256,2048]{1,0:T(8,128)(2,1)}, bf16[256,2048]{1,0:T(8,128)(2,1)}, u32[]{:S(2)}, u32[]{:S(2)}) collective-permute-start(bf16[256,2048]{1,0:T(8,128)(2,1)} %get-tuple-element.566), channel_id=1, source_target_pairs={{1,0},{2,1},{3,2},{4,3},{5,4},{6,5},{7,6},{8,7},{9,8},{10,9},{11,1... | collective-permute-start | bytes 3145736 | tf_op jit(solution)/shard_map/ppermute | solution.py:19
  41.1 5.1 %copy-start.30 = (f32[512,16]{0,1:T(8,128)}, f32[512,16]{0,1:T(8,128)S(1)}, u32[]{:S(2)}) copy-start(f32[512,16]{0,1:T(8,128)S(1)} %get-tuple-element.569) | copy-start | bytes 98308
  41.1 5.1 %copy-start.13 = (bf16[512,1024]{1,0:T(8,128)(2,1)S(1)}, bf16[512,1024]{1,0:T(8,128)(2,1)}, u32[]{:S(2)}) copy-start(bf16[512,1024]{1,0:T(8,128)(2,1)} %copy.32) | copy-start | bytes 3145732
  41.1 5.1 %copy-start.16 = (bf16[512,1024]{1,0:T(8,128)(2,1)S(1)}, bf16[512,1024]{1,0:T(8,128)(2,1)}, u32[]{:S(2)}) copy-start(bf16[512,1024]{1,0:T(8,128)(2,1)} %copy-done.15) | copy-start | bytes 3145732
  92.8 40.3 %copy-start.2 = (f32[512,1024]{1,0:T(8,128)}, f32[512,1024]{1,0:T(8,128)S(1)}, u32[]{:S(2)}) copy-start(f32[512,1024]{1,0:T(8,128)S(1)} %get-tuple-element.572) | copy-start | bytes 6291460
  92.8 40.3 %copy-start.36 = (f32[512]{0:T(512)}, f32[512]{0:T(512)S(1)}, u32[]{:S(2)}) copy-start(f32[512]{0:T(512)S(1)} %fusion.139) | copy-start | bytes 6148
  92.9 37.1 %copy-start.27 = (f32[100,512]{1,0:T(8,128)S(1)}, f32[100,512]{1,0:T(8,128)}, u32[]{:S(2)}) copy-start(f32[100,512]{1,0:T(8,128)} %param.29) | copy-start | bytes 614404
  93.4 37.2 %copy-start.21 = (bf16[512,100]{0,1:T(8,128)(2,1)}, bf16[512,100]{0,1:T(8,128)(2,1)S(1)}, u32[]{:S(2)}) copy-start(bf16[512,100]{0,1:T(8,128)(2,1)S(1)} %get-tuple-element.574) | copy-start | bytes 307204
  133.1 4.2 copy-start.20
  283.3 11.0 %copy-start.4 = (f32[512,16,64]{0,2,1:T(8,128)S(1)}, f32[512,16,64]{0,2,1:T(8,128)}, u32[]{:S(2)}) copy-start(f32[512,16,64]{0,2,1:T(8,128)} %copy-done.3) | copy-start | bytes 6291460
  283.3 11.0 %copy-start.11 = (bf16[4,512,4,64]{1,3,2,0:T(8,128)(2,1)S(1)}, bf16[4,512,4,64]{1,3,2,0:T(8,128)(2,1)}, u32[]{:S(2)}) copy-start(bf16[4,512,4,64]{1,3,2,0:T(8,128)(2,1)} %get-tuple-element.392) | copy-start | bytes 3145732
  286.5 8.2 %copy-start.31 = (f32[512,16]{0,1:T(8,128)S(1)}, f32[512,16]{0,1:T(8,128)}, u32[]{:S(2)}) copy-start(f32[512,16]{0,1:T(8,128)} %copy-done.30) | copy-start | bytes 98308
  286.5 18.7 %collective-permute-start.2 = (bf16[256,2048]{0,1:T(8,128)(2,1)}, bf16[256,2048]{0,1:T(8,128)(2,1)}, u32[]{:S(2)}, u32[]{:S(2)}) collective-permute-start(bf16[256,2048]{0,1:T(8,128)(2,1)} %get-tuple-element.562), channel_id=1, source_target_pairs={{0,1},{1,2},{2,3},{3,4},{4,5},{5,6},{6,7},{7,8},{8,9},{9,10},{10,1... | collective-permute-start | bytes 3145736 | tf_op jit(solution)/shard_map/ppermute | solution.py:27
  288.5 19.8 %collective-permute-start.3 = (bf16[256,2048]{0,1:T(8,128)(2,1)}, bf16[256,2048]{0,1:T(8,128)(2,1)}, u32[]{:S(2)}, u32[]{:S(2)}) collective-permute-start(bf16[256,2048]{0,1:T(8,128)(2,1)} %get-tuple-element.561), channel_id=1, source_target_pairs={{1,0},{2,1},{3,2},{4,3},{5,4},{6,5},{7,6},{8,7},{9,8},{10,9},{11,1... | collective-permute-start | bytes 3145736 | tf_op jit(solution)/shard_map/ppermute | solution.py:27
  294.8 133.1 %reduce-scatter.7.cloned.1.call-start = ((), (), s32[]{:S(2)}) async-start(), calls=%async_computation.3 | async-start | bytes 294912
  315.9 42.2 %copy-start.33 = (f32[1024]{0:T(1024)S(1)}, f32[1024]{0:T(1024)}, u32[]{:S(2)}) copy-start(f32[1024]{0:T(1024)} %param.27) | copy-start | bytes 12292
  315.9 42.2 %copy-start.37 = (f32[512]{0:T(512)S(1)}, f32[512]{0:T(512)}, u32[]{:S(2)}) copy-start(f32[512]{0:T(512)} %copy-done.36) | copy-start | bytes 6148
  315.9 42.2 %copy-start.39 = (f32[512]{0:T(512)S(1)}, f32[512]{0:T(512)}, u32[]{:S(2)}) copy-start(f32[512]{0:T(512)} %copy-done.38) | copy-start | bytes 6148
  316.0 42.2 %copy-start.41 = (f32[512]{0:T(512)S(1)}, f32[512]{0:T(512)}, u32[]{:S(2)}) copy-start(f32[512]{0:T(512)} %copy-done.40) | copy-start | bytes 6148
  358.2 71.1 %copy-start.1 = (bf16[1024,1024]{1,0:T(8,128)(2,1)S(1)}, bf16[1024,1024]{1,0:T(8,128)(2,1)}, u32[]{:S(2)}) copy-start(bf16[1024,1024]{1,0:T(8,128)(2,1)} %param.26) | copy-start | bytes 6291460
  (27 other events, 57.3 us)
Sparse Core Ops, SparseCore 0:
  294.9 61.4 reduce-scatter.4
  359.9 67.8 reduce-scatter.6
where the time goes:
time: 439 us; the launch traced here: 436 us
  matrix products  168 us (38%)
  waiting for transfers between devices  112 us (26%)
  other arithmetic  52.6 us (12%)
  local copies, waits for them, and re-layouts  36.7 us (8%)
  blocking collectives  36.1 us (8%)
  starting transfers between devices  16 us (4%)
  between operations  14.7 us (3%)
    dot_general x16, matrix products, head_block(): jnp.einsum('rhd,ehd->hre', q_blk, k_blk, preferred_element_type=jnp.float32)  91.9 us
    unnamed x3, waiting for transfers between devices  64.9 us
    dot_general x12, matrix products, head_block(): jnp.einsum('hre,ehd->rhd', weights_bf, v_blk, preferred_element_type=jnp....  51.7 us
    reduce_scatter x1, waiting for transfers between devices, body(): lax.psum_scatter(out_term.astype(jnp.bfloat16), 'grid', scatter_dimension...  37.6 us
    all_gather x1, blocking collectives, body(): lax.all_gather(field_bf[None], 'member', axis=0, tiled=True)  36.1 us
    unnamed x94, local copies, waits for them, and re-layouts  18.2 us
    dynamic_update_slice x8, other arithmetic, attend(): blocks = lax.map(head_block, (queries, key_part, value_part))  13.6 us
  transfers between devices with their start and end apart: 6, of which 6 were waited for; matrix products, arithmetic and copies ran while one was open for 6% of the time, Pallas kernels for 0%

commit v1 on v0

v1 whole, which is shorter than its diff:
```python
import jax
import jax.numpy as jnp
from jax import lax
from jax.experimental import pallas as pl
from jax.experimental.pallas import tpu as pltpu
from jax.sharding import PartitionSpec as P

HEAD_DIM = 64
CYCLE_MAX = 128
WINDOW = 256
ROWS = 512
EXT = 1024
WIDTH = 1024
PAIR = 128
PAIRS = 8
LOG2E = 1.4426950408889634
Q_SCALE = LOG2E * HEAD_DIM**-0.5
DEAD = -30000.0
F32 = jnp.float32
BF16 = jnp.bfloat16


def params(**more):
    return pltpu.CompilerParams(vmem_limit_bytes=56 * 1024 * 1024, **more)


def dot(left, right):
    return lax.dot_general(left, right, (((1,), (0,)), ((), ())), preferred_element_type=F32)


def dot_t(left, right):
    return lax.dot_general(left, right, (((1,), (1,)), ((), ())), preferred_element_type=F32)


def lane(shape):
    return lax.broadcasted_iota(jnp.int32, shape, len(shape) - 1)


def head_mean_matrix(width):
    rows = lax.broadcasted_iota(jnp.int32, (width, width), 0) // HEAD_DIM
    cols = lax.broadcasted_iota(jnp.int32, (width, width), 1) // HEAD_DIM
    return jnp.where(rows == cols, 1.0 / HEAD_DIM, 0.0).astype(BF16)


def normed_rows(x_ref, gain_ref):
    x = x_ref[...].astype(F32)
    scale = lax.rsqrt(jnp.mean(x * x, -1, keepdims=True) + 1e-05)
    return (x * scale * gain_ref[...]).astype(BF16)


def qkv_kernel(x_ref, gain_ref, wq_ref, wk_ref, wv_ref, q_ref, k_ref, v_ref, rq_ref, rk_ref, normed):
    @pl.when(pl.program_id(0) == 0)
    def _():
        normed[...] = normed_rows(x_ref, gain_ref)

    means = head_mean_matrix(256)

    def normalised(raw):
        return lax.rsqrt(dot((raw * raw).astype(BF16), means) + 1e-06)

    rows = normed[...]
    raw = dot(rows, wq_ref[...])
    scale = normalised(raw)
    q_ref[...] = (raw * scale * Q_SCALE).astype(BF16)
    rq_ref[...] = scale.astype(BF16)
    raw = dot(rows, wk_ref[...])
    scale = normalised(raw)
    k_ref[...] = (raw * scale).astype(BF16)
    rk_ref[...] = scale.astype(BF16)
    v_ref[...] = dot(rows, wv_ref[...]).astype(BF16)


def kv_kernel(before_ref, after_ref, gain_ref, wk_ref, wv_ref, k_ref, v_ref, normed):
    @pl.when(pl.program_id(0) == 0)
    def _():
        normed[:256] = normed_rows(before_ref, gain_ref)
        normed[256:] = normed_rows(after_ref, gain_ref)

    means = head_mean_matrix(256)
    rows = normed[...]
    raw = dot(rows, wk_ref[...])
    scale = lax.rsqrt(dot((raw * raw).astype(BF16), means) + 1e-06)
    k_ref[...] = (raw * scale).astype(BF16)
    v_ref[...] = dot(rows, wv_ref[...]).astype(BF16)


def project(x, gain, wq, wk, wv):
    whole = pl.BlockSpec((ROWS, WIDTH), lambda c: (0, 0))
    gains = pl.BlockSpec((1, WIDTH), lambda c: (0, 0))
    weight = pl.BlockSpec((WIDTH, 256), lambda c: (0, c))
    out = pl.BlockSpec((ROWS, 256), lambda c: (0, c))
    shape = jax.ShapeDtypeStruct((ROWS, WIDTH), BF16)
    return pl.pallas_call(
        qkv_kernel,
        grid=(4,),
        in_specs=[whole, gains, weight, weight, weight],
        out_specs=[out] * 5,
        out_shape=[shape] * 5,
        scratch_shapes=[pltpu.VMEM((ROWS, WIDTH), BF16)],
        compiler_params=params(),
        name="project_own",
    )(x, gain, wq, wk, wv)


def project_halo(before, after, gain, wk, wv):
    part = pl.BlockSpec((256, WIDTH), lambda c: (0, 0))
    gains = pl.BlockSpec((1, WIDTH), lambda c: (0, 0))
    weight = pl.BlockSpec((WIDTH, 256), lambda c: (0, c))
    out = pl.BlockSpec((ROWS, 256), lambda c: (0, c))
    shape = jax.ShapeDtypeStruct((ROWS, WIDTH), BF16)
    return pl.pallas_call(
        kv_kernel,
        grid=(4,),
        in_specs=[part, part, gains, weight, weight],
        out_specs=[out] * 2,
        out_shape=[shape] * 2,
        scratch_shapes=[pltpu.VMEM((ROWS, WIDTH), BF16)],
        compiler_params=params(),
        name="project_halo",
    )(before, after, gain, wk, wv)


def key_extras(live_ref):
    pieces = []
    lanes = lane((CYCLE_MAX, PAIR))
    slots = lax.broadcasted_iota(jnp.int32, (CYCLE_MAX, PAIR), 0)
    for cycle in range(EXT // CYCLE_MAX):
        bias = jnp.where(slots < live_ref[cycle], 0.0, DEAD)
        pieces.append(jnp.where(lanes == 0, bias, jnp.where(lanes < 3, 1.0, 0.0)).astype(BF16))
    return pieces


def fill_ext(ext, own_ref, halo_ref):
    ext[:256, :PAIR] = halo_ref[:256]
    ext[256:768, :PAIR] = own_ref[...]
    ext[768:, :PAIR] = halo_ref[256:]


def by_head(value, low):
    zero = jnp.zeros_like(value)
    return jnp.concatenate([jnp.where(low, value, zero), jnp.where(low, zero, value)], 0)


def window_masks():
    rows = lax.broadcasted_iota(jnp.int32, (512, 256), 0) & 255
    cols = lax.broadcasted_iota(jnp.int32, (512, 256), 1)
    return cols >= rows, cols <= rows


def forward_kernel(live_ref, q_ref, k_ref, kh_ref, v_ref, vh_ref, att_ref, eq_ref, kx, vx):
    @pl.when(pl.program_id(0) == 0)
    def _():
        for cycle, piece in enumerate(key_extras(live_ref)):
            kx[cycle * CYCLE_MAX : (cycle + 1) * CYCLE_MAX, PAIR:] = piece
        vx[:, PAIR:] = jnp.ones((EXT, PAIR), BF16)

    fill_ext(kx, k_ref, kh_ref)
    fill_ext(vx, v_ref, vh_ref)
    low = lane((256, PAIR)) < HEAD_DIM
    lanes = lane((512, PAIR))
    one = jnp.where(lanes == 0, 1.0, 0.0).astype(BF16)
    first, last = window_masks()
    for block in range(2):
        left = jnp.concatenate([by_head(q_ref[block * 256 : block * 256 + 256], low), one], 1)
        total = None
        for tile in range(3):
            keys = slice((block + tile) * 256, (block + tile + 1) * 256)
            weights = jnp.exp2(dot_t(left, kx[keys]))
            if tile == 0:
                weights = jnp.where(first, weights, 0.0)
            if tile == 2:
                weights = jnp.where(last, weights, 0.0)
            term = dot(weights.astype(BF16), vx[keys])
            total = term if total is None else total + term
        sums = total[:, PAIR:]
        out = total[:, :PAIR] / sums
        att_ref[block * 256 : block * 256 + 256] = jnp.where(low, out[:256], out[256:]).astype(BF16)
        shift = -jnp.log2(sums)
        high = shift.astype(BF16).astype(F32)
        extras = jnp.where(
            lanes == 0, 1.0, jnp.where(lanes == 1, high, jnp.where(lanes == 2, shift - high, 0.0))
        )
        eq_ref[0, block * 512 : block * 512 + 512] = extras.astype(BF16)


def attention_forward(live, q, k, kh, v, vh):
    part = pl.BlockSpec((ROWS, PAIR), lambda h, _: (0, h))
    return pl.pallas_call(
        forward_kernel,
        grid_spec=pltpu.PrefetchScalarGridSpec(
            num_scalar_prefetch=1,
            grid=(PAIRS,),
            in_specs=[part] * 5,
            out_specs=[part, pl.BlockSpec((1, EXT, PAIR), lambda h, _: (h, 0, 0))],
            scratch_shapes=[pltpu.VMEM((EXT, 2 * PAIR), BF16), pltpu.VMEM((EXT, 2 * PAIR), BF16)],
        ),
        out_shape=[
            jax.ShapeDtypeStruct((ROWS, WIDTH), BF16),
            jax.ShapeDtypeStruct((PAIRS, EXT, PAIR), BF16),
        ],
        compiler_params=params(),
        name="attention_forward",
    )(live, q, k, kh, v, vh)


def backward_kernel(
    live_ref, q_ref, k_ref, kh_ref, v_ref, vh_ref, eq_ref, att_ref, da_ref,
    dq_ref, dk_ref, dv_ref, dkh_ref, dvh_ref, kx, vx, dkt, dvt,
):
    @pl.when(pl.program_id(0) == 0)
    def _():
        for cycle, piece in enumerate(key_extras(live_ref)):
            kx[cycle * CYCLE_MAX : (cycle + 1) * CYCLE_MAX, PAIR:] = piece
            vx[cycle * CYCLE_MAX : (cycle + 1) * CYCLE_MAX, PAIR:] = piece

    fill_ext(kx, k_ref, kh_ref)
    fill_ext(vx, v_ref, vh_ref)
    low = lane((256, PAIR)) < HEAD_DIM
    lanes = lane((512, PAIR))
    first, last = window_masks()
    feature = lax.broadcasted_iota(jnp.int32, (PAIR, 2 * PAIR), 0) // HEAD_DIM
    column = lane((PAIR, 2 * PAIR))
    wanted = (feature == column // PAIR) & ((column % PAIR == 1) | (column % PAIR == 2))
    summing = jnp.where(wanted, 1.0, 0.0).astype(BF16)
    for block in range(2):
        rows = slice(block * 256, block * 256 + 256)
        q = q_ref[rows]
        da = da_ref[rows]
        left = jnp.concatenate([by_head(q, low), eq_ref[0, block * 512 : block * 512 + 512]], 1)
        product = (da.astype(F32) * att_ref[rows].astype(F32)).astype(BF16)
        sums = dot(product, summing)
        sums = jnp.concatenate([sums[:, :PAIR], sums[:, PAIR:]], 0)
        high = sums.astype(BF16).astype(F32)
        offsets = jnp.where(lanes == 2, high - sums, -sums).astype(BF16)
        left_d = jnp.concatenate([by_head(da, low), offsets], 1)
        q_t = q.T
        da_t = da.T
        dq = None
        for tile in range(3):
            place = block + tile
            keys = slice(place * 256, (place + 1) * 256)
            weights = jnp.exp2(dot_t(left, kx[keys]))
            if tile == 0:
                weights = jnp.where(first, weights, 0.0)
            if tile == 2:
                weights = jnp.where(last, weights, 0.0)
            slope = (weights * dot_t(left_d, vx[keys])).astype(BF16)
            weights = weights.astype(BF16)
            term = dot(slope, kx[keys, :PAIR])
            dq = term if dq is None else dq + term
            dk_term = jnp.concatenate(
                [dot(q_t[:HEAD_DIM], slope[:256]), dot(q_t[HEAD_DIM:], slope[256:])], 0
            )
            dv_term = jnp.concatenate(
                [dot(da_t[:HEAD_DIM], weights[:256]), dot(da_t[HEAD_DIM:], weights[256:])], 0
            )
            if block == 1 and tile < 2:
                dkt[:, keys] += dk_term
                dvt[:, keys] += dv_term
            else:
                dkt[:, keys] = dk_term
                dvt[:, keys] = dv_term
        dq = dq * HEAD_DIM**-0.5
        dq_ref[rows] = jnp.where(low, dq[:256], dq[256:]).astype(BF16)
    dk = (dkt[...] * (1.0 / LOG2E)).T.astype(BF16)
    dv = dvt[...].T.astype(BF16)
    dk_ref[...] = dk[256:768]
    dv_ref[...] = dv[256:768]
    dkh_ref[:256] = dk[:256]
    dkh_ref[256:] = dk[768:]
    dvh_ref[:256] = dv[:256]
    dvh_ref[256:] = dv[768:]


def attention_backward(live, q, k, kh, v, vh, eq, att, da):
    part = pl.BlockSpec((ROWS, PAIR), lambda h, _: (0, h))
    shape = jax.ShapeDtypeStruct((ROWS, WIDTH), BF16)
    return pl.pallas_call(
        backward_kernel,
        grid_spec=pltpu.PrefetchScalarGridSpec(
            num_scalar_prefetch=1,
            grid=(PAIRS,),
            in_specs=[part] * 5 + [pl.BlockSpec((1, EXT, PAIR), lambda h, _: (h, 0, 0)), part, part],
            out_specs=[part] * 5,
            scratch_shapes=[
                pltpu.VMEM((EXT, 2 * PAIR), BF16),
                pltpu.VMEM((EXT, 2 * PAIR), BF16),
                pltpu.VMEM((PAIR, EXT), F32),
                pltpu.VMEM((PAIR, EXT), F32),
            ],
        ),
        out_shape=[shape] * 5,
        compiler_params=params(),
        name="attention_backward",
    )(live, q, k, kh, v, vh, eq, att, da)


def decode_kernel(x_ref, att_ref, wo_ref, gain_ref, wd_ref, z_ref, r_ref, field_ref):
    level = x_ref[...].astype(F32) + dot(att_ref[...], wo_ref[...])
    scale = lax.rsqrt(jnp.mean(level * level, -1, keepdims=True) + 1e-05)
    z = level * scale
    z_ref[...] = z.astype(BF16)
    r_ref[...] = jnp.broadcast_to(scale, r_ref.shape)
    decoded = (z * gain_ref[...]).astype(BF16)
    field_ref[...] = dot_t(wd_ref[...], decoded).astype(BF16)


def decode(x, att, wo, gain, wd):
    variables = wd.shape[0]
    rows = pl.BlockSpec((256, WIDTH), lambda b: (b, 0))
    return pl.pallas_call(
        decode_kernel,
        grid=(2,),
        in_specs=[
            rows,
            rows,
            pl.BlockSpec((WIDTH, WIDTH), lambda b: (0, 0)),
            pl.BlockSpec((1, WIDTH), lambda b: (0, 0)),
            pl.BlockSpec((variables, WIDTH), lambda b: (0, 0)),
        ],
        out_specs=[
            rows,
            pl.BlockSpec((256, PAIR), lambda b: (b, 0)),
            pl.BlockSpec((variables, 256), lambda b: (0, b)),
        ],
        out_shape=[
            jax.ShapeDtypeStruct((ROWS, WIDTH), BF16),
            jax.ShapeDtypeStruct((ROWS, PAIR), F32),
            jax.ShapeDtypeStruct((variables, ROWS), BF16),
        ],
        compiler_params=params(),
        name="decode",
    )(x, att, wo, gain, wd)


def kernel_slope(diff):
    return diff * lax.rsqrt(diff * diff + 0.01)


def score_kernel(
    live_ref, own_ref, all_ref, target_ref, z_ref, r_ref, gain_ref, wd_ref, wo_ref, att_ref,
    lg_ref, da_ref, term_ref, total,
):
    step = pl.program_id(0)
    own = own_ref[...].astype(F32)
    members = all_ref.shape[0]
    pair_sum = None
    for member in range(members):
        slope = kernel_slope(own - all_ref[member].astype(F32))
        pair_sum = slope if pair_sum is None else pair_sum + slope
    slots = lane((own.shape[0], CYCLE_MAX))
    live = jnp.concatenate(
        [jnp.where(slots < live_ref[2 + 2 * step + c], 1.0, 0.0) for c in range(2)], 1
    )
    grad = (kernel_slope(own - target_ref[...]) - pair_sum * (1.0 / (members - 1))) * live
    back = lax.dot_general(
        grad.astype(BF16), wd_ref[...], (((0,), (0,)), ((), ())), preferred_element_type=F32
    )
    back = back.astype(BF16).astype(F32) * gain_ref[...]
    z = z_ref[...].astype(F32)
    level_grad = r_ref[:, :1] * (back - z * jnp.mean(back * z, -1, keepdims=True))
    lg = level_grad.astype(BF16)
    lg_ref[...] = lg
    da_ref[...] = dot_t(lg, wo_ref[...]).astype(BF16)
    term = lax.dot_general(att_ref[...], lg, (((0,), (0,)), ((), ())), preferred_element_type=F32)

    @pl.when(step == 0)
    def _():
        total[...] = term

    @pl.when(step == 1)
    def _():
        term_ref[...] = (total[...] + term).astype(BF16)


def score(live, own, everyone, target, z, r, gain, wd, wo, att):
    variables = wd.shape[0]
    members = everyone.shape[0]
    rows = pl.BlockSpec((256, WIDTH), lambda b, _: (b, 0))
    whole = pl.BlockSpec((WIDTH, WIDTH), lambda b, _: (0, 0))
    return pl.pallas_call(
        score_kernel,
        grid_spec=pltpu.PrefetchScalarGridSpec(
            num_scalar_prefetch=1,
            grid=(2,),
            in_specs=[
                pl.BlockSpec((variables, 256), lambda b, _: (0, b)),
                pl.BlockSpec((members, variables, 256), lambda b, _: (0, 0, b)),
                pl.BlockSpec((variables, 256), lambda b, _: (0, b)),
                rows,
                pl.BlockSpec((256, PAIR), lambda b, _: (b, 0)),
                pl.BlockSpec((1, WIDTH), lambda b, _: (0, 0)),
                pl.BlockSpec((variables, WIDTH), lambda b, _: (0, 0)),
                whole,
                rows,
            ],
            out_specs=[rows, rows, whole],
            scratch_shapes=[pltpu.VMEM((WIDTH, WIDTH), F32)],
        ),
        out_shape=[
            jax.ShapeDtypeStruct((ROWS, WIDTH), BF16),
            jax.ShapeDtypeStruct((ROWS, WIDTH), BF16),
            jax.ShapeDtypeStruct((WIDTH, WIDTH), BF16),
        ],
        compiler_params=params(),
        name="score",
    )(live, own, everyone, target, z, r, gain, wd, wo, att)


def final_kernel(
    x_ref, gain_ref, q_ref, k_ref, rq_ref, rk_ref, dq_ref, dk_ref, dv_ref,
    kb_ref, ka_ref, vb_ref, va_ref, wq_ref, wk_ref, wv_ref, lg_ref, out_ref, total,
):
    step = pl.program_id(0)
    means = head_mean_matrix(256)

    def norm_back(y, scale, grad):
        mean = dot((y * grad).astype(BF16), means)
        return (scale.astype(F32) * (grad - y * mean)).astype(BF16)

    def gathered(own_ref, before_ref, after_ref):
        own = own_ref[...].astype(F32)
        halo = jnp.concatenate([before_ref[...], after_ref[...]], 0)
        return own + halo.astype(F32)

    q_in = norm_back(q_ref[...].astype(F32) * (1.0 / Q_SCALE), rq_ref[...], dq_ref[...].astype(F32))
    k_in = norm_back(k_ref[...].astype(F32), rk_ref[...], gathered(dk_ref, kb_ref, ka_ref))
    v_in = gathered(dv_ref, vb_ref, va_ref).astype(BF16)
    term = dot_t(q_in, wq_ref[...]) + dot_t(k_in, wk_ref[...]) + dot_t(v_in, wv_ref[...])

    @pl.when(step == 0)
    def _():
        total[...] = term

    @pl.when(step > 0)
    def _():
        total[...] += term

    @pl.when(step == 3)
    def _():
        for block in range(4):
            rows = slice(block * 128, block * 128 + 128)
            x = x_ref[rows].astype(F32)
            scale = lax.rsqrt(jnp.mean(x * x, -1, keepdims=True) + 1e-05)
            grad = total[rows] * gain_ref[...]
            y = x * scale
            back = scale * (grad - y * jnp.mean(grad * y, -1, keepdims=True))
            out_ref[rows] = lg_ref[rows].astype(F32) + back


def finish(x, gain, q, k, rq, rk, dq, dk, dv, kb, ka, vb, va, wq, wk, wv, lg):
    whole = pl.BlockSpec((ROWS, WIDTH), lambda c: (0, 0))
    gains = pl.BlockSpec((1, WIDTH), lambda c: (0, 0))
    weight = pl.BlockSpec((WIDTH, 256), lambda c: (0, c))
    part = pl.BlockSpec((ROWS, 256), lambda c: (0, c))
    half = pl.BlockSpec((256, 256), lambda c: (0, c))
    return pl.pallas_call(
        final_kernel,
        grid=(4,),
        in_specs=[whole, gains] + [part] * 7 + [half] * 4 + [weight] * 3 + [whole],
        out_specs=whole,
        out_shape=jax.ShapeDtypeStruct((ROWS, WIDTH), F32),
        scratch_shapes=[pltpu.VMEM((ROWS, WIDTH), F32)],
        compiler_params=params(),
        name="finish",
    )(x, gain, q, k, rq, rk, dq, dk, dv, kb, ka, vb, va, wq, wk, wv, lg)


def body(
    latent_grids, cycle_points, norm_gain, w_query, w_key, w_value, w_out, dec_gain, w_dec, target
):
    x = latent_grids[0]
    band = lax.axis_index("grid")
    bands = lax.axis_size("grid")
    up = [(i, i + 1) for i in range(bands - 1)]
    down = [(j, i) for i, j in up]
    norm_gain = norm_gain[None]
    dec_gain = dec_gain[None]
    live = lax.dynamic_slice(jnp.pad(cycle_points, (2, 2)), (band * 4,), (8,))

    before = lax.ppermute(x[256:], "grid", up)
    after = lax.ppermute(x[:256], "grid", down)
    q, k, v, rq, rk = project(x, norm_gain, w_query, w_key, w_value)
    kh, vh = project_halo(before, after, norm_gain, w_key, w_value)
    att, eq = attention_forward(live, q, k, kh, v, vh)
    z, r, field = decode(x, att, w_out, dec_gain, w_dec)
    members = lax.axis_size("member")
    everyone = lax.all_to_all(
        jnp.broadcast_to(field[None], (members, *field.shape)), "member", 0, 0, tiled=True
    )
    lg, da, term = score(live, field, everyone, target, z, r, dec_gain, w_dec, w_out, att)
    dq, dk, dv, dkh, dvh = attention_backward(live, q, k, kh, v, vh, eq, att, da)
    kb = lax.ppermute(dkh[256:], "grid", up)
    ka = lax.ppermute(dkh[:256], "grid", down)
    vb = lax.ppermute(dvh[256:], "grid", up)
    va = lax.ppermute(dvh[:256], "grid", down)
    sens = finish(
        x, norm_gain, q, k, rq, rk, dq, dk, dv, kb, ka, vb, va, w_query, w_key, w_value, lg
    )
    blocks = term.reshape(bands, 64, members, 128).transpose(0, 2, 1, 3)
    blocks = blocks.reshape(bands * members, 64, 128)
    pieces = lax.all_to_all(blocks, ("grid", "member"), 0, 0, tiled=True)
    out = jnp.sum(pieces.astype(F32), 0)
    return (field[None], sens[None], out)


def solution(mesh):
    placed = (P("member", "grid", None), P(), P(), P(), P(), P(), P(), P(), P(), P(None, "grid"))
    return jax.shard_map(
        body,
        mesh=mesh,
        in_specs=placed,
        out_specs=(P("member", None, "grid"), P("member", "grid", None), P("grid", "member")),
        check_vma=False,
    )
```

time: 439 us -> 157 us (0.36)
  matrix products: 168 us -> 0 us
  waiting for transfers between devices: 112 us -> 10.7 us
  Pallas kernels: 0 us -> 84.1 us
  other arithmetic: 52.6 us -> 0.97 us
  local copies, waits for them, and re-layouts: 36.7 us -> 10.8 us
  blocking collectives: 36.1 us -> 18.1 us
  starting transfers between devices: 16 us -> 30.5 us
  between operations: 14.7 us -> 0.79 us
    dot_general x39 -> x0, matrix products: 168 us -> none  [the longest x16 91.9 us: head_block(): jnp.einsum('rhd,ehd->hre', q_blk, k_blk, preferred_element_type=jnp.float32)]
    pallas_call x0 -> x7, Pallas kernels: none -> 84.1 us  [the longest x1 25.7 us: attention_backward(): pl.pallas_call(backward_kernel, grid_spec=pltpu.PrefetchScalarGridSpec(nu...]
    unnamed x3 -> x0, waiting for transfers between devices: 64.9 us -> none
    reduce_scatter x1 -> x0, waiting for transfers between devices: 37.6 us -> none  [body(): lax.psum_scatter(out_term.astype(jnp.bfloat16), 'grid', scatter_dimension...]
    all_gather x1 -> x0, blocking collectives: 36.1 us -> none  [body(): lax.all_gather(field_bf[None], 'member', axis=0, tiled=True)]
    all_to_all x0 -> x1, blocking collectives: none -> 18.1 us  [body(): lax.all_to_all(jnp.broadcast_to(field[None], (members, *field.shape)), 'm...]
    dynamic_update_slice x8 -> x0, other arithmetic: 13.6 us -> none  [attend(): blocks = lax.map(head_block, (queries, key_part, value_part))]
    unnamed x94 -> x17, local copies, waits for them, and re-layouts: 18.2 us -> 4.65 us
  transfers between devices with their start and end apart: 6 -> 7, of which waited for: 6 -> 3; matrix products, arithmetic and copies ran while one was open for 6% -> 1% of each run, Pallas kernels for 0% -> 31%
where the time goes in v1:
time: 157 us; the launch traced here: 156 us
  Pallas kernels  84.1 us (54%)
  starting transfers between devices  30.5 us (19%)
  blocking collectives  18.1 us (12%)
  local copies, waits for them, and re-layouts  10.8 us (7%)
  waiting for transfers between devices  10.7 us (7%)
    pallas_call x1, Pallas kernels, attention_backward(): pl.pallas_call(backward_kernel, grid_spec=pltpu.PrefetchScalarGridSpec(nu...  25.7 us
    all_to_all x1, blocking collectives, body(): lax.all_to_all(jnp.broadcast_to(field[None], (members, *field.shape)), 'm...  18.1 us
    pallas_call x1, Pallas kernels, attention_forward(): pl.pallas_call(forward_kernel, grid_spec=pltpu.PrefetchScalarGridSpec(num...  13.7 us
    pallas_call x1, Pallas kernels, finish(): pl.pallas_call(final_kernel, grid=(4,), in_specs=[whole, gains] + [part]...  11.7 us
    pallas_call x1, Pallas kernels, project(): pl.pallas_call(qkv_kernel, grid=(4,), in_specs=[whole, gains, weight, wei...  10.3 us
    pallas_call x1, Pallas kernels, score(): pl.pallas_call(score_kernel, grid_spec=pltpu.PrefetchScalarGridSpec(num_s...  9.41 us
    pallas_call x1, Pallas kernels, project_halo(): pl.pallas_call(kv_kernel, grid=(4,), in_specs=[part, part, gains, weight,...  8.19 us
    all_to_all x1, starting transfers between devices, body(): pieces = lax.all_to_all(blocks, ('grid', 'member'), 0, 0, tiled=True)  8.04 us
  transfers between devices with their start and end apart: 7, of which 3 were waited for; matrix products, arithmetic and copies ran while one was open for 1% of the time, Pallas kernels for 31%

profile of v1, /device:TPU:24, one launch (start us, length us, event | category | flops | bytes accessed | tf_op | source)
XLA Modules:
  0.0 155.9 jit_solution(12799804063415425698)
XLA Ops:
  0.6 1.3 slice_bitcast_fusion
  1.9 5.6 %collective-permute-start.1 = (bf16[256,1024]{1,0:T(8,128)(2,1)S(1)}, bf16[256,1024]{1,0:T(8,128)(2,1)S(1)}, u32[]{:S(2)}, u32[]{:S(2)}) collective-permute-start(bf16[256,1024]{1,0:T(8,128)(2,1)S(1)} %get-tuple-element.47), channel_id=1, source_target_pairs={{1,0},{2,1},{3,2},{4,3},{5,4},{6,5},{7,6},{8,7},{9,8},{10,9},{11,1... | collective-permute-start | bytes 1572872 | tf_op jit(solution)/shard_map/ppermute | solution.py:482
  7.5 1.9 %collective-permute-start = (bf16[256,1024]{1,0:T(8,128)(2,1)S(1)}, bf16[256,1024]{1,0:T(8,128)(2,1)S(1)}, u32[]{:S(2)}, u32[]{:S(2)}) collective-permute-start(bf16[256,1024]{1,0:T(8,128)(2,1)S(1)} %get-tuple-element.48), channel_id=1, source_target_pairs={{0,1},{1,2},{2,3},{3,4},{4,5},{5,6},{6,7},{7,8},{8,9},{9,10},{10,1... | collective-permute-start | bytes 1572872 | tf_op jit(solution)/shard_map/ppermute | solution.py:481
  9.4 10.3 %project_own.1 = (bf16[512,1024]{1,0:T(8,128)(2,1)}, bf16[512,1024]{1,0:T(8,128)(2,1)}, bf16[512,1024]{1,0:T(8,128)(2,1)}, bf16[512,1024]{1,0:T(8,128)(2,1)}, bf16[512,1024]{1,0:T(8,128)(2,1)}) custom-call(bf16[512,1024]{1,0:T(8,128)(2,1)} %bitcast.15, f32[1,1024]{1,0:T(1,128)} %bitcast.23, bf16[1024,1024]{1,0:T(8,128)(2,1)} %wq_ref.3, ...), custom_call_target="tpu_custom_call" | custom-call | tf_op jit(solution)/shard_map/project_own/pallas_call | solution.py:93
  21.9 8.2 %project_halo.1 = (bf16[512,1024]{1,0:T(8,128)(2,1)}, bf16[512,1024]{1,0:T(8,128)(2,1)}) custom-call(bf16[256,1024]{1,0:T(8,128)(2,1)} %copy-done.4, bf16[256,1024]{1,0:T(8,128)(2,1)} %copy-done.3, f32[1,1024]{1,0:T(1,128)} %bitcast.24, bf16[1024,1024]{1,0:T(8,128)(2,1)} %wk_ref.5, bf16[1024,1024]{1,0:T(8,128)(2,1)} %wv_ref.5), custom_call_target="tpu_custom_call" | custom-call | tf_op jit(solution)/shard_map/project_halo/pallas_call | solution.py:111
  30.1 13.7 %attention_forward.1 = (bf16[512,1024]{1,0:T(8,128)(2,1)}, bf16[8,1024,128]{2,1,0:T(8,128)(2,1)}) custom-call(s32[8]{0:T(128)} %pad_dynamic-slice_fusion.live_ref, bf16[512,1024]{1,0:T(8,128)(2,1)} %get-tuple-element.23.q_ref, bf16[512,1024]{1,0:T(8,128)(2,1)} %get-tuple-element.24.k_ref, bf16[512,1024]{1,0:T(8,128)(2,1)} %get-tuple-element.25.kh_ref, ...), custom_call_target="tpu_custom_call" | custom-call | tf_op jit(solution)/shard_map/attention_forward/pallas_call | solution.py:188
  43.9 5.1 %decode.1 = (bf16[512,1024]{1,0:T(8,128)(2,1)}, f32[512,128]{1,0:T(8,128)}, bf16[100,512]{1,0:T(8,128)(2,1)}) custom-call(bf16[512,1024]{1,0:T(8,128)(2,1)} %bitcast.16, bf16[512,1024]{1,0:T(8,128)(2,1)} %get-tuple-element.28.att_ref, bf16[1024,1024]{1,0:T(8,128)(2,1)} %wo_ref.3, f32[1,1024]{1,0:T(1,128)} %bitcast.26, bf16[100,1024]{1,0:T(8,128)(2,1)} %wd_ref.3), custom_call_target="tpu_custom_call" | custom-call | tf_op jit(solution)/shard_map/decode/pallas_call | solution.py:311
  49.0 1.0 broadcast_in_dim.21
  49.9 18.1 %all_to_all.10.all_ref = bf16[8,100,512]{2,1,0:T(8,128)(2,1)} all-to-all(bf16[8,100,512]{2,1,0:T(8,128)(2,1)S(1)} %broadcast_in_dim.21), channel_id=1, replica_groups=mesh['member'=8,'grid'=16] {'member'}, dimensions={0} | all-to-all | bytes 1638400 | tf_op jit(solution)/shard_map/all_to_all | solution.py:488
  68.0 9.4 %score.1 = (bf16[512,1024]{1,0:T(8,128)(2,1)}, bf16[512,1024]{1,0:T(8,128)(2,1)}, bf16[1024,1024]{1,0:T(8,128)(2,1)}) custom-call(s32[8]{0:T(128)} %pad_dynamic-slice_fusion.live_ref, bf16[100,512]{1,0:T(8,128)(2,1)} %get-tuple-element.29.own_ref, bf16[8,100,512]{2,1,0:T(8,128)(2,1)} %all_to_all.10.all_ref, f32[100,512]{1,0:T(8,128)} %target_ref.1, ...), custom_call_target="tpu_custom_call" | custom-call | tf_op jit(solution)/shard_map/score/pallas_call | solution.py:381
  77.5 2.2 %copy.14 = bf16[128,8,8,128]{3,2,1,0:T(8,128)(2,1)S(1)} copy(bf16[128,8,8,128]{3,1,2,0:T(8,128)(2,1)} %bitcast.20) | data formatting | bytes 4194304
  79.7 1.9 %copy.13 = bf16[16,64,8,128]{3,1,2,0:T(8,128)(2,1)} copy(bf16[16,64,8,128]{3,2,1,0:T(8,128)(2,1)S(1)} %bitcast.19) | data formatting | bytes 4194304 | tf_op jit(solution)/shard_map/reshape | solution.py:500
  81.6 8.0 %all-to-all-start.1 = ((bf16[128,64,128]{2,1,0:T(8,128)(2,1)}), bf16[128,64,128]{2,1,0:T(8,128)(2,1)S(1)}, u32[]{:S(2)}, u32[]{:S(2)}) async-start(bf16[128,64,128]{2,1,0:T(8,128)(2,1)} %bitcast.18), calls=%async_computation.1 | async-start | bytes 4194304 | tf_op jit(solution)/shard_map/all_to_all | solution.py:502
  89.7 25.7 %attention_backward.1 = (bf16[512,1024]{1,0:T(8,128)(2,1)}, bf16[512,1024]{1,0:T(8,128)(2,1)}, bf16[512,1024]{1,0:T(8,128)(2,1)}, bf16[512,1024]{1,0:T(8,128)(2,1)}, bf16[512,1024]{1,0:T(8,128)(2,1)}) custom-call(s32[8]{0:T(128)} %pad_dynamic-slice_fusion.live_ref, bf16[512,1024]{1,0:T(8,128)(2,1)} %get-tuple-element.23.q_ref, ...), custom_call_target="tpu_custom_call" | custom-call | tf_op jit(solution)/shard_map/attention_backward/pallas_call | solution.py:278
  115.3 1.4 fusion.1
  116.7 5.4 %collective-permute-start.3 = (bf16[256,1024]{1,0:T(8,128)(2,1)S(1)}, bf16[256,1024]{1,0:T(8,128)(2,1)S(1)}, u32[]{:S(2)}, u32[]{:S(2)}) collective-permute-start(bf16[256,1024]{1,0:T(8,128)(2,1)S(1)} %get-tuple-element.45), channel_id=1, source_target_pairs={{1,0},{2,1},{3,2},{4,3},{5,4},{6,5},{7,6},{8,7},{9,8},{10,9},{11,1... | collective-permute-start | bytes 1572872 | tf_op jit(solution)/shard_map/ppermute | solution.py:494
  122.0 1.9 %collective-permute-start.2 = (bf16[256,1024]{1,0:T(8,128)(2,1)S(1)}, bf16[256,1024]{1,0:T(8,128)(2,1)S(1)}, u32[]{:S(2)}, u32[]{:S(2)}) collective-permute-start(bf16[256,1024]{1,0:T(8,128)(2,1)S(1)} %get-tuple-element.46), channel_id=1, source_target_pairs={{0,1},{1,2},{2,3},{3,4},{4,5},{5,6},{6,7},{7,8},{8,9},{9,10},{10,1... | collective-permute-start | bytes 1572872 | tf_op jit(solution)/shard_map/ppermute | solution.py:493
  124.1 5.8 %collective-permute-start.5 = (bf16[256,1024]{1,0:T(8,128)(2,1)S(1)}, bf16[256,1024]{1,0:T(8,128)(2,1)S(1)}, u32[]{:S(2)}, u32[]{:S(2)}) collective-permute-start(bf16[256,1024]{1,0:T(8,128)(2,1)S(1)} %get-tuple-element.43), channel_id=1, source_target_pairs={{1,0},{2,1},{3,2},{4,3},{5,4},{6,5},{7,6},{8,7},{9,8},{10,9},{11,1... | collective-permute-start | bytes 1572872 | tf_op jit(solution)/shard_map/ppermute | solution.py:496
  129.8 1.9 %collective-permute-start.4 = (bf16[256,1024]{1,0:T(8,128)(2,1)S(1)}, bf16[256,1024]{1,0:T(8,128)(2,1)S(1)}, u32[]{:S(2)}, u32[]{:S(2)}) collective-permute-start(bf16[256,1024]{1,0:T(8,128)(2,1)S(1)} %get-tuple-element.44), channel_id=1, source_target_pairs={{0,1},{1,2},{2,3},{3,4},{4,5},{5,6},{6,7},{7,8},{8,9},{9,10},{10,1... | collective-permute-start | bytes 1572872 | tf_op jit(solution)/shard_map/ppermute | solution.py:495
  131.8 2.9 %collective-permute-done.2.kb_ref = bf16[256,1024]{1,0:T(8,128)(2,1)S(1)} collective-permute-done((bf16[256,1024]{1,0:T(8,128)(2,1)S(1)}, bf16[256,1024]{1,0:T(8,128)(2,1)S(1)}, u32[]{:S(2)}, u32[]{:S(2)}) %collective-permute-start.2) | collective-permute-done | bytes 524320 | tf_op jit(solution)/shard_map/ppermute | solution.py:493
  134.7 1.8 %collective-permute-done.5.va_ref = bf16[256,1024]{1,0:T(8,128)(2,1)S(1)} collective-permute-done((bf16[256,1024]{1,0:T(8,128)(2,1)S(1)}, bf16[256,1024]{1,0:T(8,128)(2,1)S(1)}, u32[]{:S(2)}, u32[]{:S(2)}) %collective-permute-start.5) | collective-permute-done | bytes 524320 | tf_op jit(solution)/shard_map/ppermute | solution.py:496
  136.5 5.9 %collective-permute-done.4.vb_ref = bf16[256,1024]{1,0:T(8,128)(2,1)S(1)} collective-permute-done((bf16[256,1024]{1,0:T(8,128)(2,1)S(1)}, bf16[256,1024]{1,0:T(8,128)(2,1)S(1)}, u32[]{:S(2)}, u32[]{:S(2)}) %collective-permute-start.4) | collective-permute-done | bytes 524320 | tf_op jit(solution)/shard_map/ppermute | solution.py:495
  143.3 11.7 %finish.1 = f32[512,1024]{1,0:T(8,128)} custom-call(bf16[512,1024]{1,0:T(8,128)(2,1)} %bitcast.17, f32[1,1024]{1,0:T(1,128)} %bitcast.25, bf16[512,1024]{1,0:T(8,128)(2,1)} %get-tuple-element.23.q_ref, bf16[512,1024]{1,0:T(8,128)(2,1)} %get-tuple-element.24.k_ref, bf16[512,1024]{1,0:T(8,128)(2,1)} %get-tuple-element.30.rq_ref, ...), custom_call_target="tpu_custom_call" | custom-call | tf_op jit(solution)/shard_map/finish/pallas_call | solution.py:457
  155.0 1.0 convert_reduce_fusion
  (22 shorter events, 3.1 us)
Async XLA Ops:
  1.9 18.5 %collective-permute-start.1 = (bf16[256,1024]{1,0:T(8,128)(2,1)S(1)}, bf16[256,1024]{1,0:T(8,128)(2,1)S(1)}, u32[]{:S(2)}, u32[]{:S(2)}) collective-permute-start(bf16[256,1024]{1,0:T(8,128)(2,1)S(1)} %get-tuple-element.47), channel_id=1, source_target_pairs={{1,0},{2,1},{3,2},{4,3},{5,4},{6,5},{7,6},{8,7},{9,8},{10,9},{11,1... | collective-permute-start | bytes 1572872 | tf_op jit(solution)/shard_map/ppermute | solution.py:482
  7.5 12.9 %collective-permute-start = (bf16[256,1024]{1,0:T(8,128)(2,1)S(1)}, bf16[256,1024]{1,0:T(8,128)(2,1)S(1)}, u32[]{:S(2)}, u32[]{:S(2)}) collective-permute-start(bf16[256,1024]{1,0:T(8,128)(2,1)S(1)} %get-tuple-element.48), channel_id=1, source_target_pairs={{0,1},{1,2},{2,3},{3,4},{4,5},{5,6},{6,7},{7,8},{8,9},{9,10},{10,1... | collective-permute-start | bytes 1572872 | tf_op jit(solution)/shard_map/ppermute | solution.py:481
  9.4 10.4 %copy-start.7 = (s32[64]{0:T(128)S(1)}, s32[64]{0:T(128)}, u32[]{:S(2)}) copy-start(s32[64]{0:T(128)} %param.11) | copy-start | bytes 772
  20.4 0.8 copy-start.3
  21.2 0.8 copy-start.4
  81.6 73.4 %all-to-all-start.1 = ((bf16[128,64,128]{2,1,0:T(8,128)(2,1)}), bf16[128,64,128]{2,1,0:T(8,128)(2,1)S(1)}, u32[]{:S(2)}, u32[]{:S(2)}) async-start(bf16[128,64,128]{2,1,0:T(8,128)(2,1)} %bitcast.18), calls=%async_computation.1 | async-start | bytes 4194304 | tf_op jit(solution)/shard_map/all_to_all | solution.py:502
  115.3 8.7 %copy-start = (bf16[512,1024]{1,0:T(8,128)(2,1)S(1)}, bf16[512,1024]{1,0:T(8,128)(2,1)}, u32[]{:S(2)}) copy-start(bf16[512,1024]{1,0:T(8,128)(2,1)} %get-tuple-element.40) | copy-start | bytes 3145732
  116.7 15.1 %collective-permute-start.3 = (bf16[256,1024]{1,0:T(8,128)(2,1)S(1)}, bf16[256,1024]{1,0:T(8,128)(2,1)S(1)}, u32[]{:S(2)}, u32[]{:S(2)}) collective-permute-start(bf16[256,1024]{1,0:T(8,128)(2,1)S(1)} %get-tuple-element.45), channel_id=1, source_target_pairs={{1,0},{2,1},{3,2},{4,3},{5,4},{6,5},{7,6},{8,7},{9,8},{10,9},{11,1... | collective-permute-start | bytes 1572872 | tf_op jit(solution)/shard_map/ppermute | solution.py:494
  122.0 12.6 %collective-permute-start.2 = (bf16[256,1024]{1,0:T(8,128)(2,1)S(1)}, bf16[256,1024]{1,0:T(8,128)(2,1)S(1)}, u32[]{:S(2)}, u32[]{:S(2)}) collective-permute-start(bf16[256,1024]{1,0:T(8,128)(2,1)S(1)} %get-tuple-element.46), channel_id=1, source_target_pairs={{0,1},{1,2},{2,3},{3,4},{4,5},{5,6},{6,7},{7,8},{8,9},{9,10},{10,1... | collective-permute-start | bytes 1572872 | tf_op jit(solution)/shard_map/ppermute | solution.py:493
  124.1 12.4 %collective-permute-start.5 = (bf16[256,1024]{1,0:T(8,128)(2,1)S(1)}, bf16[256,1024]{1,0:T(8,128)(2,1)S(1)}, u32[]{:S(2)}, u32[]{:S(2)}) collective-permute-start(bf16[256,1024]{1,0:T(8,128)(2,1)S(1)} %get-tuple-element.43), channel_id=1, source_target_pairs={{1,0},{2,1},{3,2},{4,3},{5,4},{6,5},{7,6},{8,7},{9,8},{10,9},{11,1... | collective-permute-start | bytes 1572872 | tf_op jit(solution)/shard_map/ppermute | solution.py:496
  129.8 12.6 %collective-permute-start.4 = (bf16[256,1024]{1,0:T(8,128)(2,1)S(1)}, bf16[256,1024]{1,0:T(8,128)(2,1)S(1)}, u32[]{:S(2)}, u32[]{:S(2)}) collective-permute-start(bf16[256,1024]{1,0:T(8,128)(2,1)S(1)} %get-tuple-element.44), channel_id=1, source_target_pairs={{0,1},{1,2},{2,3},{3,4},{4,5},{5,6},{6,7},{7,8},{8,9},{9,10},{10,1... | collective-permute-start | bytes 1572872 | tf_op jit(solution)/shard_map/ppermute | solution.py:495
  131.8 10.7 %copy-start.1 = (bf16[256,1024]{1,0:T(8,128)(2,1)}, bf16[256,1024]{1,0:T(8,128)(2,1)S(1)}, u32[]{:S(2)}) copy-start(bf16[256,1024]{1,0:T(8,128)(2,1)S(1)} %collective-permute-done.3.ka_ref) | copy-start | bytes 1572868
  134.7 7.8 %copy-start.2 = (bf16[256,1024]{1,0:T(8,128)(2,1)}, bf16[256,1024]{1,0:T(8,128)(2,1)S(1)}, u32[]{:S(2)}) copy-start(bf16[256,1024]{1,0:T(8,128)(2,1)S(1)} %collective-permute-done.2.kb_ref) | copy-start | bytes 1572868
  136.5 5.9 %copy-start.5 = (bf16[256,1024]{1,0:T(8,128)(2,1)}, bf16[256,1024]{1,0:T(8,128)(2,1)S(1)}, u32[]{:S(2)}) copy-start(bf16[256,1024]{1,0:T(8,128)(2,1)S(1)} %collective-permute-done.5.va_ref) | copy-start | bytes 1572868
  142.4 0.9 copy-start.6

commit v2 on v0

v2 whole, which is shorter than its diff:
```python
import jax
import jax.numpy as jnp
from jax import lax
from jax.experimental import pallas as pl
from jax.experimental.pallas import tpu as pltpu
from jax.sharding import PartitionSpec as P

HEAD_DIM = 64
CYCLE_MAX = 128
WINDOW = 256
ROWS = 512
EXT = 1024
WIDTH = 1024
PAIR = 128
PAIRS = 8
LOG2E = 1.4426950408889634
Q_SCALE = LOG2E * HEAD_DIM**-0.5
DEAD = -30000.0
F32 = jnp.float32
BF16 = jnp.bfloat16


def params(mib):
    return pltpu.CompilerParams(vmem_limit_bytes=mib * 1024 * 1024)


def dot(left, right):
    return lax.dot_general(left, right, (((1,), (0,)), ((), ())), preferred_element_type=F32)


def dot_t(left, right):
    return lax.dot_general(left, right, (((1,), (1,)), ((), ())), preferred_element_type=F32)


def lane(shape):
    return lax.broadcasted_iota(jnp.int32, shape, len(shape) - 1)


def head_mean_matrix(width):
    rows = lax.broadcasted_iota(jnp.int32, (width, width), 0) // HEAD_DIM
    cols = lax.broadcasted_iota(jnp.int32, (width, width), 1) // HEAD_DIM
    return jnp.where(rows == cols, 1.0 / HEAD_DIM, 0.0).astype(BF16)


def normed_rows(x_ref, gain_ref):
    x = x_ref[...].astype(F32)
    scale = lax.rsqrt(jnp.mean(x * x, -1, keepdims=True) + 1e-05)
    return (x * scale * gain_ref[...]).astype(BF16)


HBM = pl.BlockSpec(memory_space=pl.ANY)
WHOLE = pl.BlockSpec(memory_space=pltpu.VMEM)


def start_all(sources, targets, semaphores):
    copies = [
        pltpu.make_async_copy(source, target, semaphores.at[place])
        for place, (source, target) in enumerate(zip(sources, targets))
    ]
    for copy in copies:
        copy.start()
    return copies


def wait_all(copies):
    for copy in copies:
        copy.wait()


def head_scales(raw, means, epsilon):
    return [
        lax.rsqrt(dot((part * part).astype(BF16), means) + epsilon)
        for part in (raw[:, c : c + 256] for c in range(0, WIDTH, 256))
    ]


def project_kernel(
    x_hbm, gain_ref, wq_hbm, wk_hbm, wv_hbm, q_hbm, k_hbm, v_hbm, rq_hbm, rk_hbm,
    x, wq, wk, wv, q, k, v, rq, rk, in_sems, out_sems,
):
    loads = start_all((x_hbm, wq_hbm, wk_hbm, wv_hbm), (x, wq, wk, wv), in_sems)
    buffers = (q, rq, k, rk, v)
    outs = (q_hbm, rq_hbm, k_hbm, rk_hbm, v_hbm)
    stores = [
        pltpu.make_async_copy(buffer, out, out_sems.at[place])
        for place, (buffer, out) in enumerate(zip(buffers, outs))
    ]
    means = head_mean_matrix(256)
    loads[0].wait()
    rows = normed_rows(x, gain_ref)
    for weight, out, scale_out, factor, place in ((wq, q, rq, Q_SCALE, 0), (wk, k, rk, 1.0, 1)):
        loads[place + 1].wait()
        raw = dot(rows, weight[...])
        for index, scale in enumerate(head_scales(raw, means, 1e-06)):
            columns = slice(index * 256, index * 256 + 256)
            out[:, columns] = (raw[:, columns] * scale * factor).astype(BF16)
            scale_out[:, columns] = scale.astype(BF16)
        stores[2 * place].start()
        stores[2 * place + 1].start()
    loads[3].wait()
    v[...] = dot(rows, wv[...]).astype(BF16)
    stores[4].start()
    wait_all(stores)


def project(x, gain, wq, wk, wv):
    shape = jax.ShapeDtypeStruct((ROWS, WIDTH), BF16)
    square = pltpu.VMEM((WIDTH, WIDTH), BF16)
    rows = pltpu.VMEM((ROWS, WIDTH), BF16)
    return pl.pallas_call(
        project_kernel,
        in_specs=[HBM, WHOLE, HBM, HBM, HBM],
        out_specs=[HBM] * 5,
        out_shape=[shape] * 5,
        scratch_shapes=[
            rows, square, square, square, rows, rows, rows, rows, rows,
            pltpu.SemaphoreType.DMA((4,)),
            pltpu.SemaphoreType.DMA((5,)),
        ],
        compiler_params=params(56),
        name="project_own",
    )(x, gain, wq, wk, wv)


def key_extras(live_ref):
    pieces = []
    lanes = lane((CYCLE_MAX, PAIR))
    slots = lax.broadcasted_iota(jnp.int32, (CYCLE_MAX, PAIR), 0)
    for cycle in range(EXT // CYCLE_MAX):
        bias = jnp.where(slots < live_ref[cycle], 0.0, DEAD)
        pieces.append(jnp.where(lanes == 0, bias, jnp.where(lanes < 3, 1.0, 0.0)).astype(BF16))
    return pieces


def by_head(value, low):
    zero = jnp.zeros_like(value)
    return jnp.concatenate([jnp.where(low, value, zero), jnp.where(low, zero, value)], 0)


def window_mask(shape, query_dim):
    queries = lax.broadcasted_iota(jnp.int32, shape, query_dim) & 255
    keys = lax.broadcasted_iota(jnp.int32, shape, 1 - query_dim)
    return (keys >= queries) & (keys <= queries + 2 * WINDOW)


def attend_pair(q, kx, vx, low, inside, one):
    lanes = lane((512, PAIR))
    spans = [slice(block * 256, block * 256 + 768) for block in range(2)]
    scores = []
    for block in range(2):
        left = jnp.concatenate([by_head(q[block * 256 : block * 256 + 256], low), one], 1)
        scores.append(dot_t(left, kx[spans[block]]))
    weights = [jnp.where(inside, jnp.exp2(score), 0.0).astype(BF16) for score in scores]
    rows, extras = [], []
    for block in range(2):
        total = dot(weights[block], vx[spans[block]])
        sums = total[:, PAIR:]
        out = total[:, :PAIR] / sums
        rows.append(jnp.where(low, out[:256], out[256:]).astype(BF16))
        shift = -jnp.log2(sums)
        high = shift.astype(BF16).astype(F32)
        extra = jnp.where(
            lanes == 0, 1.0, jnp.where(lanes == 1, high, jnp.where(lanes == 2, shift - high, 0.0))
        )
        extras.append(extra.astype(BF16))
    return rows, extras


def front_kernel(
    live_ref, before_hbm, after_hbm, wk_hbm, wv_hbm, q_hbm, k_hbm, v_hbm, x_hbm, wo_hbm,
    gain_ref, dec_gain_ref, wd_ref,
    kx_hbm, vx_hbm, att_hbm, eq_hbm, z_hbm, r_hbm, field_hbm, copies_hbm,
    halo, wk, wv, q, ke, ve, x, wo, att, eq, z, r, field, kx, vx, in_sems, out_sems,
):
    own = pl.ds(256, 512)
    loads = start_all(
        (before_hbm, after_hbm, wk_hbm, wv_hbm, q_hbm, k_hbm, v_hbm, wo_hbm, x_hbm),
        (halo.at[pl.ds(0, 256)], halo.at[pl.ds(256, 256)], wk, wv, q, ke.at[own], ve.at[own], wo, x),
        in_sems,
    )
    for cycle, piece in enumerate(key_extras(live_ref)):
        kx[cycle * CYCLE_MAX : (cycle + 1) * CYCLE_MAX, PAIR:] = piece
    vx[:, PAIR:] = jnp.ones((EXT, PAIR), BF16)
    means = head_mean_matrix(256)
    wait_all(loads[:3])
    rows = normed_rows(halo, gain_ref)
    raw = dot(rows, wk[...])
    for index, scale in enumerate(head_scales(raw, means, 1e-06)):
        columns = slice(index * 256, index * 256 + 256)
        part = (raw[:, columns] * scale).astype(BF16)
        ke[:256, columns] = part[:256]
        ke[768:, columns] = part[256:]
    loads[3].wait()
    part = dot(rows, wv[...]).astype(BF16)
    ve[:256] = part[:256]
    ve[768:] = part[256:]
    wait_all(loads[4:7])
    stores = start_all((ke, ve), (kx_hbm, vx_hbm), out_sems)
    low = lane((256, PAIR)) < HEAD_DIM
    one = jnp.where(lane((512, PAIR)) == 0, 1.0, 0.0).astype(BF16)
    inside = window_mask((512, 768), 0)

    def pair_step(pair, carry):
        columns = pl.ds(pl.multiple_of(pair * PAIR, PAIR), PAIR)
        kx[:, :PAIR] = ke[:, columns]
        vx[:, :PAIR] = ve[:, columns]
        rows, extras = attend_pair(q[:, columns], kx, vx, low, inside, one)
        for block in range(2):
            att[block * 256 : block * 256 + 256, columns] = rows[block]
            eq[pair, block * 512 : block * 512 + 512] = extras[block]
        return carry

    lax.fori_loop(0, PAIRS, pair_step, 0)
    stores += [
        pltpu.make_async_copy(source, target, out_sems.at[2 + place])
        for place, (source, target) in enumerate(
            ((att, att_hbm), (eq, eq_hbm), (z, z_hbm), (r, r_hbm), (field, field_hbm))
        )
    ]
    stores += [
        pltpu.make_async_copy(field, copies_hbm.at[member], out_sems.at[7 + member])
        for member in range(copies_hbm.shape[0])
    ]
    stores[2].start()
    stores[3].start()
    wait_all(loads[7:])
    level = x[...].astype(F32) + dot(att[...], wo[...])
    scale = lax.rsqrt(jnp.mean(level * level, -1, keepdims=True) + 1e-05)
    normal = level * scale
    decoded = (normal * dec_gain_ref[...]).astype(BF16)
    field[...] = dot_t(wd_ref[...], decoded).astype(BF16)
    for store in stores[6:]:
        store.start()
    z[...] = normal.astype(BF16)
    r[...] = jnp.broadcast_to(scale, r.shape)
    stores[4].start()
    stores[5].start()
    wait_all(stores)


def front(live, before, after, wk, wv, q, k, v, x, wo, gain, dec_gain, wd, members):
    variables = wd.shape[0]
    square = pltpu.VMEM((WIDTH, WIDTH), BF16)
    rows = pltpu.VMEM((ROWS, WIDTH), BF16)
    shape = jax.ShapeDtypeStruct((ROWS, WIDTH), BF16)
    ext = jax.ShapeDtypeStruct((EXT, WIDTH), BF16)
    return pl.pallas_call(
        front_kernel,
        in_specs=[pl.BlockSpec(memory_space=pltpu.SMEM)] + [HBM] * 9 + [WHOLE] * 3,
        out_specs=[HBM] * 8,
        out_shape=[
            ext,
            ext,
            shape,
            jax.ShapeDtypeStruct((PAIRS, EXT, PAIR), BF16),
            shape,
            jax.ShapeDtypeStruct((ROWS, PAIR), F32),
            jax.ShapeDtypeStruct((variables, ROWS), BF16),
            jax.ShapeDtypeStruct((members, variables, ROWS), BF16),
        ],
        scratch_shapes=[
            rows, square, square, rows,
            pltpu.VMEM((EXT, WIDTH), BF16),
            pltpu.VMEM((EXT, WIDTH), BF16),
            rows, square, rows,
            pltpu.VMEM((PAIRS, EXT, PAIR), BF16),
            rows,
            pltpu.VMEM((ROWS, PAIR), F32),
            pltpu.VMEM((variables, ROWS), BF16),
            pltpu.VMEM((EXT, 2 * PAIR), BF16),
            pltpu.VMEM((EXT, 2 * PAIR), BF16),
            pltpu.SemaphoreType.DMA((9,)),
            pltpu.SemaphoreType.DMA((7 + members,)),
        ],
        compiler_params=params(56),
        name="halo_attention_decode",
    )(live, before, after, wk, wv, q, k, v, x, wo, gain, dec_gain, wd)


def backward_kernel(
    live_ref, q_ref, ke_ref, ve_ref, eq_ref, att_ref, da_ref,
    dq_ref, dk_ref, dv_ref, low_ref, high_ref, kx, vx, dka, dva,
):
    @pl.when(pl.program_id(0) == 0)
    def _():
        for cycle, piece in enumerate(key_extras(live_ref)):
            kx[cycle * CYCLE_MAX : (cycle + 1) * CYCLE_MAX, PAIR:] = piece
            vx[cycle * CYCLE_MAX : (cycle + 1) * CYCLE_MAX, PAIR:] = piece

    kx[:, :PAIR] = ke_ref[...]
    vx[:, :PAIR] = ve_ref[...]
    low = lane((256, PAIR)) < HEAD_DIM
    lanes = lane((512, PAIR))
    inside = window_mask((768, 512), 1)
    feature = lax.broadcasted_iota(jnp.int32, (PAIR, 2 * PAIR), 0) // HEAD_DIM
    column = lane((PAIR, 2 * PAIR))
    wanted = (feature == column // PAIR) & ((column % PAIR == 1) | (column % PAIR == 2))
    summing = jnp.where(wanted, 1.0, 0.0).astype(BF16)
    for block in range(2):
        rows = slice(block * 256, block * 256 + 256)
        keys = slice(block * 256, block * 256 + 768)
        q = by_head(q_ref[rows], low)
        da = by_head(da_ref[rows], low)
        left = jnp.concatenate([q, eq_ref[0, block * 512 : block * 512 + 512]], 1)
        product = (da_ref[rows].astype(F32) * att_ref[rows].astype(F32)).astype(BF16)
        sums = dot(product, summing)
        sums = jnp.concatenate([sums[:, :PAIR], sums[:, PAIR:]], 0)
        top = sums.astype(BF16).astype(F32)
        left_d = jnp.concatenate([da, jnp.where(lanes == 2, top - sums, -sums).astype(BF16)], 1)
        weights = jnp.where(inside, jnp.exp2(dot_t(kx[keys], left)), 0.0)
        slope = (weights * dot_t(vx[keys], left_d)).astype(BF16)
        dv = dot(weights.astype(BF16), da)
        dk = dot(slope, q)
        turned = kx[keys, :PAIR].T
        dq = jnp.concatenate(
            [dot(turned[:HEAD_DIM], slope[:, :256]), dot(turned[HEAD_DIM:], slope[:, 256:])], 0
        )
        dq_ref[rows] = (dq * HEAD_DIM**-0.5).T.astype(BF16)
        if block == 0:
            dka[:768] = dk
            dva[:768] = dv
        else:
            dka[256:768] += dk[:512]
            dka[768:] = dk[512:]
            dva[256:768] += dv[:512]
            dva[768:] = dv[512:]
    dk = (dka[...] * (1.0 / LOG2E)).astype(BF16)
    dv = dva[...].astype(BF16)
    dk_ref[...] = dk[256:768]
    dv_ref[...] = dv[256:768]
    low_ref[0] = dk[:256]
    low_ref[1] = dv[:256]
    high_ref[0] = dk[768:]
    high_ref[1] = dv[768:]


def attention_backward(live, q, ke, ve, eq, att, da):
    part = pl.BlockSpec((ROWS, PAIR), lambda h, _: (0, h))
    ext = pl.BlockSpec((EXT, PAIR), lambda h, _: (0, h))
    edge = pl.BlockSpec((2, 256, PAIR), lambda h, _: (0, 0, h))
    shape = jax.ShapeDtypeStruct((ROWS, WIDTH), BF16)
    return pl.pallas_call(
        backward_kernel,
        grid_spec=pltpu.PrefetchScalarGridSpec(
            num_scalar_prefetch=1,
            grid=(PAIRS,),
            in_specs=[part, ext, ext, pl.BlockSpec((1, EXT, PAIR), lambda h, _: (h, 0, 0)), part, part],
            out_specs=[part] * 3 + [edge] * 2,
            scratch_shapes=[
                pltpu.VMEM((EXT, 2 * PAIR), BF16),
                pltpu.VMEM((EXT, 2 * PAIR), BF16),
                pltpu.VMEM((EXT, PAIR), F32),
                pltpu.VMEM((EXT, PAIR), F32),
            ],
        ),
        out_shape=[shape] * 3 + [jax.ShapeDtypeStruct((2, 256, WIDTH), BF16)] * 2,
        compiler_params=params(56),
        name="attention_backward",
    )(live, q, ke, ve, eq, att, da)


def kernel_slope(diff):
    return diff * lax.rsqrt(diff * diff + 0.01)


def score_kernel(
    live_ref, own_ref, all_hbm, target_ref, z_hbm, r_hbm, gain_ref, wd_ref, wo_hbm, att_hbm,
    lg_hbm, da_hbm, term_hbm,
    everyone, z, r, wo, att, lg, da, term, in_sems, out_sems,
):
    loads = start_all(
        (all_hbm, z_hbm, r_hbm, wo_hbm, att_hbm), (everyone, z, r, wo, att), in_sems
    )
    stores = [
        pltpu.make_async_copy(source, target, out_sems.at[place])
        for place, (source, target) in enumerate(((lg, lg_hbm), (da, da_hbm), (term, term_hbm)))
    ]
    members = everyone.shape[0]
    own = own_ref[...].astype(F32)
    slots = lane((own.shape[0], CYCLE_MAX))
    live = jnp.concatenate(
        [jnp.where(slots < live_ref[2 + cycle], 1.0, 0.0) for cycle in range(ROWS // CYCLE_MAX)], 1
    )
    loads[0].wait()
    pair_sum = None
    for member in range(members):
        slope = kernel_slope(own - everyone[member].astype(F32))
        pair_sum = slope if pair_sum is None else pair_sum + slope
    grad = (kernel_slope(own - target_ref[...]) - pair_sum * (1.0 / (members - 1))) * live
    back = lax.dot_general(
        grad.astype(BF16), wd_ref[...], (((0,), (0,)), ((), ())), preferred_element_type=F32
    )
    back = back.astype(BF16).astype(F32) * gain_ref[...]
    wait_all(loads[1:3])
    normal = z[...].astype(F32)
    level_grad = r[:, :1] * (back - normal * jnp.mean(back * normal, -1, keepdims=True))
    lg[...] = level_grad.astype(BF16)
    stores[0].start()
    loads[4].wait()
    whole = lax.dot_general(
        att[...], lg[...], (((0,), (0,)), ((), ())), preferred_element_type=F32
    ).astype(BF16)
    for row in range(term.shape[0]):
        for column in range(term.shape[1]):
            term[row, column] = whole[row * 64 : row * 64 + 64, column * 128 : column * 128 + 128]
    stores[2].start()
    loads[3].wait()
    da[...] = dot_t(lg[...], wo[...]).astype(BF16)
    stores[1].start()
    wait_all(stores)


def score(live, own, everyone, target, z, r, gain, wd, wo, att):
    square = pltpu.VMEM((WIDTH, WIDTH), BF16)
    rows = pltpu.VMEM((ROWS, WIDTH), BF16)
    shape = jax.ShapeDtypeStruct((ROWS, WIDTH), BF16)
    return pl.pallas_call(
        score_kernel,
        in_specs=[pl.BlockSpec(memory_space=pltpu.SMEM), WHOLE, HBM, WHOLE, HBM, HBM, WHOLE, WHOLE, HBM, HBM],
        out_specs=[HBM] * 3,
        out_shape=[shape, shape, jax.ShapeDtypeStruct((16, 8, 64, 128), BF16)],
        scratch_shapes=[
            pltpu.VMEM(everyone.shape, BF16),
            rows,
            pltpu.VMEM((ROWS, PAIR), F32),
            square, rows, rows, rows,
            pltpu.VMEM((16, 8, 64, 128), BF16),
            pltpu.SemaphoreType.DMA((5,)),
            pltpu.SemaphoreType.DMA((3,)),
        ],
        compiler_params=params(56),
        name="score",
    )(live, own, everyone, target, z, r, gain, wd, wo, att)


def final_kernel(
    x_hbm, gain_ref, q_hbm, rq_hbm, dq_hbm, wq_hbm, dv_hbm, before_hbm, after_hbm, wv_hbm,
    dk_hbm, k_hbm, rk_hbm, wk_hbm, lg_hbm, out_hbm,
    x, q, rq, dq, wq, dv, before, after, wv, dk, k, rk, wk, lg, out, in_sems, out_sems,
):
    loads = start_all(
        (q_hbm, rq_hbm, dq_hbm, wq_hbm, dv_hbm, before_hbm, after_hbm, wv_hbm,
         dk_hbm, k_hbm, rk_hbm, wk_hbm, x_hbm, lg_hbm),
        (q, rq, dq, wq, dv, before, after, wv, dk, k, rk, wk, x, lg),
        in_sems,
    )
    means = head_mean_matrix(256)

    def norm_back(y, scale, grad):
        product = (y * grad).astype(BF16)
        mean = jnp.concatenate(
            [dot(product[:, c : c + 256], means) for c in range(0, WIDTH, 256)], 1
        )
        return (scale.astype(F32) * (grad - y * mean)).astype(BF16)

    def gathered(own, kind):
        halo = jnp.concatenate([before[kind], after[kind]], 0)
        return own[...].astype(F32) + halo.astype(F32)

    wait_all(loads[:3])
    q_in = norm_back(q[...].astype(F32) * (1.0 / Q_SCALE), rq[...], dq[...].astype(F32))
    loads[3].wait()
    total = dot_t(q_in, wq[...])
    wait_all(loads[4:8])
    total += dot_t(gathered(dv, 1).astype(BF16), wv[...])
    wait_all(loads[8:12])
    k_in = norm_back(k[...].astype(F32), rk[...], gathered(dk, 0))
    total += dot_t(k_in, wk[...])
    wait_all(loads[12:])
    stores = []
    for block in range(2):
        rows = slice(block * 256, block * 256 + 256)
        state = x[rows].astype(F32)
        scale = lax.rsqrt(jnp.mean(state * state, -1, keepdims=True) + 1e-05)
        grad = total[rows] * gain_ref[...]
        y = state * scale
        back = scale * (grad - y * jnp.mean(grad * y, -1, keepdims=True))
        out[rows] = lg[rows].astype(F32) + back
        place = pl.ds(block * 256, 256)
        stores.append(pltpu.make_async_copy(out.at[place], out_hbm.at[place], out_sems.at[block]))
        stores[-1].start()
    wait_all(stores)


def finish(x, gain, q, k, rq, rk, dq, dk, dv, before, after, wq, wk, wv, lg):
    square = pltpu.VMEM((WIDTH, WIDTH), BF16)
    rows = pltpu.VMEM((ROWS, WIDTH), BF16)
    edge = pltpu.VMEM((2, 256, WIDTH), BF16)
    return pl.pallas_call(
        final_kernel,
        in_specs=[HBM, WHOLE] + [HBM] * 13,
        out_specs=HBM,
        out_shape=jax.ShapeDtypeStruct((ROWS, WIDTH), F32),
        scratch_shapes=[
            rows, rows, rows, rows, square, rows, edge, edge, square, rows, rows, rows, square, rows,
            pltpu.VMEM((ROWS, WIDTH), F32),
            pltpu.SemaphoreType.DMA((14,)),
            pltpu.SemaphoreType.DMA((2,)),
        ],
        compiler_params=params(56),
        name="finish",
    )(x, gain, q, rq, dq, wq, dv, before, after, wv, dk, k, rk, wk, lg)


def body(
    latent_grids, cycle_points, norm_gain, w_query, w_key, w_value, w_out, dec_gain, w_dec, target
):
    x = latent_grids[0]
    band = lax.axis_index("grid")
    bands = lax.axis_size("grid")
    up = [(i, i + 1) for i in range(bands - 1)]
    down = [(j, i) for i, j in up]
    norm_gain = norm_gain[None]
    dec_gain = dec_gain[None]
    live = lax.dynamic_slice(jnp.pad(cycle_points, (2, 2)), (band * 4,), (8,))

    before = lax.ppermute(x[256:], "grid", up)
    after = lax.ppermute(x[:256], "grid", down)
    q, k, v, rq, rk = project(x, norm_gain, w_query, w_key, w_value)
    members = lax.axis_size("member")
    ke, ve, att, eq, z, r, field, copies = front(
        live, before, after, w_key, w_value, q, k, v, x, w_out, norm_gain, dec_gain, w_dec, members
    )
    everyone = lax.all_to_all(copies, "member", 0, 0, tiled=True)
    lg, da, term = score(live, field, everyone, target, z, r, dec_gain, w_dec, w_out, att)
    dq, dk, dv, low, high = attention_backward(live, q, ke, ve, eq, att, da)
    grad_before = lax.ppermute(high, "grid", up)
    grad_after = lax.ppermute(low, "grid", down)
    sens = finish(
        x, norm_gain, q, k, rq, rk, dq, dk, dv, grad_before, grad_after,
        w_query, w_key, w_value, lg,
    )
    blocks = term.reshape(bands * members, 64, 128)
    pieces = lax.all_to_all(blocks, ("grid", "member"), 0, 0, tiled=True)
    out = jnp.sum(pieces.astype(F32), 0)
    return (field[None], sens[None], out)


def solution(mesh):
    placed = (P("member", "grid", None), P(), P(), P(), P(), P(), P(), P(), P(), P(None, "grid"))
    return jax.shard_map(
        body,
        mesh=mesh,
        in_specs=placed,
        out_specs=(P("member", None, "grid"), P("member", "grid", None), P("grid", "member")),
        check_vma=False,
    )
```

time: 439 us -> 127 us (0.29)
  matrix products: 168 us -> 0 us
  waiting for transfers between devices: 112 us -> 14.3 us
  Pallas kernels: 0 us -> 66 us
  other arithmetic: 52.6 us -> 0.97 us
  local copies, waits for them, and re-layouts: 36.7 us -> 3.65 us
  blocking collectives: 36.1 us -> 16.7 us
  between operations: 14.7 us -> 0.74 us
  starting transfers between devices: 16 us -> 23.4 us
    dot_general x39 -> x0, matrix products: 168 us -> none  [the longest x16 91.9 us: head_block(): jnp.einsum('rhd,ehd->hre', q_blk, k_blk, preferred_element_type=jnp.float32)]
    pallas_call x0 -> x5, Pallas kernels: none -> 66 us  [the longest x1 20.6 us: attention_backward(): pl.pallas_call(backward_kernel, grid_spec=pltpu.PrefetchScalarGridSpec(nu...]
    unnamed x3 -> x0, waiting for transfers between devices: 64.9 us -> none
    reduce_scatter x1 -> x0, waiting for transfers between devices: 37.6 us -> none  [body(): lax.psum_scatter(out_term.astype(jnp.bfloat16), 'grid', scatter_dimension...]
    all_gather x1 -> x0, blocking collectives: 36.1 us -> none  [body(): lax.all_gather(field_bf[None], 'member', axis=0, tiled=True)]
    all_to_all x0 -> x1, blocking collectives: none -> 16.7 us  [body(): everyone = lax.all_to_all(copies, 'member', 0, 0, tiled=True)]
    unnamed x94 -> x10, local copies, waits for them, and re-layouts: 18.2 us -> 1.78 us
    dynamic_update_slice x8 -> x0, other arithmetic: 13.6 us -> none  [attend(): blocks = lax.map(head_block, (queries, key_part, value_part))]
  transfers between devices with their start and end apart: 6 -> 5, of which waited for: 6 -> 3; matrix products, arithmetic and copies ran while one was open for 6% -> 0% of each run, Pallas kernels for 0% -> 32%
where the time goes in v2:
time: 127 us; the launch traced here: 126 us
  Pallas kernels  66 us (52%)
  starting transfers between devices  23.4 us (18%)
  blocking collectives  16.7 us (13%)
  waiting for transfers between devices  14.3 us (11%)
  local copies, waits for them, and re-layouts  3.65 us (3%)
    pallas_call x1, Pallas kernels, attention_backward(): pl.pallas_call(backward_kernel, grid_spec=pltpu.PrefetchScalarGridSpec(nu...  20.6 us
    pallas_call x1, Pallas kernels, front(): pl.pallas_call(front_kernel, in_specs=[pl.BlockSpec(memory_space=pltpu.SM...  18.7 us
    all_to_all x1, blocking collectives, body(): everyone = lax.all_to_all(copies, 'member', 0, 0, tiled=True)  16.7 us
    pallas_call x1, Pallas kernels, finish(): pl.pallas_call(final_kernel, in_specs=[HBM, WHOLE] + [HBM] * 13, out_spec...  11.3 us
    ppermute x1, waiting for transfers between devices, body(): grad_before = lax.ppermute(high, 'grid', up)  11 us
    pallas_call x1, Pallas kernels, project(): pl.pallas_call(project_kernel, in_specs=[HBM, WHOLE, HBM, HBM, HBM], out_...  8.14 us
    all_to_all x1, starting transfers between devices, body(): pieces = lax.all_to_all(blocks, ('grid', 'member'), 0, 0, tiled=True)  8.03 us
    pallas_call x1, Pallas kernels, score(): pl.pallas_call(score_kernel, in_specs=[pl.BlockSpec(memory_space=pltpu.SM...  7.27 us
  transfers between devices with their start and end apart: 5, of which 3 were waited for; matrix products, arithmetic and copies ran while one was open for 0% of the time, Pallas kernels for 32%

profile of v2, /device:TPU:24, one launch (start us, length us, event | category | flops | bytes accessed | tf_op | source)
XLA Modules:
  0.0 125.8 jit_solution(5076982664768957083)
XLA Ops:
  0.6 1.3 %slice_bitcast_fusion = (bf16[256,1024]{1,0:T(8,128)(2,1)S(1)}, bf16[256,1024]{1,0:T(8,128)(2,1)S(1)}) fusion(bf16[1,512,1024]{2,1,0:T(8,128)(2,1)} %param.10), kind=kLoop, calls=%fused_computation.1 | loop fusion | bytes 2097152 | tf_op jit(solution)/shard_map/slice | solution.py:518
  1.9 5.6 %collective-permute-start.1 = (bf16[256,1024]{1,0:T(8,128)(2,1)S(1)}, bf16[256,1024]{1,0:T(8,128)(2,1)S(1)}, u32[]{:S(2)}, u32[]{:S(2)}) collective-permute-start(bf16[256,1024]{1,0:T(8,128)(2,1)S(1)} %get-tuple-element.45), channel_id=1, source_target_pairs={{1,0},{2,1},{3,2},{4,3},{5,4},{6,5},{7,6},{8,7},{9,8},{10,9},{11,1... | collective-permute-start | bytes 1572872 | tf_op jit(solution)/shard_map/ppermute | solution.py:518
  7.5 1.9 %collective-permute-start = (bf16[256,1024]{1,0:T(8,128)(2,1)S(1)}, bf16[256,1024]{1,0:T(8,128)(2,1)S(1)}, u32[]{:S(2)}, u32[]{:S(2)}) collective-permute-start(bf16[256,1024]{1,0:T(8,128)(2,1)S(1)} %get-tuple-element.46), channel_id=1, source_target_pairs={{0,1},{1,2},{2,3},{3,4},{4,5},{5,6},{6,7},{7,8},{8,9},{9,10},{10,1... | collective-permute-start | bytes 1572872 | tf_op jit(solution)/shard_map/ppermute | solution.py:517
  9.4 0.0 copy-start.4
  9.4 8.1 %project_own.1 = (bf16[512,1024]{1,0:T(8,128)(2,1)}, bf16[512,1024]{1,0:T(8,128)(2,1)}, bf16[512,1024]{1,0:T(8,128)(2,1)}, bf16[512,1024]{1,0:T(8,128)(2,1)}, bf16[512,1024]{1,0:T(8,128)(2,1)}) custom-call(bf16[512,1024]{1,0:T(8,128)(2,1)} %bitcast.10, f32[1,1024]{1,0:T(1,128)} %bitcast.16, bf16[1024,1024]{1,0:T(8,128)(2,1)} %wq_hbm.3, ...), custom_call_target="tpu_custom_call" | custom-call | tf_op jit(solution)/shard_map/project_own/pallas_call | solution.py:110
  17.6 0.6 pad_dynamic-slice_fusion.live_ref
  18.2 0.0 collective-permute-done.1.after_hbm
  18.2 1.9 %collective-permute-done.before_hbm = bf16[256,1024]{1,0:T(8,128)(2,1)S(1)} collective-permute-done((bf16[256,1024]{1,0:T(8,128)(2,1)S(1)}, bf16[256,1024]{1,0:T(8,128)(2,1)S(1)}, u32[]{:S(2)}, u32[]{:S(2)}) %collective-permute-start) | collective-permute-done | bytes 524320 | tf_op jit(solution)/shard_map/ppermute | solution.py:517
  20.1 0.0 copy-done.2
  20.1 0.8 copy-done.3
  20.9 18.7 %halo_attention_decode.1 = (bf16[1024,1024]{1,0:T(8,128)(2,1)}, bf16[1024,1024]{1,0:T(8,128)(2,1)}, bf16[512,1024]{1,0:T(8,128)(2,1)}, bf16[8,1024,128]{2,1,0:T(...) custom-call(s32[8]{0:T(128)} %pad_dynamic-slice_fusion.live_ref, ...), custom_call_target="tpu_custom_call" | custom-call | tf_op jit(solution)/shard_map/halo_attention_decode/pallas_call | solution.py:247
  39.7 16.7 %all_to_all.10.all_hbm = bf16[8,100,512]{2,1,0:T(8,128)(2,1)} all-to-all(bf16[8,100,512]{2,1,0:T(8,128)(2,1)} %get-tuple-element.33), channel_id=1, replica_groups=mesh['member'=8,'grid'=16] {'member'}, dimensions={0} | all-to-all | bytes 1638400 | tf_op jit(solution)/shard_map/all_to_all | solution.py:524
  56.3 7.3 %score.1 = (bf16[512,1024]{1,0:T(8,128)(2,1)}, bf16[512,1024]{1,0:T(8,128)(2,1)}, bf16[16,8,64,128]{3,2,1,0:T(8,128)(2,1)}) custom-call(s32[8]{0:T(128)} %pad_dynamic-slice_fusion.live_ref, bf16[100,512]{1,0:T(8,128)(2,1)} %get-tuple-element.27.own_ref, bf16[8,100,512]{2,1,0:T(8,128)(2,1)} %all_to_all.10.all_hbm, f32[100,512]{1,0:T(8,128)} %target_ref.1, ...), custom_call_target="tpu_custom_call" | custom-call | tf_op jit(solution)/shard_map/score/pallas_call | solution.py:417
  63.6 8.0 %all-to-all-start.1 = ((bf16[128,64,128]{2,1,0:T(8,128)(2,1)}), bf16[128,64,128]{2,1,0:T(8,128)(2,1)S(1)}, u32[]{:S(2)}, u32[]{:S(2)}) async-start(bf16[128,64,128]{2,1,0:T(8,128)(2,1)} %bitcast.13), calls=%async_computation.1 | async-start | bytes 4194304 | tf_op jit(solution)/shard_map/all_to_all | solution.py:534
  71.6 20.6 %attention_backward.1 = (bf16[512,1024]{1,0:T(8,128)(2,1)}, bf16[512,1024]{1,0:T(8,128)(2,1)}, bf16[512,1024]{1,0:T(8,128)(2,1)}, bf16[2,256,1024]{2,1,0:T(8,128)(2,1)}, bf16[2,256,1024]{2,1,0:T(8,128)(2,1)}) custom-call(s32[8]{0:T(128)} %pad_dynamic-slice_fusion.live_ref, bf16[512,1024]{1,0:T(8,128)(2,1)} %get-tuple-element.24.q_hbm.q_ref, ...), custom_call_target="tpu_custom_call" | custom-call | tf_op jit(solution)/shard_map/attention_backward/pallas_call | solution.py:342
  92.2 2.1 %collective-permute-start.2 = (bf16[2,256,1024]{2,1,0:T(8,128)(2,1)}, bf16[2,256,1024]{2,1,0:T(8,128)(2,1)S(1)}, u32[]{:S(2)}, u32[]{:S(2)}) collective-permute-start(bf16[2,256,1024]{2,1,0:T(8,128)(2,1)} %get-tuple-element.39), channel_id=1, source_target_pairs={{0,1},{1,2},{2,3},{3,4},{4,5},{5,6},{6,7},{7,8},{8,9},{9,10},{10,1... | collective-permute-start | bytes 3145736 | tf_op jit(solution)/shard_map/ppermute | solution.py:527
  94.3 5.8 %collective-permute-start.3 = (bf16[2,256,1024]{2,1,0:T(8,128)(2,1)}, bf16[2,256,1024]{2,1,0:T(8,128)(2,1)S(1)}, u32[]{:S(2)}, u32[]{:S(2)}) collective-permute-start(bf16[2,256,1024]{2,1,0:T(8,128)(2,1)} %get-tuple-element.40), channel_id=1, source_target_pairs={{1,0},{2,1},{3,2},{4,3},{5,4},{6,5},{7,6},{8,7},{9,8},{10,9},{11,1... | collective-permute-start | bytes 3145736 | tf_op jit(solution)/shard_map/ppermute | solution.py:528
  100.1 11.0 %collective-permute-done.2.before_hbm = bf16[2,256,1024]{2,1,0:T(8,128)(2,1)S(1)} collective-permute-done((bf16[2,256,1024]{2,1,0:T(8,128)(2,1)}, bf16[2,256,1024]{2,1,0:T(8,128)(2,1)S(1)}, u32[]{:S(2)}, u32[]{:S(2)}) %collective-permute-start.2) | collective-permute-done | bytes 1048608 | tf_op jit(solution)/shard_map/ppermute | solution.py:527
  111.1 1.4 %collective-permute-done.3.after_hbm = bf16[2,256,1024]{2,1,0:T(8,128)(2,1)S(1)} collective-permute-done((bf16[2,256,1024]{2,1,0:T(8,128)(2,1)}, bf16[2,256,1024]{2,1,0:T(8,128)(2,1)S(1)}, u32[]{:S(2)}, u32[]{:S(2)}) %collective-permute-start.3) | collective-permute-done | bytes 1048608 | tf_op jit(solution)/shard_map/ppermute | solution.py:528
  112.5 0.0 copy-done
  112.5 1.0 copy-done.1
  113.5 11.3 %finish.1 = f32[512,1024]{1,0:T(8,128)} custom-call(bf16[512,1024]{1,0:T(8,128)(2,1)} %bitcast.12, f32[1,1024]{1,0:T(1,128)} %bitcast.18, bf16[512,1024]{1,0:T(8,128)(2,1)} %get-tuple-element.24.q_hbm.q_ref, bf16[512,1024]{1,0:T(8,128)(2,1)} %get-tuple-element.28.rq_hbm, bf16[512,1024]{1,0:T(8,128)(2,1)} %get-tuple-element.37.dq_hbm, ...), custom_call_target="tpu_custom_call" | custom-call | tf_op jit(solution)/shard_map/finish/pallas_call | solution.py:489
  124.8 0.0 all-to-all-done.1
  124.8 1.0 convert_reduce_fusion
  (5 shorter events, 0.0 us)
Async XLA Ops:
  1.9 16.3 %collective-permute-start.1 = (bf16[256,1024]{1,0:T(8,128)(2,1)S(1)}, bf16[256,1024]{1,0:T(8,128)(2,1)S(1)}, u32[]{:S(2)}, u32[]{:S(2)}) collective-permute-start(bf16[256,1024]{1,0:T(8,128)(2,1)S(1)} %get-tuple-element.45), channel_id=1, source_target_pairs={{1,0},{2,1},{3,2},{4,3},{5,4},{6,5},{7,6},{8,7},{9,8},{10,9},{11,1... | collective-permute-start | bytes 1572872 | tf_op jit(solution)/shard_map/ppermute | solution.py:518
  7.5 12.6 %collective-permute-start = (bf16[256,1024]{1,0:T(8,128)(2,1)S(1)}, bf16[256,1024]{1,0:T(8,128)(2,1)S(1)}, u32[]{:S(2)}, u32[]{:S(2)}) collective-permute-start(bf16[256,1024]{1,0:T(8,128)(2,1)S(1)} %get-tuple-element.46), channel_id=1, source_target_pairs={{0,1},{1,2},{2,3},{3,4},{4,5},{5,6},{6,7},{7,8},{8,9},{9,10},{10,1... | collective-permute-start | bytes 1572872 | tf_op jit(solution)/shard_map/ppermute | solution.py:517
  9.4 8.2 %copy-start.4 = (s32[64]{0:T(128)S(1)}, s32[64]{0:T(128)}, u32[]{:S(2)}) copy-start(s32[64]{0:T(128)} %param.11) | copy-start | bytes 772
  18.2 1.9 %copy-start.2 = (bf16[256,1024]{1,0:T(8,128)(2,1)}, bf16[256,1024]{1,0:T(8,128)(2,1)S(1)}, u32[]{:S(2)}) copy-start(bf16[256,1024]{1,0:T(8,128)(2,1)S(1)} %collective-permute-done.1.after_hbm) | copy-start | bytes 1572868
  20.1 0.8 copy-start.3
  63.6 61.2 %all-to-all-start.1 = ((bf16[128,64,128]{2,1,0:T(8,128)(2,1)}), bf16[128,64,128]{2,1,0:T(8,128)(2,1)S(1)}, u32[]{:S(2)}, u32[]{:S(2)}) async-start(bf16[128,64,128]{2,1,0:T(8,128)(2,1)} %bitcast.13), calls=%async_computation.1 | async-start | bytes 4194304 | tf_op jit(solution)/shard_map/all_to_all | solution.py:534
  92.2 18.9 %collective-permute-start.2 = (bf16[2,256,1024]{2,1,0:T(8,128)(2,1)}, bf16[2,256,1024]{2,1,0:T(8,128)(2,1)S(1)}, u32[]{:S(2)}, u32[]{:S(2)}) collective-permute-start(bf16[2,256,1024]{2,1,0:T(8,128)(2,1)} %get-tuple-element.39), channel_id=1, source_target_pairs={{0,1},{1,2},{2,3},{3,4},{4,5},{5,6},{6,7},{7,8},{8,9},{9,10},{10,1... | collective-permute-start | bytes 3145736 | tf_op jit(solution)/shard_map/ppermute | solution.py:527
  94.3 18.2 %collective-permute-start.3 = (bf16[2,256,1024]{2,1,0:T(8,128)(2,1)}, bf16[2,256,1024]{2,1,0:T(8,128)(2,1)S(1)}, u32[]{:S(2)}, u32[]{:S(2)}) collective-permute-start(bf16[2,256,1024]{2,1,0:T(8,128)(2,1)} %get-tuple-element.40), channel_id=1, source_target_pairs={{1,0},{2,1},{3,2},{4,3},{5,4},{6,5},{7,6},{8,7},{9,8},{10,9},{11,1... | collective-permute-start | bytes 3145736 | tf_op jit(solution)/shard_map/ppermute | solution.py:528
  111.1 1.4 %copy-start = (bf16[2,256,1024]{2,1,0:T(8,128)(2,1)}, bf16[2,256,1024]{2,1,0:T(8,128)(2,1)S(1)}, u32[]{:S(2)}) copy-start(bf16[2,256,1024]{2,1,0:T(8,128)(2,1)S(1)} %collective-permute-done.2.before_hbm) | copy-start | bytes 3145732
  112.5 1.0 copy-start.1

commit v3 on v2

--- a/solution.py
+++ b/solution.py
@@ -3,7 +3,7 @@
 from jax import lax
 from jax.experimental import pallas as pl
 from jax.experimental.pallas import tpu as pltpu
-from jax.sharding import PartitionSpec as P
+from jax.sharding import Mesh, PartitionSpec as P
 
 HEAD_DIM = 64
 CYCLE_MAX = 128
@@ -22,6 +22,10 @@
 
 def params(mib):
     return pltpu.CompilerParams(vmem_limit_bytes=mib * 1024 * 1024)
+
+
+def cost(gigaflops):
+    return pl.CostEstimate(flops=int(gigaflops * 1e9), bytes_accessed=4 << 20, transcendentals=0)
 
 
 def dot(left, right):
@@ -122,12 +126,19 @@
     )(x, gain, wq, wk, wv)
 
 
-def key_extras(live_ref):
+def live_points(cycle_points_ref, cycle):
+    index = lax.axis_index(("chip", "core")) * (ROWS // CYCLE_MAX) - WINDOW // CYCLE_MAX + cycle
+    count = cycle_points_ref.shape[0]
+    points = cycle_points_ref[jnp.clip(index, 0, count - 1)]
+    return jnp.where((index >= 0) & (index < count), points, 0)
+
+
+def key_extras(points_ref):
     pieces = []
     lanes = lane((CYCLE_MAX, PAIR))
     slots = lax.broadcasted_iota(jnp.int32, (CYCLE_MAX, PAIR), 0)
     for cycle in range(EXT // CYCLE_MAX):
-        bias = jnp.where(slots < live_ref[cycle], 0.0, DEAD)
+        bias = jnp.where(slots < live_points(points_ref, cycle), 0.0, DEAD)
         pieces.append(jnp.where(lanes == 0, bias, jnp.where(lanes < 3, 1.0, 0.0)).astype(BF16))
     return pieces
 
@@ -167,7 +178,7 @@
 
 
 def front_kernel(
-    live_ref, before_hbm, after_hbm, wk_hbm, wv_hbm, q_hbm, k_hbm, v_hbm, x_hbm, wo_hbm,
+    points_ref, before_hbm, after_hbm, wk_hbm, wv_hbm, q_hbm, k_hbm, v_hbm, x_hbm, wo_hbm,
     gain_ref, dec_gain_ref, wd_ref,
     kx_hbm, vx_hbm, att_hbm, eq_hbm, z_hbm, r_hbm, field_hbm, copies_hbm,
     halo, wk, wv, q, ke, ve, x, wo, att, eq, z, r, field, kx, vx, in_sems, out_sems,
@@ -178,7 +189,7 @@
         (halo.at[pl.ds(0, 256)], halo.at[pl.ds(256, 256)], wk, wv, q, ke.at[own], ve.at[own], wo, x),
         in_sems,
     )
-    for cycle, piece in enumerate(key_extras(live_ref)):
+    for cycle, piece in enumerate(key_extras(points_ref)):
         kx[cycle * CYCLE_MAX : (cycle + 1) * CYCLE_MAX, PAIR:] = piece
     vx[:, PAIR:] = jnp.ones((EXT, PAIR), BF16)
     means = head_mean_matrix(256)
@@ -277,86 +288,117 @@
     )(live, before, after, wk, wv, q, k, v, x, wo, gain, dec_gain, wd)
 
 
-def backward_kernel(
-    live_ref, q_ref, ke_ref, ve_ref, eq_ref, att_ref, da_ref,
-    dq_ref, dk_ref, dv_ref, low_ref, high_ref, kx, vx, dka, dva,
-):
+def weights_kernel(points_ref, q_ref, ke_ref, eq_ref, edge_ref, own_ref, kx):
     @pl.when(pl.program_id(0) == 0)
     def _():
-        for cycle, piece in enumerate(key_extras(live_ref)):
+        for cycle, piece in enumerate(key_extras(points_ref)):
             kx[cycle * CYCLE_MAX : (cycle + 1) * CYCLE_MAX, PAIR:] = piece
-            vx[cycle * CYCLE_MAX : (cycle + 1) * CYCLE_MAX, PAIR:] = piece
 
     kx[:, :PAIR] = ke_ref[...]
-    vx[:, :PAIR] = ve_ref[...]
     low = lane((256, PAIR)) < HEAD_DIM
+    inside = window_mask((768, 512), 1)
+    for block in range(2):
+        q = by_head(q_ref[block * 256 : block * 256 + 256], low)
+        left = jnp.concatenate([q, eq_ref[0, block * 512 : block * 512 + 512]], 1)
+        scores = dot_t(kx[block * 256 : block * 256 + 768], left)
+        weights = jnp.where(inside, jnp.exp2(scores), 0.0).astype(BF16)
+        edge_ref[0, block] = weights[:256] if block == 0 else weights[512:]
+        own_ref[0, block] = weights[256:] if block == 0 else weights[:512]
+
+
+def attention_weights(live, q, ke, eq):
+    part = pl.BlockSpec((ROWS, PAIR), lambda h, _: (0, h))
+    ext = pl.BlockSpec((EXT, PAIR), lambda h, _: (0, h))
+    return pl.pallas_call(
+        weights_kernel,
+        grid_spec=pltpu.PrefetchScalarGridSpec(
+            num_scalar_prefetch=1,
+            grid=(PAIRS,),
+            in_specs=[part, ext, pl.BlockSpec((1, EXT, PAIR), lambda h, _: (h, 0, 0))],
+            out_specs=[
+                pl.BlockSpec((1, 2, 256, 512), lambda h, _: (h, 0, 0, 0)),
+                pl.BlockSpec((1, 2, 512, 512), lambda h, _: (h, 0, 0, 0)),
+            ],
+            scratch_shapes=[pltpu.VMEM((EXT, 2 * PAIR), BF16)],
+        ),
+        out_shape=[
+            jax.ShapeDtypeStruct((PAIRS, 2, 256, 512), BF16),
+            jax.ShapeDtypeStruct((PAIRS, 2, 512, 512), BF16),
+        ],
+        compiler_params=params(56),
+        cost_estimate=cost(8),
+        name="attention_weights",
+    )(live, q, ke, eq)
+
+
+def slope_operands(q_rows, att_rows, da_rows, low):
     lanes = lane((512, PAIR))
-    inside = window_mask((768, 512), 1)
     feature = lax.broadcasted_iota(jnp.int32, (PAIR, 2 * PAIR), 0) // HEAD_DIM
     column = lane((PAIR, 2 * PAIR))
     wanted = (feature == column // PAIR) & ((column % PAIR == 1) | (column % PAIR == 2))
     summing = jnp.where(wanted, 1.0, 0.0).astype(BF16)
+    q = by_head(q_rows, low)
+    da = by_head(da_rows, low)
+    product = (da_rows.astype(F32) * att_rows.astype(F32)).astype(BF16)
+    sums = dot(product, summing)
+    sums = jnp.concatenate([sums[:, :PAIR], sums[:, PAIR:]], 0)
+    top = sums.astype(BF16).astype(F32)
+    offsets = jnp.where(lanes == 2, top - sums, -sums).astype(BF16)
+    return q, da, jnp.concatenate([da, offsets], 1)
+
+
+def ones_extra(count):
+    lanes = lane((count, PAIR))
+    return jnp.where((lanes == 1) | (lanes == 2), 1.0, 0.0).astype(BF16)
+
+
+def query_piece(keys, slope):
+    turned = keys.T
+    piece = jnp.concatenate(
+        [dot(turned[:HEAD_DIM], slope[:, :256]), dot(turned[HEAD_DIM:], slope[:, 256:])], 0
+    )
+    return (piece * HEAD_DIM**-0.5).T
+
+
+def own_kernel(
+    q_ref, ka_ref, kb_ref, va_ref, vb_ref, att_ref, da_ref, w_ref, part_ref, dq_ref, dk_ref, dv_ref
+):
+    low = lane((256, PAIR)) < HEAD_DIM
+    values = jnp.concatenate([va_ref[...], vb_ref[...]], 0)
+    values = jnp.concatenate([values, ones_extra(512)], 1)
+    keys = jnp.concatenate([ka_ref[...], kb_ref[...]], 0)
+    operands, slopes = [], []
     for block in range(2):
         rows = slice(block * 256, block * 256 + 256)
-        keys = slice(block * 256, block * 256 + 768)
-        q = by_head(q_ref[rows], low)
-        da = by_head(da_ref[rows], low)
-        left = jnp.concatenate([q, eq_ref[0, block * 512 : block * 512 + 512]], 1)
-        product = (da_ref[rows].astype(F32) * att_ref[rows].astype(F32)).astype(BF16)
-        sums = dot(product, summing)
-        sums = jnp.concatenate([sums[:, :PAIR], sums[:, PAIR:]], 0)
-        top = sums.astype(BF16).astype(F32)
-        left_d = jnp.concatenate([da, jnp.where(lanes == 2, top - sums, -sums).astype(BF16)], 1)
-        weights = jnp.where(inside, jnp.exp2(dot_t(kx[keys], left)), 0.0)
-        slope = (weights * dot_t(vx[keys], left_d)).astype(BF16)
-        dv = dot(weights.astype(BF16), da)
-        dk = dot(slope, q)
-        turned = kx[keys, :PAIR].T
-        dq = jnp.concatenate(
-            [dot(turned[:HEAD_DIM], slope[:, :256]), dot(turned[HEAD_DIM:], slope[:, 256:])], 0
-        )
-        dq_ref[rows] = (dq * HEAD_DIM**-0.5).T.astype(BF16)
-        if block == 0:
-            dka[:768] = dk
-            dva[:768] = dv
-        else:
-            dka[256:768] += dk[:512]
-            dka[768:] = dk[512:]
-            dva[256:768] += dv[:512]
-            dva[768:] = dv[512:]
-    dk = (dka[...] * (1.0 / LOG2E)).astype(BF16)
-    dv = dva[...].astype(BF16)
-    dk_ref[...] = dk[256:768]
-    dv_ref[...] = dv[256:768]
-    low_ref[0] = dk[:256]
-    low_ref[1] = dv[:256]
-    high_ref[0] = dk[768:]
-    high_ref[1] = dv[768:]
-
-
-def attention_backward(live, q, ke, ve, eq, att, da):
-    part = pl.BlockSpec((ROWS, PAIR), lambda h, _: (0, h))
-    ext = pl.BlockSpec((EXT, PAIR), lambda h, _: (0, h))
-    edge = pl.BlockSpec((2, 256, PAIR), lambda h, _: (0, 0, h))
+        operands.append(slope_operands(q_ref[rows], att_ref[rows], da_ref[rows], low))
+        slope = w_ref[0, block].astype(F32) * dot_t(values, operands[block][2])
+        slopes.append(slope.astype(BF16))
+    weights = jnp.concatenate([w_ref[0, 0], w_ref[0, 1]], 1)
+    dv_ref[...] = dot(weights, jnp.concatenate([operands[0][1], operands[1][1]], 0)).astype(BF16)
+    dk = dot(jnp.concatenate(slopes, 1), jnp.concatenate([operands[0][0], operands[1][0]], 0))
+    dk_ref[...] = (dk * (1.0 / LOG2E)).astype(BF16)
+    for block in range(2):
+        rows = slice(block * 256, block * 256 + 256)
+        piece = query_piece(keys, slopes[block])
+        dq_ref[rows] = (part_ref[rows].astype(F32) + piece).astype(BF16)
+
+
+def own_backward(q, ke, ve, att, da, weights, dq):
+    part = pl.BlockSpec((ROWS, PAIR), lambda h: (0, h))
+    second = pl.BlockSpec((256, PAIR), lambda h: (1, h))
+    third = pl.BlockSpec((256, PAIR), lambda h: (2, h))
     shape = jax.ShapeDtypeStruct((ROWS, WIDTH), BF16)
     return pl.pallas_call(
-        backward_kernel,
-        grid_spec=pltpu.PrefetchScalarGridSpec(
-            num_scalar_prefetch=1,
-            grid=(PAIRS,),
-            in_specs=[part, ext, ext, pl.BlockSpec((1, EXT, PAIR), lambda h, _: (h, 0, 0)), part, part],
-            out_specs=[part] * 3 + [edge] * 2,
-            scratch_shapes=[
-                pltpu.VMEM((EXT, 2 * PAIR), BF16),
-                pltpu.VMEM((EXT, 2 * PAIR), BF16),
-                pltpu.VMEM((EXT, PAIR), F32),
-                pltpu.VMEM((EXT, PAIR), F32),
-            ],
-        ),
-        out_shape=[shape] * 3 + [jax.ShapeDtypeStruct((2, 256, WIDTH), BF16)] * 2,
+        own_kernel,
+        grid=(PAIRS,),
+        in_specs=[part, second, third, second, third, part, part]
+        + [pl.BlockSpec((1, 2, 512, 512), lambda h: (h, 0, 0, 0)), part],
+        out_specs=[part] * 3,
+        out_shape=[shape] * 3,
         compiler_params=params(56),
-        name="attention_backward",
-    )(live, q, ke, ve, eq, att, da)
+        cost_estimate=cost(15),
+        name="own_backward",
+    )(q, ke, ke, ve, ve, att, da, weights, dq)
 
 
 def kernel_slope(diff):
@@ -364,73 +406,141 @@
 
 
 def score_kernel(
-    live_ref, own_ref, all_hbm, target_ref, z_hbm, r_hbm, gain_ref, wd_ref, wo_hbm, att_hbm,
-    lg_hbm, da_hbm, term_hbm,
-    everyone, z, r, wo, att, lg, da, term, in_sems, out_sems,
+    points_ref, own_ref, all_hbm, target_hbm, z_hbm, r_hbm, gain_ref, wd_ref, wo_hbm, att_hbm,
+    q_hbm, ke_hbm, ve_hbm, w_hbm,
+    lg_hbm, da_hbm, mine_hbm, theirs_hbm, dq_hbm, low_hbm, high_hbm,
+    everyone, target, z, r, wo, att, q, ke, ve, w, lg, da, term, dq, edges,
+    in_sems, edge_sems, out_sems,
 ):
+    halves = (pl.ds(0, 256), pl.ds(768, 256))
     loads = start_all(
-        (all_hbm, z_hbm, r_hbm, wo_hbm, att_hbm), (everyone, z, r, wo, att), in_sems
+        [all_hbm, target_hbm, z_hbm, r_hbm, att_hbm, wo_hbm, q_hbm]
+        + [ref.at[half] for ref in (ve_hbm, ke_hbm) for half in halves]
+        + [w_hbm],
+        [everyone, target, z, r, att, wo, q]
+        + [ref.at[half] for ref in (ve, ke) for half in range(2)]
+        + [w],
+        in_sems,
     )
     stores = [
-        pltpu.make_async_copy(source, target, out_sems.at[place])
-        for place, (source, target) in enumerate(((lg, lg_hbm), (da, da_hbm), (term, term_hbm)))
+        pltpu.make_async_copy(source, place, out_sems.at[index])
+        for index, (source, place) in enumerate(
+            (
+                (lg, lg_hbm),
+                (da, da_hbm),
+                (term.at[lax.axis_index("core")], mine_hbm),
+                (term.at[1 - lax.axis_index("core")], theirs_hbm),
+                (dq, dq_hbm),
+            )
+        )
     ]
     members = everyone.shape[0]
     own = own_ref[...].astype(F32)
     slots = lane((own.shape[0], CYCLE_MAX))
     live = jnp.concatenate(
-        [jnp.where(slots < live_ref[2 + cycle], 1.0, 0.0) for cycle in range(ROWS // CYCLE_MAX)], 1
-    )
-    loads[0].wait()
+        [jnp.where(slots < live_points(points_ref, 2 + cycle), 1.0, 0.0) for cycle in range(ROWS // CYCLE_MAX)], 1
+    )
+    wait_all(loads[:2])
     pair_sum = None
     for member in range(members):
         slope = kernel_slope(own - everyone[member].astype(F32))
         pair_sum = slope if pair_sum is None else pair_sum + slope
-    grad = (kernel_slope(own - target_ref[...]) - pair_sum * (1.0 / (members - 1))) * live
+    grad = (kernel_slope(own - target[...]) - pair_sum * (1.0 / (members - 1))) * live
     back = lax.dot_general(
         grad.astype(BF16), wd_ref[...], (((0,), (0,)), ((), ())), preferred_element_type=F32
     )
     back = back.astype(BF16).astype(F32) * gain_ref[...]
-    wait_all(loads[1:3])
+    wait_all(loads[2:4])
     normal = z[...].astype(F32)
     level_grad = r[:, :1] * (back - normal * jnp.mean(back * normal, -1, keepdims=True))
     lg[...] = level_grad.astype(BF16)
     stores[0].start()
-    loads[4].wait()
+    wait_all(loads[4:6])
+    da[...] = dot_t(lg[...], wo[...]).astype(BF16)
+    stores[1].start()
     whole = lax.dot_general(
         att[...], lg[...], (((0,), (0,)), ((), ())), preferred_element_type=F32
     ).astype(BF16)
-    for row in range(term.shape[0]):
-        for column in range(term.shape[1]):
-            term[row, column] = whole[row * 64 : row * 64 + 64, column * 128 : column * 128 + 128]
+    for row in range(16):
+        for column in range(8):
+            for half in range(2):
+                first = row * 64 + half * 32
+                term[half, row, column] = whole[
+                    first : first + 32, column * 128 : column * 128 + 128
+                ]
     stores[2].start()
-    loads[3].wait()
-    da[...] = dot_t(lg[...], wo[...]).astype(BF16)
-    stores[1].start()
+    stores[3].start()
+    wait_all(loads[6:])
+
+    low = lane((256, PAIR)) < HEAD_DIM
+    ones = ones_extra(256)
+
+    def store(pair, block):
+        columns = pl.ds(pl.multiple_of(pair * PAIR, PAIR), PAIR)
+        place = (low_hbm, high_hbm)[block]
+        return pltpu.make_async_copy(
+            edges.at[block, :, :, columns], place.at[:, :, columns], edge_sems.at[block, pair]
+        )
+
+    def pair_step(step, carry):
+        for pair in (step * 2, step * 2 + 1):
+            columns = pl.ds(pl.multiple_of(pair * PAIR, PAIR), PAIR)
+            for block in range(2):
+                rows = slice(block * 256, block * 256 + 256)
+                queries, grads, left = slope_operands(
+                    q[rows, columns], att[rows, columns], da[rows, columns], low
+                )
+                weights = w[pair, block]
+                slope = dot_t(jnp.concatenate([ve[block, :, columns], ones], 1), left)
+                slope = (weights.astype(F32) * slope).astype(BF16)
+                edges[block, 0, :, columns] = (dot(slope, queries) * (1.0 / LOG2E)).astype(BF16)
+                edges[block, 1, :, columns] = dot(weights, grads).astype(BF16)
+                dq[rows, columns] = query_piece(ke[block, :, columns], slope).astype(BF16)
+        for pair in (step * 2, step * 2 + 1):
+            for block in range(2):
+                store(pair, block).start()
+        return carry
+
+    lax.fori_loop(0, PAIRS // 2, pair_step, 0)
+    stores[4].start()
+    for pair in range(PAIRS):
+        for block in range(2):
+            store(pair, block).wait()
     wait_all(stores)
 
 
-def score(live, own, everyone, target, z, r, gain, wd, wo, att):
+def score(live, own, everyone, target, z, r, gain, wd, wo, att, q, ke, ve, weights):
     square = pltpu.VMEM((WIDTH, WIDTH), BF16)
     rows = pltpu.VMEM((ROWS, WIDTH), BF16)
+    halves = pltpu.VMEM((2, 256, WIDTH), BF16)
     shape = jax.ShapeDtypeStruct((ROWS, WIDTH), BF16)
+    edge = jax.ShapeDtypeStruct((2, 256, WIDTH), BF16)
+    term = jax.ShapeDtypeStruct((16, 8, 32, 128), BF16)
     return pl.pallas_call(
         score_kernel,
-        in_specs=[pl.BlockSpec(memory_space=pltpu.SMEM), WHOLE, HBM, WHOLE, HBM, HBM, WHOLE, WHOLE, HBM, HBM],
-        out_specs=[HBM] * 3,
-        out_shape=[shape, shape, jax.ShapeDtypeStruct((16, 8, 64, 128), BF16)],
+        in_specs=[pl.BlockSpec(memory_space=pltpu.SMEM), WHOLE]
+        + [HBM] * 4 + [WHOLE] * 2 + [HBM] * 6,
+        out_specs=[HBM] * 7,
+        out_shape=[shape, shape, term, term, shape, edge, edge],
         scratch_shapes=[
             pltpu.VMEM(everyone.shape, BF16),
+            pltpu.VMEM(target.shape, F32),
             rows,
             pltpu.VMEM((ROWS, PAIR), F32),
-            square, rows, rows, rows,
-            pltpu.VMEM((16, 8, 64, 128), BF16),
+            square, rows, rows, halves, halves,
+            pltpu.VMEM((PAIRS, 2, 256, 512), BF16),
+            rows, rows,
+            pltpu.VMEM((2, 16, 8, 32, 128), BF16),
+            rows,
+            pltpu.VMEM((2, 2, 256, WIDTH), BF16),
+            pltpu.SemaphoreType.DMA((12,)),
+            pltpu.SemaphoreType.DMA((2, PAIRS)),
             pltpu.SemaphoreType.DMA((5,)),
-            pltpu.SemaphoreType.DMA((3,)),
         ],
         compiler_params=params(56),
-        name="score",
-    )(live, own, everyone, target, z, r, gain, wd, wo, att)
+        cost_estimate=cost(15),
+        name="score_and_edges",
+    )(live, own, everyone, target, z, r, gain, wd, wo, att, q, ke, ve, weights)
 
 
 def final_kernel(
@@ -506,42 +616,51 @@
     latent_grids, cycle_points, norm_gain, w_query, w_key, w_value, w_out, dec_gain, w_dec, target
 ):
     x = latent_grids[0]
-    band = lax.axis_index("grid")
-    bands = lax.axis_size("grid")
+    grid = ("chip", "core")
+    bands = lax.axis_size(grid)
     up = [(i, i + 1) for i in range(bands - 1)]
     down = [(j, i) for i, j in up]
     norm_gain = norm_gain[None]
     dec_gain = dec_gain[None]
-    live = lax.dynamic_slice(jnp.pad(cycle_points, (2, 2)), (band * 4,), (8,))
-
-    before = lax.ppermute(x[256:], "grid", up)
-    after = lax.ppermute(x[:256], "grid", down)
+
+    before = lax.ppermute(x[256:], grid, up)
+    after = lax.ppermute(x[:256], grid, down)
     q, k, v, rq, rk = project(x, norm_gain, w_query, w_key, w_value)
     members = lax.axis_size("member")
     ke, ve, att, eq, z, r, field, copies = front(
-        live, before, after, w_key, w_value, q, k, v, x, w_out, norm_gain, dec_gain, w_dec, members
+        cycle_points, before, after, w_key, w_value, q, k, v, x, w_out, norm_gain, dec_gain, w_dec, members
     )
     everyone = lax.all_to_all(copies, "member", 0, 0, tiled=True)
-    lg, da, term = score(live, field, everyone, target, z, r, dec_gain, w_dec, w_out, att)
-    dq, dk, dv, low, high = attention_backward(live, q, ke, ve, eq, att, da)
-    grad_before = lax.ppermute(high, "grid", up)
-    grad_after = lax.ppermute(low, "grid", down)
+    edge_weights, own_weights = attention_weights(cycle_points, q, ke, eq)
+    lg, da, mine, theirs, dq, low, high = score(
+        cycle_points, field, everyone, target, z, r, dec_gain, w_dec, w_out, att, q, ke, ve, edge_weights
+    )
+    sibling = lax.ppermute(theirs, "core", [(0, 1), (1, 0)])
+    grad_before = lax.ppermute(high, grid, up)
+    grad_after = lax.ppermute(low, grid, down)
+    dq, dk, dv = own_backward(q, ke, ve, att, da, own_weights, dq)
     sens = finish(
         x, norm_gain, q, k, rq, rk, dq, dk, dv, grad_before, grad_after,
         w_query, w_key, w_value, lg,
     )
-    blocks = term.reshape(bands * members, 64, 128)
-    pieces = lax.all_to_all(blocks, ("grid", "member"), 0, 0, tiled=True)
-    out = jnp.sum(pieces.astype(F32), 0)
+    blocks = (mine.astype(F32) + sibling.astype(F32)).astype(BF16)
+    pieces = lax.all_to_all(
+        blocks.reshape(128, 32, 128), ("chip", "core", "member"), 0, 0, tiled=True
+    )
+    halves = jnp.sum(pieces.reshape(8, 2, 8, 32, 128).astype(F32), (0, 2))
+    out = halves.reshape(64, 128)
     return (field[None], sens[None], out)
 
 
 def solution(mesh):
-    placed = (P("member", "grid", None), P(), P(), P(), P(), P(), P(), P(), P(), P(None, "grid"))
+    members, bands = mesh.devices.shape
+    mesh = Mesh(mesh.devices.reshape(members, bands // 2, 2), ("member", "chip", "core"))
+    grid = ("chip", "core")
+    placed = (P("member", grid, None), P(), P(), P(), P(), P(), P(), P(), P(), P(None, grid))
     return jax.shard_map(
         body,
         mesh=mesh,
         in_specs=placed,
-        out_specs=(P("member", None, "grid"), P("member", "grid", None), P("grid", "member")),
+        out_specs=(P("member", None, grid), P("member", grid, None), P(grid, "member")),
         check_vma=False,
     )

time: 127 us -> 124 us (0.976)
  blocking collectives: 16.7 us -> 0 us
  Pallas kernels: 66 us -> 81.7 us
  waiting for transfers between devices: 14.3 us -> 2.54 us
  starting transfers between devices: 23.4 us -> 29.1 us
  other arithmetic: 0.97 us -> 3.29 us
    all_to_all x1 -> x0, blocking collectives: 16.7 us -> none  [body(): everyone = lax.all_to_all(copies, 'member', 0, 0, tiled=True)]
    ppermute x4 -> x5, waiting for transfers between devices: 14.3 us -> 2.53 us  [the longest x1 2.52 us: body(): before = lax.ppermute(x[256:], grid, up)]
    pallas_call x1, Pallas kernels: 7.27 us -> 16.8 us  [score(): pl.pallas_call(score_kernel, in_specs=[pl.BlockSpec(memory_space=pltpu.SM...]
    pallas_call x1 -> x2, Pallas kernels: 20.6 us -> 26.7 us  [the longest x1 15.5 us: own_backward(): pl.pallas_call(own_kernel, grid=(PAIRS,), in_specs=[part, second, third,...]
    all_to_all x1 -> x2, starting transfers between devices: 8.03 us -> 13.8 us  [the longest x1 7.25 us: body(): everyone = lax.all_to_all(copies, 'member', 0, 0, tiled=True)]
    convert_element_type x0 -> x1, other arithmetic: none -> 2.51 us  [body(): blocks = (mine.astype(F32) + sibling.astype(F32)).astype(BF16)]
    ppermute x4 -> x5, starting transfers between devices: 15.4 us -> 15.2 us  [the longest x1 5.57 us: body(): after = lax.ppermute(x[:256], grid, down)]
  transfers between devices with their start and end apart: 5 -> 7, of which waited for: 3 -> 1; matrix products, arithmetic and copies ran while one was open for 0% -> 2% of each run, Pallas kernels for 32% -> 38%
where the time goes in v3:
time: 124 us; the launch traced here: 122 us
  Pallas kernels  81.7 us (66%)
  starting transfers between devices  29.1 us (23%)
  local copies, waits for them, and re-layouts  4.32 us (3%)
  other arithmetic  3.29 us (3%)
  waiting for transfers between devices  2.54 us (2%)
    pallas_call x1, Pallas kernels, front(): pl.pallas_call(front_kernel, in_specs=[pl.BlockSpec(memory_space=pltpu.SM...  18.8 us
    pallas_call x1, Pallas kernels, score(): pl.pallas_call(score_kernel, in_specs=[pl.BlockSpec(memory_space=pltpu.SM...  16.8 us
    pallas_call x1, Pallas kernels, own_backward(): pl.pallas_call(own_kernel, grid=(PAIRS,), in_specs=[part, second, third,...  15.5 us
    pallas_call x1, Pallas kernels, finish(): pl.pallas_call(final_kernel, in_specs=[HBM, WHOLE] + [HBM] * 13, out_spec...  11.3 us
    pallas_call x1, Pallas kernels, attention_weights(): pl.pallas_call(weights_kernel, grid_spec=pltpu.PrefetchScalarGridSpec(num...  11.2 us
    pallas_call x1, Pallas kernels, project(): pl.pallas_call(project_kernel, in_specs=[HBM, WHOLE, HBM, HBM, HBM], out_...  8.13 us
    all_to_all x1, starting transfers between devices, body(): everyone = lax.all_to_all(copies, 'member', 0, 0, tiled=True)  7.25 us
    all_to_all x1, starting transfers between devices, body(): lax.all_to_all(blocks.reshape(128, 32, 128), ('chip', 'core', 'member'),...  6.57 us
  transfers between devices with their start and end apart: 7, of which 1 were waited for; matrix products, arithmetic and copies ran while one was open for 2% of the time, Pallas kernels for 38%

profile of v3, /device:TPU:24, one launch (start us, length us, event | category | flops | bytes accessed | tf_op | source)
XLA Modules:
  0.0 121.7 jit_solution(1540935267331777740)
XLA Ops:
  0.6 1.3 %slice_bitcast_fusion = (bf16[256,1024]{1,0:T(8,128)(2,1)S(1)}, bf16[256,1024]{1,0:T(8,128)(2,1)S(1)}) fusion(bf16[1,512,1024]{2,1,0:T(8,128)(2,1)} %param.10), kind=kLoop, calls=%fused_computation.2 | loop fusion | bytes 2097152 | tf_op jit(solution)/shard_map/slice | solution.py:627
  1.9 5.6 %collective-permute-start.1 = (bf16[256,1024]{1,0:T(8,128)(2,1)S(1)}, bf16[256,1024]{1,0:T(8,128)(2,1)S(1)}, u32[]{:S(2)}, u32[]{:S(2)}) collective-permute-start(bf16[256,1024]{1,0:T(8,128)(2,1)S(1)} %get-tuple-element.53), channel_id=1, source_target_pairs={{1,0},{2,1},{3,2},{4,3},{5,4},{6,5},{7,6},{8,7},{9,8},{10,9},{11,1... | collective-permute-start | bytes 1572872 | tf_op jit(solution)/shard_map/ppermute | solution.py:627
  7.5 1.9 %collective-permute-start = (bf16[256,1024]{1,0:T(8,128)(2,1)S(1)}, bf16[256,1024]{1,0:T(8,128)(2,1)S(1)}, u32[]{:S(2)}, u32[]{:S(2)}) collective-permute-start(bf16[256,1024]{1,0:T(8,128)(2,1)S(1)} %get-tuple-element.54), channel_id=1, source_target_pairs={{0,1},{1,2},{2,3},{3,4},{4,5},{5,6},{6,7},{7,8},{8,9},{9,10},{10,1... | collective-permute-start | bytes 1572872 | tf_op jit(solution)/shard_map/ppermute | solution.py:626
  9.4 8.1 %project_own.1 = (bf16[512,1024]{1,0:T(8,128)(2,1)}, bf16[512,1024]{1,0:T(8,128)(2,1)}, bf16[512,1024]{1,0:T(8,128)(2,1)}, bf16[512,1024]{1,0:T(8,128)(2,1)}, bf16[512,1024]{1,0:T(8,128)(2,1)}) custom-call(bf16[512,1024]{1,0:T(8,128)(2,1)} %bitcast.13, f32[1,1024]{1,0:T(1,128)} %bitcast.18, bf16[1024,1024]{1,0:T(8,128)(2,1)} %wq_hbm.3, ...), custom_call_target="tpu_custom_call" | custom-call | tf_op jit(solution)/shard_map/project_own/pallas_call | solution.py:114
  17.5 0.0 collective-permute-done.1.after_hbm
  17.6 2.5 %collective-permute-done.before_hbm = bf16[256,1024]{1,0:T(8,128)(2,1)S(1)} collective-permute-done((bf16[256,1024]{1,0:T(8,128)(2,1)S(1)}, bf16[256,1024]{1,0:T(8,128)(2,1)S(1)}, u32[]{:S(2)}, u32[]{:S(2)}) %collective-permute-start) | collective-permute-done | bytes 524320 | tf_op jit(solution)/shard_map/ppermute | solution.py:626
  20.1 0.8 copy-done.4
  20.9 18.8 %halo_attention_decode.1 = (bf16[1024,1024]{1,0:T(8,128)(2,1)}, bf16[1024,1024]{1,0:T(8,128)(2,1)}, bf16[512,1024]{1,0:T(8,128)(2,1)}, bf16[8,1024,128]{2,1,0:T(...) custom-call(s32[64]{0:T(128)} %points_ref.5, ...), custom_call_target="tpu_custom_call" | custom-call | tf_op jit(solution)/shard_map/halo_attention_decode/pallas_call | solution.py:258
  39.7 7.3 %all-to-all-start = ((bf16[8,100,512]{2,1,0:T(8,128)(2,1)}), bf16[8,100,512]{2,1,0:T(8,128)(2,1)S(1)}, u32[]{:S(2)}, u32[]{:S(2)}) async-start(bf16[8,100,512]{2,1,0:T(8,128)(2,1)} %get-tuple-element.36), calls=%async_computation | async-start | bytes 1703936 | tf_op jit(solution)/shard_map/all_to_all | solution.py:633
  46.9 11.2 %attention_weights.1 = (bf16[8,2,256,512]{3,2,1,0:T(8,128)(2,1)}, bf16[8,2,512,512]{3,2,1,0:T(8,128)(2,1)}) custom-call(s32[64]{0:T(128)} %points_ref.5, bf16[512,1024]{1,0:T(8,128)(2,1)} %get-tuple-element.28.q_hbm.q_ref, bf16[1024,1024]{1,0:T(8,128)(2,1)} %get-tuple-element.33.ke_ref.ke_hbm.ka_ref.kb_ref, bf16[8,1024,128]{2,1,0:T(8,128)(2,1)} %get-tuple-element.39.eq_ref), custom_call_target="tpu_custom_call" | custom-call | flops 8000000000 | bytes 4194304 | tf_op jit(solution)/shard_map/attention_weights/pallas_call | solution.py:312
  58.1 0.0 all-to-all-done.all_hbm
  58.1 0.9 copy-done.2
  59.1 16.8 %score_and_edges.1 = (bf16[512,1024]{1,0:T(8,128)(2,1)}, bf16[512,1024]{1,0:T(8,128)(2,1)}, bf16[16,8,32,128]{3,2,1,0:T(8,128)(2,1)}, bf16[16,8,32,128]{3,2,1,0:...) custom-call(s32[64]{0:T(128)} %points_ref.5, ...), custom_call_target="tpu_custom_call" | custom-call | flops 15000000512 | bytes 4194304 | tf_op jit(solution)/shard_map/score_and_edges/pallas_call | solution.py:519
  75.9 0.1 collective-permute-start.4
  76.0 2.4 %collective-permute-start.2 = (bf16[2,256,1024]{2,1,0:T(8,128)(2,1)}, bf16[2,256,1024]{2,1,0:T(8,128)(2,1)S(1)}, u32[]{:S(2)}, u32[]{:S(2)}) collective-permute-start(bf16[2,256,1024]{2,1,0:T(8,128)(2,1)} %get-tuple-element.46), channel_id=1, source_target_pairs={{0,1},{1,2},{2,3},{3,4},{4,5},{5,6},{6,7},{7,8},{8,9},{9,10},{10,1... | collective-permute-start | bytes 3145736 | tf_op jit(solution)/shard_map/ppermute | solution.py:639
  78.4 5.3 %collective-permute-start.3 = (bf16[2,256,1024]{2,1,0:T(8,128)(2,1)}, bf16[2,256,1024]{2,1,0:T(8,128)(2,1)S(1)}, u32[]{:S(2)}, u32[]{:S(2)}) collective-permute-start(bf16[2,256,1024]{2,1,0:T(8,128)(2,1)} %get-tuple-element.47), channel_id=1, source_target_pairs={{1,0},{2,1},{3,2},{4,3},{5,4},{6,5},{7,6},{8,7},{9,8},{10,9},{11,1... | collective-permute-start | bytes 3145736 | tf_op jit(solution)/shard_map/ppermute | solution.py:640
  83.7 2.5 %add_convert_fusion = bf16[16,8,32,128]{3,2,1,0:T(8,128)(2,1)} fusion(bf16[16,8,32,128]{3,2,1,0:T(8,128)(2,1)S(1)} %collective-permute-done.4, bf16[16,8,32,128]{3,2,1,0:T(8,128)(2,1)} %get-tuple-element.51), kind=kLoop, calls=%fused_computation.1 | loop fusion | flops 2097152 | bytes 3145728 | tf_op jit(solution)/shard_map/convert_element_type | solution.py:646
  86.2 6.6 %all-to-all-start.1 = ((bf16[128,32,128]{2,1,0:T(8,128)(2,1)}), bf16[128,32,128]{2,1,0:T(8,128)(2,1)S(1)}, u32[]{:S(2)}, u32[]{:S(2)}) async-start(bf16[128,32,128]{2,1,0:T(8,128)(2,1)} %bitcast.7), calls=%async_computation.1 | async-start | bytes 2097152 | tf_op jit(solution)/shard_map/all_to_all | solution.py:647
  92.8 15.5 %own_backward.1 = (bf16[512,1024]{1,0:T(8,128)(2,1)}, bf16[512,1024]{1,0:T(8,128)(2,1)}, bf16[512,1024]{1,0:T(8,128)(2,1)}) custom-call(bf16[512,1024]{1,0:T(8,128)(2,1)} %get-tuple-element.28.q_hbm.q_ref, bf16[1024,1024]{1,0:T(8,128)(2,1)} %get-tuple-element.33.ke_ref.ke_hbm.ka_ref.kb_ref, bf16[1024,1024]{1,0:T(8,128)(2,1)} %get-tuple-element.33.ke_ref.ke_hbm.ka_ref.kb_ref, ...), custom_call_target="tpu_custom_call" | custom-call | flops 15000000512 | bytes 4194304 | tf_op jit(solution)/shard_map/own_backward/pallas_call | solution.py:391
  108.3 0.0 collective-permute-done.2.before_hbm
  108.3 0.9 copy-done
  109.3 0.3 copy-done.1
  109.6 11.3 %finish.1 = f32[512,1024]{1,0:T(8,128)} custom-call(bf16[512,1024]{1,0:T(8,128)(2,1)} %bitcast.15, f32[1,1024]{1,0:T(1,128)} %bitcast.20, bf16[512,1024]{1,0:T(8,128)(2,1)} %get-tuple-element.28.q_hbm.q_ref, bf16[512,1024]{1,0:T(8,128)(2,1)} %get-tuple-element.32.rq_hbm, bf16[512,1024]{1,0:T(8,128)(2,1)} %get-tuple-element.44.dq_hbm, ...), custom_call_target="tpu_custom_call" | custom-call | tf_op jit(solution)/shard_map/finish/pallas_call | solution.py:599
  120.9 0.8 convert_reduce_fusion
  (9 shorter events, 0.0 us)
Async XLA Ops:
  1.9 15.6 %collective-permute-start.1 = (bf16[256,1024]{1,0:T(8,128)(2,1)S(1)}, bf16[256,1024]{1,0:T(8,128)(2,1)S(1)}, u32[]{:S(2)}, u32[]{:S(2)}) collective-permute-start(bf16[256,1024]{1,0:T(8,128)(2,1)S(1)} %get-tuple-element.53), channel_id=1, source_target_pairs={{1,0},{2,1},{3,2},{4,3},{5,4},{6,5},{7,6},{8,7},{9,8},{10,9},{11,1... | collective-permute-start | bytes 1572872 | tf_op jit(solution)/shard_map/ppermute | solution.py:627
  7.5 12.6 %collective-permute-start = (bf16[256,1024]{1,0:T(8,128)(2,1)S(1)}, bf16[256,1024]{1,0:T(8,128)(2,1)S(1)}, u32[]{:S(2)}, u32[]{:S(2)}) collective-permute-start(bf16[256,1024]{1,0:T(8,128)(2,1)S(1)} %get-tuple-element.54), channel_id=1, source_target_pairs={{0,1},{1,2},{2,3},{3,4},{4,5},{5,6},{6,7},{7,8},{8,9},{9,10},{10,1... | collective-permute-start | bytes 1572872 | tf_op jit(solution)/shard_map/ppermute | solution.py:626
  17.6 2.5 %copy-start.3 = (bf16[256,1024]{1,0:T(8,128)(2,1)}, bf16[256,1024]{1,0:T(8,128)(2,1)S(1)}, u32[]{:S(2)}) copy-start(bf16[256,1024]{1,0:T(8,128)(2,1)S(1)} %collective-permute-done.1.after_hbm) | copy-start | bytes 1572868
  20.1 0.8 copy-start.4
  39.7 18.4 %all-to-all-start = ((bf16[8,100,512]{2,1,0:T(8,128)(2,1)}), bf16[8,100,512]{2,1,0:T(8,128)(2,1)S(1)}, u32[]{:S(2)}, u32[]{:S(2)}) async-start(bf16[8,100,512]{2,1,0:T(8,128)(2,1)} %get-tuple-element.36), calls=%async_computation | async-start | bytes 1703936 | tf_op jit(solution)/shard_map/all_to_all | solution.py:633
  58.1 0.9 copy-start.2
  75.9 7.8 %collective-permute-start.4 = (bf16[16,8,32,128]{3,2,1,0:T(8,128)(2,1)}, bf16[16,8,32,128]{3,2,1,0:T(8,128)(2,1)S(1)}, u32[]{:S(2)}, u32[]{:S(2)}) collective-permute-start(bf16[16,8,32,128]{3,2,1,0:T(8,128)(2,1)} %get-tuple-element.52), channel_id=1, source_target_pairs={{0,1},{1,0},{2,3},{3,2},{4,5},{5,4},{6,7},{7,6},{8,9},{9,8},{10,11... | collective-permute-start | bytes 3145736 | tf_op jit(solution)/shard_map/ppermute | solution.py:638
  76.0 32.3 %collective-permute-start.2 = (bf16[2,256,1024]{2,1,0:T(8,128)(2,1)}, bf16[2,256,1024]{2,1,0:T(8,128)(2,1)S(1)}, u32[]{:S(2)}, u32[]{:S(2)}) collective-permute-start(bf16[2,256,1024]{2,1,0:T(8,128)(2,1)} %get-tuple-element.46), channel_id=1, source_target_pairs={{0,1},{1,2},{2,3},{3,4},{4,5},{5,6},{6,7},{7,8},{8,9},{9,10},{10,1... | collective-permute-start | bytes 3145736 | tf_op jit(solution)/shard_map/ppermute | solution.py:639
  78.4 29.9 %collective-permute-start.3 = (bf16[2,256,1024]{2,1,0:T(8,128)(2,1)}, bf16[2,256,1024]{2,1,0:T(8,128)(2,1)S(1)}, u32[]{:S(2)}, u32[]{:S(2)}) collective-permute-start(bf16[2,256,1024]{2,1,0:T(8,128)(2,1)} %get-tuple-element.47), channel_id=1, source_target_pairs={{1,0},{2,1},{3,2},{4,3},{5,4},{6,5},{7,6},{8,7},{9,8},{10,9},{11,1... | collective-permute-start | bytes 3145736 | tf_op jit(solution)/shard_map/ppermute | solution.py:640
  86.2 34.7 %all-to-all-start.1 = ((bf16[128,32,128]{2,1,0:T(8,128)(2,1)}), bf16[128,32,128]{2,1,0:T(8,128)(2,1)S(1)}, u32[]{:S(2)}, u32[]{:S(2)}) async-start(bf16[128,32,128]{2,1,0:T(8,128)(2,1)} %bitcast.7), calls=%async_computation.1 | async-start | bytes 2097152 | tf_op jit(solution)/shard_map/all_to_all | solution.py:647
  108.3 1.0 copy-start
  108.3 1.3 %copy-start.1 = (bf16[2,256,1024]{2,1,0:T(8,128)(2,1)}, bf16[2,256,1024]{2,1,0:T(8,128)(2,1)S(1)}, u32[]{:S(2)}) copy-start(bf16[2,256,1024]{2,1,0:T(8,128)(2,1)S(1)} %collective-permute-done.3.after_hbm) | copy-start | bytes 3145732

commit v4 on v3

--- a/solution.py
+++ b/solution.py
@@ -108,7 +108,7 @@
 
 
 def project(x, gain, wq, wk, wv):
-    shape = jax.ShapeDtypeStruct((ROWS, WIDTH), BF16)
+    shape = pltpu.HBM((ROWS, WIDTH), BF16)
     square = pltpu.VMEM((WIDTH, WIDTH), BF16)
     rows = pltpu.VMEM((ROWS, WIDTH), BF16)
     return pl.pallas_call(
@@ -253,8 +253,8 @@
     variables = wd.shape[0]
     square = pltpu.VMEM((WIDTH, WIDTH), BF16)
     rows = pltpu.VMEM((ROWS, WIDTH), BF16)
-    shape = jax.ShapeDtypeStruct((ROWS, WIDTH), BF16)
-    ext = jax.ShapeDtypeStruct((EXT, WIDTH), BF16)
+    shape = pltpu.HBM((ROWS, WIDTH), BF16)
+    ext = pltpu.HBM((EXT, WIDTH), BF16)
     return pl.pallas_call(
         front_kernel,
         in_specs=[pl.BlockSpec(memory_space=pltpu.SMEM)] + [HBM] * 9 + [WHOLE] * 3,
@@ -263,11 +263,11 @@
             ext,
             ext,
             shape,
-            jax.ShapeDtypeStruct((PAIRS, EXT, PAIR), BF16),
+            pltpu.HBM((PAIRS, EXT, PAIR), BF16),
             shape,
-            jax.ShapeDtypeStruct((ROWS, PAIR), F32),
-            jax.ShapeDtypeStruct((variables, ROWS), BF16),
-            jax.ShapeDtypeStruct((members, variables, ROWS), BF16),
+            pltpu.HBM((ROWS, PAIR), F32),
+            pltpu.HBM((variables, ROWS), BF16),
+            pltpu.HBM((members, variables, ROWS), BF16),
         ],
         scratch_shapes=[
             rows, square, square, rows,
@@ -322,8 +322,8 @@
             scratch_shapes=[pltpu.VMEM((EXT, 2 * PAIR), BF16)],
         ),
         out_shape=[
-            jax.ShapeDtypeStruct((PAIRS, 2, 256, 512), BF16),
-            jax.ShapeDtypeStruct((PAIRS, 2, 512, 512), BF16),
+            pltpu.HBM((PAIRS, 2, 256, 512), BF16),
+            pltpu.HBM((PAIRS, 2, 512, 512), BF16),
         ],
         compiler_params=params(56),
         cost_estimate=cost(8),
@@ -354,10 +354,17 @@
 
 def query_piece(keys, slope):
     turned = keys.T
-    piece = jnp.concatenate(
-        [dot(turned[:HEAD_DIM], slope[:, :256]), dot(turned[HEAD_DIM:], slope[:, 256:])], 0
-    )
-    return (piece * HEAD_DIM**-0.5).T
+    halves = []
+    for first in (0, 128):
+        piece = jnp.concatenate(
+            [
+                dot(turned[:HEAD_DIM], slope[:, first : first + 128]),
+                dot(turned[HEAD_DIM:], slope[:, first + 256 : first + 384]),
+            ],
+            0,
+        )
+        halves.append((piece * HEAD_DIM**-0.5).T)
+    return jnp.concatenate(halves, 0)
 
 
 def own_kernel(
@@ -387,7 +394,7 @@
     part = pl.BlockSpec((ROWS, PAIR), lambda h: (0, h))
     second = pl.BlockSpec((256, PAIR), lambda h: (1, h))
     third = pl.BlockSpec((256, PAIR), lambda h: (2, h))
-    shape = jax.ShapeDtypeStruct((ROWS, WIDTH), BF16)
+    shape = pltpu.HBM((ROWS, WIDTH), BF16)
     return pl.pallas_call(
         own_kernel,
         grid=(PAIRS,),
@@ -483,7 +490,7 @@
         )
 
     def pair_step(step, carry):
-        for pair in (step * 2, step * 2 + 1):
+        for pair in [step * 4 + place for place in range(4)]:
             columns = pl.ds(pl.multiple_of(pair * PAIR, PAIR), PAIR)
             for block in range(2):
                 rows = slice(block * 256, block * 256 + 256)
@@ -496,12 +503,12 @@
                 edges[block, 0, :, columns] = (dot(slope, queries) * (1.0 / LOG2E)).astype(BF16)
                 edges[block, 1, :, columns] = dot(weights, grads).astype(BF16)
                 dq[rows, columns] = query_piece(ke[block, :, columns], slope).astype(BF16)
-        for pair in (step * 2, step * 2 + 1):
+        for pair in [step * 4 + place for place in range(4)]:
             for block in range(2):
                 store(pair, block).start()
         return carry
 
-    lax.fori_loop(0, PAIRS // 2, pair_step, 0)
+    lax.fori_loop(0, PAIRS // 4, pair_step, 0)
     stores[4].start()
     for pair in range(PAIRS):
         for block in range(2):
@@ -513,9 +520,9 @@
     square = pltpu.VMEM((WIDTH, WIDTH), BF16)
     rows = pltpu.VMEM((ROWS, WIDTH), BF16)
     halves = pltpu.VMEM((2, 256, WIDTH), BF16)
-    shape = jax.ShapeDtypeStruct((ROWS, WIDTH), BF16)
-    edge = jax.ShapeDtypeStruct((2, 256, WIDTH), BF16)
-    term = jax.ShapeDtypeStruct((16, 8, 32, 128), BF16)
+    shape = pltpu.HBM((ROWS, WIDTH), BF16)
+    edge = pltpu.HBM((2, 256, WIDTH), BF16)
+    term = pltpu.HBM((16, 8, 32, 128), BF16)
     return pl.pallas_call(
         score_kernel,
         in_specs=[pl.BlockSpec(memory_space=pltpu.SMEM), WHOLE]
@@ -537,7 +544,7 @@
             pltpu.SemaphoreType.DMA((2, PAIRS)),
             pltpu.SemaphoreType.DMA((5,)),
         ],
-        compiler_params=params(56),
+        compiler_params=params(50),
         cost_estimate=cost(15),
         name="score_and_edges",
     )(live, own, everyone, target, z, r, gain, wd, wo, att, q, ke, ve, weights)
@@ -600,14 +607,14 @@
         final_kernel,
         in_specs=[HBM, WHOLE] + [HBM] * 13,
         out_specs=HBM,
-        out_shape=jax.ShapeDtypeStruct((ROWS, WIDTH), F32),
+        out_shape=pltpu.HBM((ROWS, WIDTH), F32),
         scratch_shapes=[
             rows, rows, rows, rows, square, rows, edge, edge, square, rows, rows, rows, square, rows,
             pltpu.VMEM((ROWS, WIDTH), F32),
             pltpu.SemaphoreType.DMA((14,)),
             pltpu.SemaphoreType.DMA((2,)),
         ],
-        compiler_params=params(56),
+        compiler_params=params(53),
         name="finish",
     )(x, gain, q, rq, dq, wq, dv, before, after, wv, dk, k, rk, wk, lg)
 

time: 124 us -> 122 us (0.984)
  Pallas kernels: 81.7 us -> 80.1 us
    unnamed x10 -> x26, local copies, waits for them, and re-layouts: 3.05 us -> 3.08 us
where the time goes in v4:
time: 122 us; the launch traced here: 120 us
  Pallas kernels  80.1 us (66%)
  starting transfers between devices  29.1 us (24%)
  local copies, waits for them, and re-layouts  4.35 us (4%)
  other arithmetic  3.31 us (3%)
  waiting for transfers between devices  2.52 us (2%)
    pallas_call x1, Pallas kernels, front(): pl.pallas_call(front_kernel, in_specs=[pl.BlockSpec(memory_space=pltpu.SM...  18.7 us
    pallas_call x1, Pallas kernels, score(): pl.pallas_call(score_kernel, in_specs=[pl.BlockSpec(memory_space=pltpu.SM...  16 us
    pallas_call x1, Pallas kernels, own_backward(): pl.pallas_call(own_kernel, grid=(PAIRS,), in_specs=[part, second, third,...  15.3 us
    pallas_call x1, Pallas kernels, attention_weights(): pl.pallas_call(weights_kernel, grid_spec=pltpu.PrefetchScalarGridSpec(num...  11.3 us
    pallas_call x1, Pallas kernels, finish(): pl.pallas_call(final_kernel, in_specs=[HBM, WHOLE] + [HBM] * 13, out_spec...  10.6 us
    pallas_call x1, Pallas kernels, project(): pl.pallas_call(project_kernel, in_specs=[HBM, WHOLE, HBM, HBM, HBM], out_...  8.15 us
    all_to_all x1, starting transfers between devices, body(): everyone = lax.all_to_all(copies, 'member', 0, 0, tiled=True)  7.28 us
    all_to_all x1, starting transfers between devices, body(): lax.all_to_all(blocks.reshape(128, 32, 128), ('chip', 'core', 'member'),...  6.57 us
  transfers between devices with their start and end apart: 7, of which 1 were waited for; matrix products, arithmetic and copies ran while one was open for 2% of the time, Pallas kernels for 38%

profile of v4, /device:TPU:24, one launch (start us, length us, event | category | flops | bytes accessed | tf_op | source)
XLA Modules:
  0.0 120.2 jit_solution(10599405341692984865)
XLA Ops:
  0.6 1.3 %slice_bitcast_fusion = (bf16[256,1024]{1,0:T(8,128)(2,1)S(1)}, bf16[256,1024]{1,0:T(8,128)(2,1)S(1)}) fusion(bf16[1,512,1024]{2,1,0:T(8,128)(2,1)} %param.10), kind=kLoop, calls=%fused_computation.2 | loop fusion | bytes 2097152 | tf_op jit(solution)/shard_map/slice | solution.py:634
  1.9 5.6 %collective-permute-start.1 = (bf16[256,1024]{1,0:T(8,128)(2,1)S(1)}, bf16[256,1024]{1,0:T(8,128)(2,1)S(1)}, u32[]{:S(2)}, u32[]{:S(2)}) collective-permute-start(bf16[256,1024]{1,0:T(8,128)(2,1)S(1)} %get-tuple-element.53), channel_id=1, source_target_pairs={{1,0},{2,1},{3,2},{4,3},{5,4},{6,5},{7,6},{8,7},{9,8},{10,9},{11,1... | collective-permute-start | bytes 1572872 | tf_op jit(solution)/shard_map/ppermute | solution.py:634
  7.5 1.9 %collective-permute-start = (bf16[256,1024]{1,0:T(8,128)(2,1)S(1)}, bf16[256,1024]{1,0:T(8,128)(2,1)S(1)}, u32[]{:S(2)}, u32[]{:S(2)}) collective-permute-start(bf16[256,1024]{1,0:T(8,128)(2,1)S(1)} %get-tuple-element.54), channel_id=1, source_target_pairs={{0,1},{1,2},{2,3},{3,4},{4,5},{5,6},{6,7},{7,8},{8,9},{9,10},{10,1... | collective-permute-start | bytes 1572872 | tf_op jit(solution)/shard_map/ppermute | solution.py:633
  9.4 8.2 %project_own.1 = (bf16[512,1024]{1,0:T(8,128)(2,1)}, bf16[512,1024]{1,0:T(8,128)(2,1)}, bf16[512,1024]{1,0:T(8,128)(2,1)}, bf16[512,1024]{1,0:T(8,128)(2,1)}, bf16[512,1024]{1,0:T(8,128)(2,1)}) custom-call(bf16[512,1024]{1,0:T(8,128)(2,1)} %bitcast.19, f32[1,1024]{1,0:T(1,128)} %bitcast.13, bf16[1024,1024]{1,0:T(8,128)(2,1)} %wq_hbm.3, ...), custom_call_target="tpu_custom_call" | custom-call | tf_op jit(solution)/shard_map/project_own/pallas_call | solution.py:114
  17.6 2.5 %collective-permute-done.before_hbm = bf16[256,1024]{1,0:T(8,128)(2,1)S(1)} collective-permute-done((bf16[256,1024]{1,0:T(8,128)(2,1)S(1)}, bf16[256,1024]{1,0:T(8,128)(2,1)S(1)}, u32[]{:S(2)}, u32[]{:S(2)}) %collective-permute-start) | collective-permute-done | bytes 524320 | tf_op jit(solution)/shard_map/ppermute | solution.py:633
  20.1 0.8 copy-done.12
  20.9 18.7 %halo_attention_decode.1 = (bf16[1024,1024]{1,0:T(8,128)(2,1)}, bf16[1024,1024]{1,0:T(8,128)(2,1)}, bf16[512,1024]{1,0:T(8,128)(2,1)}, bf16[8,1024,128]{2,1,0:T(...) custom-call(s32[64]{0:T(128)} %points_ref.5, ...), custom_call_target="tpu_custom_call" | custom-call | tf_op jit(solution)/shard_map/halo_attention_decode/pallas_call | solution.py:258
  39.6 7.3 %all-to-all-start = ((bf16[8,100,512]{2,1,0:T(8,128)(2,1)}), bf16[8,100,512]{2,1,0:T(8,128)(2,1)S(1)}, u32[]{:S(2)}, u32[]{:S(2)}) async-start(bf16[8,100,512]{2,1,0:T(8,128)(2,1)} %get-tuple-element.36), calls=%async_computation | async-start | bytes 1703936 | tf_op jit(solution)/shard_map/all_to_all | solution.py:640
  47.0 0.0 copy-start.8
  47.0 11.3 %attention_weights.1 = (bf16[8,2,256,512]{3,2,1,0:T(8,128)(2,1)}, bf16[8,2,512,512]{3,2,1,0:T(8,128)(2,1)}) custom-call(s32[64]{0:T(128)} %points_ref.5, bf16[512,1024]{1,0:T(8,128)(2,1)} %get-tuple-element.28.q_hbm.q_ref, bf16[1024,1024]{1,0:T(8,128)(2,1)} %get-tuple-element.33.ke_ref.ke_hbm.ka_ref.kb_ref, bf16[8,1024,128]{2,1,0:T(8,128)(2,1)} %get-tuple-element.39.eq_ref), custom_call_target="tpu_custom_call" | custom-call | flops 8000000000 | bytes 4194304 | tf_op jit(solution)/shard_map/attention_weights/pallas_call | solution.py:312
  58.4 0.0 copy-start.7
  58.4 0.9 copy-done.7
  59.3 16.0 %score_and_edges.1 = (bf16[512,1024]{1,0:T(8,128)(2,1)}, bf16[512,1024]{1,0:T(8,128)(2,1)}, bf16[16,8,32,128]{3,2,1,0:T(8,128)(2,1)}, bf16[16,8,32,128]{3,2,1,0:...) custom-call(s32[64]{0:T(128)S(1)} %copy-done.3, ...), custom_call_target="tpu_custom_call" | custom-call | flops 15000000512 | bytes 4194304 | tf_op jit(solution)/shard_map/score_and_edges/pallas_call | solution.py:526
  75.3 0.1 collective-permute-start.4
  75.4 2.4 %collective-permute-start.2 = (bf16[2,256,1024]{2,1,0:T(8,128)(2,1)}, bf16[2,256,1024]{2,1,0:T(8,128)(2,1)S(1)}, u32[]{:S(2)}, u32[]{:S(2)}) collective-permute-start(bf16[2,256,1024]{2,1,0:T(8,128)(2,1)} %get-tuple-element.46), channel_id=1, source_target_pairs={{0,1},{1,2},{2,3},{3,4},{4,5},{5,6},{6,7},{7,8},{8,9},{9,10},{10,1... | collective-permute-start | bytes 3145736 | tf_op jit(solution)/shard_map/ppermute | solution.py:646
  77.8 5.3 %collective-permute-start.3 = (bf16[2,256,1024]{2,1,0:T(8,128)(2,1)}, bf16[2,256,1024]{2,1,0:T(8,128)(2,1)S(1)}, u32[]{:S(2)}, u32[]{:S(2)}) collective-permute-start(bf16[2,256,1024]{2,1,0:T(8,128)(2,1)} %get-tuple-element.47), channel_id=1, source_target_pairs={{1,0},{2,1},{3,2},{4,3},{5,4},{6,5},{7,6},{8,7},{9,8},{10,9},{11,1... | collective-permute-start | bytes 3145736 | tf_op jit(solution)/shard_map/ppermute | solution.py:647
  83.1 2.5 %add_convert_fusion = bf16[16,8,32,128]{3,2,1,0:T(8,128)(2,1)} fusion(bf16[16,8,32,128]{3,2,1,0:T(8,128)(2,1)S(1)} %collective-permute-done.4, bf16[16,8,32,128]{3,2,1,0:T(8,128)(2,1)} %get-tuple-element.51), kind=kLoop, calls=%fused_computation.1 | loop fusion | flops 2097152 | bytes 3145728 | tf_op jit(solution)/shard_map/convert_element_type | solution.py:653
  85.6 6.6 %all-to-all-start.1 = ((bf16[128,32,128]{2,1,0:T(8,128)(2,1)}), bf16[128,32,128]{2,1,0:T(8,128)(2,1)S(1)}, u32[]{:S(2)}, u32[]{:S(2)}) async-start(bf16[128,32,128]{2,1,0:T(8,128)(2,1)} %bitcast.7), calls=%async_computation.1 | async-start | bytes 2097152 | tf_op jit(solution)/shard_map/all_to_all | solution.py:654
  92.2 0.0 copy-start.1
  92.2 15.3 %own_backward.1 = (bf16[512,1024]{1,0:T(8,128)(2,1)}, bf16[512,1024]{1,0:T(8,128)(2,1)}, bf16[512,1024]{1,0:T(8,128)(2,1)}) custom-call(bf16[512,1024]{1,0:T(8,128)(2,1)} %get-tuple-element.28.q_hbm.q_ref, bf16[1024,1024]{1,0:T(8,128)(2,1)} %get-tuple-element.33.ke_ref.ke_hbm.ka_ref.kb_ref, bf16[1024,1024]{1,0:T(8,128)(2,1)} %get-tuple-element.33.ke_ref.ke_hbm.ka_ref.kb_ref, ...), custom_call_target="tpu_custom_call" | custom-call | flops 15000000512 | bytes 4194304 | tf_op jit(solution)/shard_map/own_backward/pallas_call | solution.py:398
  107.5 1.0 copy-done.9
  108.5 0.3 copy-done.10
  108.8 10.6 %finish.1 = f32[512,1024]{1,0:T(8,128)} custom-call(bf16[512,1024]{1,0:T(8,128)(2,1)} %bitcast.21, f32[1,1024]{1,0:T(1,128)S(1)} %bitcast.15, bf16[512,1024]{1,0:T(8,128)(2,1)} %get-tuple-element.28.q_hbm.q_ref, bf16[512,1024]{1,0:T(8,128)(2,1)} %get-tuple-element.32.rq_hbm, bf16[512,1024]{1,0:T(8,128)(2,1)} %get-tuple-element.44.dq_hbm, ...), custom_call_target="tpu_custom_call" | custom-call | tf_op jit(solution)/shard_map/finish/pallas_call | solution.py:606
  119.4 0.8 convert_reduce_fusion
  (25 shorter events, 0.1 us)
Async XLA Ops:
  1.9 15.7 %collective-permute-start.1 = (bf16[256,1024]{1,0:T(8,128)(2,1)S(1)}, bf16[256,1024]{1,0:T(8,128)(2,1)S(1)}, u32[]{:S(2)}, u32[]{:S(2)}) collective-permute-start(bf16[256,1024]{1,0:T(8,128)(2,1)S(1)} %get-tuple-element.53), channel_id=1, source_target_pairs={{1,0},{2,1},{3,2},{4,3},{5,4},{6,5},{7,6},{8,7},{9,8},{10,9},{11,1... | collective-permute-start | bytes 1572872 | tf_op jit(solution)/shard_map/ppermute | solution.py:634
  7.5 12.6 %collective-permute-start = (bf16[256,1024]{1,0:T(8,128)(2,1)S(1)}, bf16[256,1024]{1,0:T(8,128)(2,1)S(1)}, u32[]{:S(2)}, u32[]{:S(2)}) collective-permute-start(bf16[256,1024]{1,0:T(8,128)(2,1)S(1)} %get-tuple-element.54), channel_id=1, source_target_pairs={{0,1},{1,2},{2,3},{3,4},{4,5},{5,6},{6,7},{7,8},{8,9},{9,10},{10,1... | collective-permute-start | bytes 1572872 | tf_op jit(solution)/shard_map/ppermute | solution.py:633
  17.6 2.5 %copy-start.11 = (bf16[256,1024]{1,0:T(8,128)(2,1)}, bf16[256,1024]{1,0:T(8,128)(2,1)S(1)}, u32[]{:S(2)}) copy-start(bf16[256,1024]{1,0:T(8,128)(2,1)S(1)} %collective-permute-done.1.after_hbm) | copy-start | bytes 1572868
  20.1 0.8 copy-start.12
  39.6 18.7 %all-to-all-start = ((bf16[8,100,512]{2,1,0:T(8,128)(2,1)}), bf16[8,100,512]{2,1,0:T(8,128)(2,1)S(1)}, u32[]{:S(2)}, u32[]{:S(2)}) async-start(bf16[8,100,512]{2,1,0:T(8,128)(2,1)} %get-tuple-element.36), calls=%async_computation | async-start | bytes 1703936 | tf_op jit(solution)/shard_map/all_to_all | solution.py:640
  46.9 11.4 %copy-start = (bf16[100,1024]{1,0:T(8,128)(2,1)S(1)}, bf16[100,1024]{1,0:T(8,128)(2,1)}, u32[]{:S(2)}) copy-start(bf16[100,1024]{1,0:T(8,128)(2,1)} %wd_ref.3) | copy-start | bytes 614404
  46.9 11.4 %copy-start.2 = (f32[1024]{0:T(1024)S(1)}, f32[1024]{0:T(1024)}, u32[]{:S(2)}) copy-start(f32[1024]{0:T(1024)} %param.17) | copy-start | bytes 12292
  46.9 11.4 %copy-start.3 = (s32[64]{0:T(128)S(1)}, s32[64]{0:T(128)}, u32[]{:S(2)}) copy-start(s32[64]{0:T(128)} %points_ref.5) | copy-start | bytes 772
  46.9 11.4 %copy-start.4 = (bf16[512,1024]{1,0:T(8,128)(2,1)S(1)}, bf16[512,1024]{1,0:T(8,128)(2,1)}, u32[]{:S(2)}) copy-start(bf16[512,1024]{1,0:T(8,128)(2,1)} %get-tuple-element.35.att_hbm.att_ref) | copy-start | bytes 3145732
  46.9 11.4 %copy-start.5 = (bf16[512,1024]{1,0:T(8,128)(2,1)S(1)}, bf16[512,1024]{1,0:T(8,128)(2,1)}, u32[]{:S(2)}) copy-start(bf16[512,1024]{1,0:T(8,128)(2,1)} %get-tuple-element.37.z_hbm) | copy-start | bytes 3145732
  46.9 11.4 %copy-start.6 = (f32[512,128]{1,0:T(8,128)S(1)}, f32[512,128]{1,0:T(8,128)}, u32[]{:S(2)}) copy-start(f32[512,128]{1,0:T(8,128)} %get-tuple-element.38.r_hbm) | copy-start | bytes 786436
  47.0 11.4 %copy-start.8 = (bf16[100,512]{1,0:T(8,128)(2,1)S(1)}, bf16[100,512]{1,0:T(8,128)(2,1)}, u32[]{:S(2)}) copy-start(bf16[100,512]{1,0:T(8,128)(2,1)} %get-tuple-element.31.own_ref) | copy-start | bytes 307204
  58.4 0.9 copy-start.7
  75.3 7.8 %collective-permute-start.4 = (bf16[16,8,32,128]{3,2,1,0:T(8,128)(2,1)}, bf16[16,8,32,128]{3,2,1,0:T(8,128)(2,1)S(1)}, u32[]{:S(2)}, u32[]{:S(2)}) collective-permute-start(bf16[16,8,32,128]{3,2,1,0:T(8,128)(2,1)} %get-tuple-element.52), channel_id=1, source_target_pairs={{0,1},{1,0},{2,3},{3,2},{4,5},{5,4},{6,7},{7,6},{8,9},{9,8},{10,11... | collective-permute-start | bytes 3145736 | tf_op jit(solution)/shard_map/ppermute | solution.py:645
  75.4 32.1 %collective-permute-start.2 = (bf16[2,256,1024]{2,1,0:T(8,128)(2,1)}, bf16[2,256,1024]{2,1,0:T(8,128)(2,1)S(1)}, u32[]{:S(2)}, u32[]{:S(2)}) collective-permute-start(bf16[2,256,1024]{2,1,0:T(8,128)(2,1)} %get-tuple-element.46), channel_id=1, source_target_pairs={{0,1},{1,2},{2,3},{3,4},{4,5},{5,6},{6,7},{7,8},{8,9},{9,10},{10,1... | collective-permute-start | bytes 3145736 | tf_op jit(solution)/shard_map/ppermute | solution.py:646
  77.8 29.7 %collective-permute-start.3 = (bf16[2,256,1024]{2,1,0:T(8,128)(2,1)}, bf16[2,256,1024]{2,1,0:T(8,128)(2,1)S(1)}, u32[]{:S(2)}, u32[]{:S(2)}) collective-permute-start(bf16[2,256,1024]{2,1,0:T(8,128)(2,1)} %get-tuple-element.47), channel_id=1, source_target_pairs={{1,0},{2,1},{3,2},{4,3},{5,4},{6,5},{7,6},{8,7},{9,8},{10,9},{11,1... | collective-permute-start | bytes 3145736 | tf_op jit(solution)/shard_map/ppermute | solution.py:647
  85.6 33.8 %all-to-all-start.1 = ((bf16[128,32,128]{2,1,0:T(8,128)(2,1)}), bf16[128,32,128]{2,1,0:T(8,128)(2,1)S(1)}, u32[]{:S(2)}, u32[]{:S(2)}) async-start(bf16[128,32,128]{2,1,0:T(8,128)(2,1)} %bitcast.7), calls=%async_computation.1 | async-start | bytes 2097152 | tf_op jit(solution)/shard_map/all_to_all | solution.py:654
  92.2 16.7 %copy-start.1 = (f32[1024]{0:T(1024)S(1)}, f32[1024]{0:T(1024)}, u32[]{:S(2)}) copy-start(f32[1024]{0:T(1024)} %param.12) | copy-start | bytes 12292
  107.5 1.0 copy-start.9
  107.5 1.3 %copy-start.10 = (bf16[2,256,1024]{2,1,0:T(8,128)(2,1)}, bf16[2,256,1024]{2,1,0:T(8,128)(2,1)S(1)}, u32[]{:S(2)}) copy-start(bf16[2,256,1024]{2,1,0:T(8,128)(2,1)S(1)} %collective-permute-done.3.after_hbm) | copy-start | bytes 3145732

commit v5 on v4

--- a/solution.py
+++ b/solution.py
@@ -367,8 +367,8 @@
     return jnp.concatenate(halves, 0)
 
 
-def own_kernel(
-    q_ref, ka_ref, kb_ref, va_ref, vb_ref, att_ref, da_ref, w_ref, part_ref, dq_ref, dk_ref, dv_ref
+def own_pair(
+    q_ref, ka_ref, kb_ref, va_ref, vb_ref, att_ref, da_ref, w_ref, part_ref, dq_ref, dk_ref, dv_ref, side
 ):
     low = lane((256, PAIR)) < HEAD_DIM
     values = jnp.concatenate([va_ref[...], vb_ref[...]], 0)
@@ -378,9 +378,9 @@
     for block in range(2):
         rows = slice(block * 256, block * 256 + 256)
         operands.append(slope_operands(q_ref[rows], att_ref[rows], da_ref[rows], low))
-        slope = w_ref[0, block].astype(F32) * dot_t(values, operands[block][2])
+        slope = w_ref[side, block].astype(F32) * dot_t(values, operands[block][2])
         slopes.append(slope.astype(BF16))
-    weights = jnp.concatenate([w_ref[0, 0], w_ref[0, 1]], 1)
+    weights = jnp.concatenate([w_ref[side, 0], w_ref[side, 1]], 1)
     dv_ref[...] = dot(weights, jnp.concatenate([operands[0][1], operands[1][1]], 0)).astype(BF16)
     dk = dot(jnp.concatenate(slopes, 1), jnp.concatenate([operands[0][0], operands[1][0]], 0))
     dk_ref[...] = (dk * (1.0 / LOG2E)).astype(BF16)
@@ -390,16 +390,22 @@
         dq_ref[rows] = (part_ref[rows].astype(F32) + piece).astype(BF16)
 
 
+def own_kernel(*refs):
+    for side in range(2):
+        columns = slice(side * PAIR, side * PAIR + PAIR)
+        own_pair(*(ref if place == 7 else ref.at[:, columns] for place, ref in enumerate(refs)), side)
+
+
 def own_backward(q, ke, ve, att, da, weights, dq):
-    part = pl.BlockSpec((ROWS, PAIR), lambda h: (0, h))
-    second = pl.BlockSpec((256, PAIR), lambda h: (1, h))
-    third = pl.BlockSpec((256, PAIR), lambda h: (2, h))
+    part = pl.BlockSpec((ROWS, 2 * PAIR), lambda h: (0, h))
+    second = pl.BlockSpec((256, 2 * PAIR), lambda h: (1, h))
+    third = pl.BlockSpec((256, 2 * PAIR), lambda h: (2, h))
     shape = pltpu.HBM((ROWS, WIDTH), BF16)
     return pl.pallas_call(
         own_kernel,
-        grid=(PAIRS,),
+        grid=(PAIRS // 2,),
         in_specs=[part, second, third, second, third, part, part]
-        + [pl.BlockSpec((1, 2, 512, 512), lambda h: (h, 0, 0, 0)), part],
+        + [pl.BlockSpec((2, 2, 512, 512), lambda h: (h, 0, 0, 0)), part],
         out_specs=[part] * 3,
         out_shape=[shape] * 3,
         compiler_params=params(56),

time: 122 us -> 121 us (level)
  transfers between devices with their start and end apart: 7 -> 7, of which waited for: 1 -> 1; matrix products, arithmetic and copies ran while one was open for 2% -> 2% of each run, Pallas kernels for 38% -> 37%
where the time goes in v5:
time: 121 us; the launch traced here: 120 us
  Pallas kernels  79.4 us (66%)
  starting transfers between devices  29.1 us (24%)
  local copies, waits for them, and re-layouts  4.35 us (4%)
  other arithmetic  3.31 us (3%)
  waiting for transfers between devices  2.52 us (2%)
    pallas_call x1, Pallas kernels, front(): pl.pallas_call(front_kernel, in_specs=[pl.BlockSpec(memory_space=pltpu.SM...  18.7 us
    pallas_call x1, Pallas kernels, score(): pl.pallas_call(score_kernel, in_specs=[pl.BlockSpec(memory_space=pltpu.SM...  16 us
    pallas_call x1, Pallas kernels, own_backward(): pl.pallas_call(own_kernel, grid=(PAIRS // 2,), in_specs=[part, second, th...  14.7 us
    pallas_call x1, Pallas kernels, attention_weights(): pl.pallas_call(weights_kernel, grid_spec=pltpu.PrefetchScalarGridSpec(num...  11.3 us
    pallas_call x1, Pallas kernels, finish(): pl.pallas_call(final_kernel, in_specs=[HBM, WHOLE] + [HBM] * 13, out_spec...  10.6 us
    pallas_call x1, Pallas kernels, project(): pl.pallas_call(project_kernel, in_specs=[HBM, WHOLE, HBM, HBM, HBM], out_...  8.15 us
    all_to_all x1, starting transfers between devices, body(): everyone = lax.all_to_all(copies, 'member', 0, 0, tiled=True)  7.28 us
    all_to_all x1, starting transfers between devices, body(): lax.all_to_all(blocks.reshape(128, 32, 128), ('chip', 'core', 'member'),...  6.57 us
  transfers between devices with their start and end apart: 7, of which 1 were waited for; matrix products, arithmetic and copies ran while one was open for 2% of the time, Pallas kernels for 37%

profile of v5, /device:TPU:24, one launch (start us, length us, event | category | flops | bytes accessed | tf_op | source)
XLA Modules:
  0.0 119.6 jit_solution(13335759208529675532)
XLA Ops:
  0.6 1.3 %slice_bitcast_fusion = (bf16[256,1024]{1,0:T(8,128)(2,1)S(1)}, bf16[256,1024]{1,0:T(8,128)(2,1)S(1)}) fusion(bf16[1,512,1024]{2,1,0:T(8,128)(2,1)} %param.10), kind=kLoop, calls=%fused_computation.2 | loop fusion | bytes 2097152 | tf_op jit(solution)/shard_map/slice | solution.py:640
  1.9 5.6 %collective-permute-start.1 = (bf16[256,1024]{1,0:T(8,128)(2,1)S(1)}, bf16[256,1024]{1,0:T(8,128)(2,1)S(1)}, u32[]{:S(2)}, u32[]{:S(2)}) collective-permute-start(bf16[256,1024]{1,0:T(8,128)(2,1)S(1)} %get-tuple-element.53), channel_id=1, source_target_pairs={{1,0},{2,1},{3,2},{4,3},{5,4},{6,5},{7,6},{8,7},{9,8},{10,9},{11,1... | collective-permute-start | bytes 1572872 | tf_op jit(solution)/shard_map/ppermute | solution.py:640
  7.5 1.9 %collective-permute-start = (bf16[256,1024]{1,0:T(8,128)(2,1)S(1)}, bf16[256,1024]{1,0:T(8,128)(2,1)S(1)}, u32[]{:S(2)}, u32[]{:S(2)}) collective-permute-start(bf16[256,1024]{1,0:T(8,128)(2,1)S(1)} %get-tuple-element.54), channel_id=1, source_target_pairs={{0,1},{1,2},{2,3},{3,4},{4,5},{5,6},{6,7},{7,8},{8,9},{9,10},{10,1... | collective-permute-start | bytes 1572872 | tf_op jit(solution)/shard_map/ppermute | solution.py:639
  9.4 8.2 %project_own.1 = (bf16[512,1024]{1,0:T(8,128)(2,1)}, bf16[512,1024]{1,0:T(8,128)(2,1)}, bf16[512,1024]{1,0:T(8,128)(2,1)}, bf16[512,1024]{1,0:T(8,128)(2,1)}, bf16[512,1024]{1,0:T(8,128)(2,1)}) custom-call(bf16[512,1024]{1,0:T(8,128)(2,1)} %bitcast.19, f32[1,1024]{1,0:T(1,128)} %bitcast.13, bf16[1024,1024]{1,0:T(8,128)(2,1)} %wq_hbm.3, ...), custom_call_target="tpu_custom_call" | custom-call | tf_op jit(solution)/shard_map/project_own/pallas_call | solution.py:114
  17.6 2.5 %collective-permute-done.before_hbm = bf16[256,1024]{1,0:T(8,128)(2,1)S(1)} collective-permute-done((bf16[256,1024]{1,0:T(8,128)(2,1)S(1)}, bf16[256,1024]{1,0:T(8,128)(2,1)S(1)}, u32[]{:S(2)}, u32[]{:S(2)}) %collective-permute-start) | collective-permute-done | bytes 524320 | tf_op jit(solution)/shard_map/ppermute | solution.py:639
  20.1 0.8 copy-done.12
  20.9 18.7 %halo_attention_decode.1 = (bf16[1024,1024]{1,0:T(8,128)(2,1)}, bf16[1024,1024]{1,0:T(8,128)(2,1)}, bf16[512,1024]{1,0:T(8,128)(2,1)}, bf16[8,1024,128]{2,1,0:T(...) custom-call(s32[64]{0:T(128)} %points_ref.5, ...), custom_call_target="tpu_custom_call" | custom-call | tf_op jit(solution)/shard_map/halo_attention_decode/pallas_call | solution.py:258
  39.6 7.3 %all-to-all-start = ((bf16[8,100,512]{2,1,0:T(8,128)(2,1)}), bf16[8,100,512]{2,1,0:T(8,128)(2,1)S(1)}, u32[]{:S(2)}, u32[]{:S(2)}) async-start(bf16[8,100,512]{2,1,0:T(8,128)(2,1)} %get-tuple-element.36), calls=%async_computation | async-start | bytes 1703936 | tf_op jit(solution)/shard_map/all_to_all | solution.py:646
  47.0 0.0 copy-start.8
  47.0 11.3 %attention_weights.1 = (bf16[8,2,256,512]{3,2,1,0:T(8,128)(2,1)}, bf16[8,2,512,512]{3,2,1,0:T(8,128)(2,1)}) custom-call(s32[64]{0:T(128)} %points_ref.5, bf16[512,1024]{1,0:T(8,128)(2,1)} %get-tuple-element.28.q_hbm.q_ref.refs_0_, bf16[1024,1024]{1,0:T(8,128)(2,1)} %get-tuple-element.33.ke_ref.ke_hbm.refs_1_.refs_2_, ...), custom_call_target="tpu_custom_call" | custom-call | flops 8000000000 | bytes 4194304 | tf_op jit(solution)/shard_map/attention_weights/pallas_call | solution.py:312
  58.4 0.0 copy-start.7
  58.4 0.9 copy-done.7
  59.3 16.0 %score_and_edges.1 = (bf16[512,1024]{1,0:T(8,128)(2,1)}, bf16[512,1024]{1,0:T(8,128)(2,1)}, bf16[16,8,32,128]{3,2,1,0:T(8,128)(2,1)}, bf16[16,8,32,128]{3,2,1,0:...) custom-call(s32[64]{0:T(128)S(1)} %copy-done.3, ...), custom_call_target="tpu_custom_call" | custom-call | flops 15000000512 | bytes 4194304 | tf_op jit(solution)/shard_map/score_and_edges/pallas_call | solution.py:532
  75.3 0.1 collective-permute-start.4
  75.4 2.4 %collective-permute-start.2 = (bf16[2,256,1024]{2,1,0:T(8,128)(2,1)}, bf16[2,256,1024]{2,1,0:T(8,128)(2,1)S(1)}, u32[]{:S(2)}, u32[]{:S(2)}) collective-permute-start(bf16[2,256,1024]{2,1,0:T(8,128)(2,1)} %get-tuple-element.46), channel_id=1, source_target_pairs={{0,1},{1,2},{2,3},{3,4},{4,5},{5,6},{6,7},{7,8},{8,9},{9,10},{10,1... | collective-permute-start | bytes 3145736 | tf_op jit(solution)/shard_map/ppermute | solution.py:652
  77.8 5.3 %collective-permute-start.3 = (bf16[2,256,1024]{2,1,0:T(8,128)(2,1)}, bf16[2,256,1024]{2,1,0:T(8,128)(2,1)S(1)}, u32[]{:S(2)}, u32[]{:S(2)}) collective-permute-start(bf16[2,256,1024]{2,1,0:T(8,128)(2,1)} %get-tuple-element.47), channel_id=1, source_target_pairs={{1,0},{2,1},{3,2},{4,3},{5,4},{6,5},{7,6},{8,7},{9,8},{10,9},{11,1... | collective-permute-start | bytes 3145736 | tf_op jit(solution)/shard_map/ppermute | solution.py:653
  83.1 2.5 %add_convert_fusion = bf16[16,8,32,128]{3,2,1,0:T(8,128)(2,1)} fusion(bf16[16,8,32,128]{3,2,1,0:T(8,128)(2,1)S(1)} %collective-permute-done.4, bf16[16,8,32,128]{3,2,1,0:T(8,128)(2,1)} %get-tuple-element.51), kind=kLoop, calls=%fused_computation.1 | loop fusion | flops 2097152 | bytes 3145728 | tf_op jit(solution)/shard_map/convert_element_type | solution.py:659
  85.6 6.6 %all-to-all-start.1 = ((bf16[128,32,128]{2,1,0:T(8,128)(2,1)}), bf16[128,32,128]{2,1,0:T(8,128)(2,1)S(1)}, u32[]{:S(2)}, u32[]{:S(2)}) async-start(bf16[128,32,128]{2,1,0:T(8,128)(2,1)} %bitcast.7), calls=%async_computation.1 | async-start | bytes 2097152 | tf_op jit(solution)/shard_map/all_to_all | solution.py:660
  92.2 0.0 copy-start.1
  92.2 14.7 %own_backward.1 = (bf16[512,1024]{1,0:T(8,128)(2,1)}, bf16[512,1024]{1,0:T(8,128)(2,1)}, bf16[512,1024]{1,0:T(8,128)(2,1)}) custom-call(bf16[512,1024]{1,0:T(8,128)(2,1)} %get-tuple-element.28.q_hbm.q_ref.refs_0_, bf16[1024,1024]{1,0:T(8,128)(2,1)} %get-tuple-element.33.ke_ref.ke_hbm.refs_1_.refs_2_, ...), custom_call_target="tpu_custom_call" | custom-call | flops 15000000512 | bytes 4194304 | tf_op jit(solution)/shard_map/own_backward/pallas_call | solution.py:404
  106.9 1.0 copy-done.9
  107.9 0.3 copy-done.10
  108.2 10.6 %finish.1 = f32[512,1024]{1,0:T(8,128)} custom-call(bf16[512,1024]{1,0:T(8,128)(2,1)} %bitcast.21, f32[1,1024]{1,0:T(1,128)S(1)} %bitcast.15, bf16[512,1024]{1,0:T(8,128)(2,1)} %get-tuple-element.28.q_hbm.q_ref.refs_0_, bf16[512,1024]{1,0:T(8,128)(2,1)} %get-tuple-element.32.rq_hbm, bf16[512,1024]{1,0:T(8,128)(2,1)} %get-tuple-element.44.dq_hbm, ...), custom_call_target="tpu_custom_call" | custom-call | tf_op jit(solution)/shard_map/finish/pallas_call | solution.py:612
  118.8 0.8 convert_reduce_fusion
  (25 shorter events, 0.1 us)
Async XLA Ops:
  1.9 15.7 %collective-permute-start.1 = (bf16[256,1024]{1,0:T(8,128)(2,1)S(1)}, bf16[256,1024]{1,0:T(8,128)(2,1)S(1)}, u32[]{:S(2)}, u32[]{:S(2)}) collective-permute-start(bf16[256,1024]{1,0:T(8,128)(2,1)S(1)} %get-tuple-element.53), channel_id=1, source_target_pairs={{1,0},{2,1},{3,2},{4,3},{5,4},{6,5},{7,6},{8,7},{9,8},{10,9},{11,1... | collective-permute-start | bytes 1572872 | tf_op jit(solution)/shard_map/ppermute | solution.py:640
  7.5 12.6 %collective-permute-start = (bf16[256,1024]{1,0:T(8,128)(2,1)S(1)}, bf16[256,1024]{1,0:T(8,128)(2,1)S(1)}, u32[]{:S(2)}, u32[]{:S(2)}) collective-permute-start(bf16[256,1024]{1,0:T(8,128)(2,1)S(1)} %get-tuple-element.54), channel_id=1, source_target_pairs={{0,1},{1,2},{2,3},{3,4},{4,5},{5,6},{6,7},{7,8},{8,9},{9,10},{10,1... | collective-permute-start | bytes 1572872 | tf_op jit(solution)/shard_map/ppermute | solution.py:639
  17.6 2.5 %copy-start.11 = (bf16[256,1024]{1,0:T(8,128)(2,1)}, bf16[256,1024]{1,0:T(8,128)(2,1)S(1)}, u32[]{:S(2)}) copy-start(bf16[256,1024]{1,0:T(8,128)(2,1)S(1)} %collective-permute-done.1.after_hbm) | copy-start | bytes 1572868
  20.1 0.8 copy-start.12
  39.6 18.7 %all-to-all-start = ((bf16[8,100,512]{2,1,0:T(8,128)(2,1)}), bf16[8,100,512]{2,1,0:T(8,128)(2,1)S(1)}, u32[]{:S(2)}, u32[]{:S(2)}) async-start(bf16[8,100,512]{2,1,0:T(8,128)(2,1)} %get-tuple-element.36), calls=%async_computation | async-start | bytes 1703936 | tf_op jit(solution)/shard_map/all_to_all | solution.py:646
  46.9 11.4 %copy-start = (bf16[100,1024]{1,0:T(8,128)(2,1)S(1)}, bf16[100,1024]{1,0:T(8,128)(2,1)}, u32[]{:S(2)}) copy-start(bf16[100,1024]{1,0:T(8,128)(2,1)} %wd_ref.3) | copy-start | bytes 614404
  46.9 11.4 %copy-start.2 = (f32[1024]{0:T(1024)S(1)}, f32[1024]{0:T(1024)}, u32[]{:S(2)}) copy-start(f32[1024]{0:T(1024)} %param.17) | copy-start | bytes 12292
  46.9 11.4 %copy-start.3 = (s32[64]{0:T(128)S(1)}, s32[64]{0:T(128)}, u32[]{:S(2)}) copy-start(s32[64]{0:T(128)} %points_ref.5) | copy-start | bytes 772
  46.9 11.4 %copy-start.4 = (bf16[512,1024]{1,0:T(8,128)(2,1)S(1)}, bf16[512,1024]{1,0:T(8,128)(2,1)}, u32[]{:S(2)}) copy-start(bf16[512,1024]{1,0:T(8,128)(2,1)} %get-tuple-element.35.att_hbm.refs_5_) | copy-start | bytes 3145732
  46.9 11.4 %copy-start.5 = (bf16[512,1024]{1,0:T(8,128)(2,1)S(1)}, bf16[512,1024]{1,0:T(8,128)(2,1)}, u32[]{:S(2)}) copy-start(bf16[512,1024]{1,0:T(8,128)(2,1)} %get-tuple-element.37.z_hbm) | copy-start | bytes 3145732
  46.9 11.4 %copy-start.6 = (f32[512,128]{1,0:T(8,128)S(1)}, f32[512,128]{1,0:T(8,128)}, u32[]{:S(2)}) copy-start(f32[512,128]{1,0:T(8,128)} %get-tuple-element.38.r_hbm) | copy-start | bytes 786436
  47.0 11.4 %copy-start.8 = (bf16[100,512]{1,0:T(8,128)(2,1)S(1)}, bf16[100,512]{1,0:T(8,128)(2,1)}, u32[]{:S(2)}) copy-start(bf16[100,512]{1,0:T(8,128)(2,1)} %get-tuple-element.31.own_ref) | copy-start | bytes 307204
  58.4 0.9 copy-start.7
  75.3 7.8 %collective-permute-start.4 = (bf16[16,8,32,128]{3,2,1,0:T(8,128)(2,1)}, bf16[16,8,32,128]{3,2,1,0:T(8,128)(2,1)S(1)}, u32[]{:S(2)}, u32[]{:S(2)}) collective-permute-start(bf16[16,8,32,128]{3,2,1,0:T(8,128)(2,1)} %get-tuple-element.52), channel_id=1, source_target_pairs={{0,1},{1,0},{2,3},{3,2},{4,5},{5,4},{6,7},{7,6},{8,9},{9,8},{10,11... | collective-permute-start | bytes 3145736 | tf_op jit(solution)/shard_map/ppermute | solution.py:651
  75.4 31.5 %collective-permute-start.2 = (bf16[2,256,1024]{2,1,0:T(8,128)(2,1)}, bf16[2,256,1024]{2,1,0:T(8,128)(2,1)S(1)}, u32[]{:S(2)}, u32[]{:S(2)}) collective-permute-start(bf16[2,256,1024]{2,1,0:T(8,128)(2,1)} %get-tuple-element.46), channel_id=1, source_target_pairs={{0,1},{1,2},{2,3},{3,4},{4,5},{5,6},{6,7},{7,8},{8,9},{9,10},{10,1... | collective-permute-start | bytes 3145736 | tf_op jit(solution)/shard_map/ppermute | solution.py:652
  77.8 29.1 %collective-permute-start.3 = (bf16[2,256,1024]{2,1,0:T(8,128)(2,1)}, bf16[2,256,1024]{2,1,0:T(8,128)(2,1)S(1)}, u32[]{:S(2)}, u32[]{:S(2)}) collective-permute-start(bf16[2,256,1024]{2,1,0:T(8,128)(2,1)} %get-tuple-element.47), channel_id=1, source_target_pairs={{1,0},{2,1},{3,2},{4,3},{5,4},{6,5},{7,6},{8,7},{9,8},{10,9},{11,1... | collective-permute-start | bytes 3145736 | tf_op jit(solution)/shard_map/ppermute | solution.py:653
  85.6 33.2 %all-to-all-start.1 = ((bf16[128,32,128]{2,1,0:T(8,128)(2,1)}), bf16[128,32,128]{2,1,0:T(8,128)(2,1)S(1)}, u32[]{:S(2)}, u32[]{:S(2)}) async-start(bf16[128,32,128]{2,1,0:T(8,128)(2,1)} %bitcast.7), calls=%async_computation.1 | async-start | bytes 2097152 | tf_op jit(solution)/shard_map/all_to_all | solution.py:660
  92.2 16.0 %copy-start.1 = (f32[1024]{0:T(1024)S(1)}, f32[1024]{0:T(1024)}, u32[]{:S(2)}) copy-start(f32[1024]{0:T(1024)} %param.12) | copy-start | bytes 12292
  106.9 1.0 copy-start.9
  106.9 1.3 %copy-start.10 = (bf16[2,256,1024]{2,1,0:T(8,128)(2,1)}, bf16[2,256,1024]{2,1,0:T(8,128)(2,1)S(1)}, u32[]{:S(2)}) copy-start(bf16[2,256,1024]{2,1,0:T(8,128)(2,1)S(1)} %collective-permute-done.3.after_hbm) | copy-start | bytes 3145732
